TPU v7x, 32 devices: a whole 2x2x4 slice. The times are simulated.
32 devices in a mesh: blk: 8 (over z, x), pair: 4 (over y, core).
Axes of the slice: x: 2, y: 2, z: 4, core: 2. Of those that a mesh axis runs over, the one named last changes fastest.
Arguments:
- amplitudes: bfloat16 [4, 96, 12, 1024], P('pair', 'blk'), may hold values from -6 to 6
- tile_mask: int32 [4, 96, 12], P('pair', 'blk'), may hold values 0 or 1
- integrals: bfloat16 [64, 1024, 1024], P('blk', 'pair'), may hold values from -0.078125 to 0.078125
- block_tiles: int32 [64, 2], P('blk'), may hold values from 0 to 11
- block_keep: int32 [64], P('blk'), may hold values 0 or 1
- slot_tile: int32 [96], replicated, may hold values from 0 to 95, each once
Outputs:
- ladder: bfloat16 [96, 4, 96, 128], P('blk', 'pair')
Inputs may be any that keep to these rules, and one draw needn't show every extreme that they name: `slot_tile`: each result tile appears in exactly one slot.
All inputs are finite; a program needn't handle non-finite values. No bound on the sum of `tile_mask` or of `block_keep` on one device may be relied on, other than what follows from the above.
Results may differ from a plain program's by a relative error of at most 0.013.
Values may be sent and summed in bfloat16 or wider, within the bound.
No kernel may reach another device: no remote copies, remote signals or barrier semaphores. Data moves between devices by JAX's collectives and lax.ppermute only.
A program may use at most 128 MiB of HBM per device.

v0:
```python
import jax
import jax.numpy as jnp
from jax import lax
from jax.sharding import PartitionSpec as P

TV = 128
BW = 8


def per_device(amplitudes, tile_mask, integrals, block_tiles, block_keep, slot_tile):
    masked = amplitudes[0] * tile_mask[0].astype(jnp.bfloat16)[:, :, None]
    tile_count = amplitudes.shape[2]
    sources = block_tiles[:, 0]
    targets = block_tiles[:, 1]
    weights = block_keep.astype(jnp.float32)
    whole_rows = lax.all_gather(masked, "blk", axis=0, tiled=True)
    rows_all = whole_rows.shape[0]
    picked = jnp.take(whole_rows, sources, axis=1)
    partial_value = jnp.einsum(
        "rkd,kde->kre",
        picked,
        lax.all_gather(integrals, "pair", axis=1, tiled=True),
        preferred_element_type=jnp.float32,
    )
    partial_value = partial_value * weights[:, None, None]
    onehot = (targets[:, None] == jnp.arange(tile_count, dtype=jnp.int32)[None, :]).astype(
        jnp.float32
    )
    per_tile = jnp.einsum("ka,kre->are", onehot, partial_value, precision=lax.Precision.HIGHEST)
    per_tile = per_tile.astype(jnp.bfloat16)
    tile_rows = (
        per_tile.reshape(tile_count, rows_all, BW, TV)
        .transpose(0, 2, 1, 3)
        .reshape(tile_count * BW, rows_all, TV)
    )
    by_slot = jnp.take(tile_rows, slot_tile, axis=0)
    received = lax.all_to_all(by_slot, "blk", split_axis=0, concat_axis=0, tiled=True)
    holders = lax.axis_size("blk")
    summed = (
        received.astype(jnp.float32)
        .reshape(holders, received.shape[0] // holders, rows_all, TV)
        .sum(0)
    )
    return summed.astype(jnp.bfloat16)[:, None]


def solution(mesh):
    placed = (
        P("pair", "blk", None, None),
        P("pair", "blk", None),
        P("blk", "pair", None),
        P("blk", None),
        P("blk"),
        P(),
    )
    return jax.shard_map(
        per_device,
        mesh=mesh,
        in_specs=placed,
        out_specs=P("blk", "pair", None, None),
        check_vma=False,
    )
```

profile of v0, /device:TPU:0, one launch (start us, length us, event | category | flops | bytes accessed | tf_op | source)
XLA Modules:
  0.0 269.2 jit_solution(8243794549857987428)
XLA Ops:
  6.5 0.0 all-gather.3.cloned.1.call-start
  6.5 0.7 convert_element_type.31
  7.2 1.8 bitcast_multiply_fusion
  9.1 0.0 copy-start.1
  9.1 0.0 copy-start
  9.1 0.0 copy-start.2
  9.1 0.0 all-gather.3.cloned.1.call-update
  9.1 0.0 all-gather.5.cloned.1.call-start
  9.2 0.7 all-gather.5.cloned.1.call-update
  9.9 0.0 copy-done.1
  9.9 0.0 copy-done
  9.9 0.0 copy-done.2
  10.0 62.7 %all-gather.3.cloned.1.call-done = bf16[96,12,1024]{2,1,0:T(8,128)(2,1)} async-done(((bf16[12,12,1024]{2,1,0:T(8,128)(2,1)}), bf16[96,12,1024]{2,1,0:T(8,128)(2,1)}) %all-gather.3.cloned.1.call-update) | async-done | bytes 2359312 | tf_op jit(solution)/shard_map/all_gather | solution.py:16
  72.7 3.2 %copy.11 = bf16[96,12,1024]{2,0,1:T(8,128)(2,1)S(1)} copy(bf16[96,12,1024]{2,1,0:T(8,128)(2,1)} %all-gather.3.cloned.1.call-done) | data formatting | bytes 4718592 | tf_op jit(solution)/shard_map/all_gather | solution.py:16
  75.9 1.8 gather_fusion
  77.7 101.2 %all-gather.5.cloned.1.call-done = bf16[8,1024,1024]{2,1,0:T(8,128)(2,1)} async-done(((bf16[8,256,1024]{2,1,0:T(8,128)(2,1)}), bf16[8,1024,1024]{2,1,0:T(8,128)(2,1)}) %all-gather.5.cloned.1.call-update) | async-done | bytes 16777232 | tf_op jit(solution)/shard_map/all_gather | solution.py:22
  178.9 9.1 %convolution_multiply_fusion = f32[8,96,1024]{2,1,0:T(8,128)S(1)} fusion(bf16[8,1024,1024]{2,1,0:T(8,128)(2,1)} %all-gather.5.cloned.1.call-done, bf16[8,96,1024]{2,1,0:T(8,128)(2,1)} %gather_fusion, f32[8]{0:T(128)S(1)} %convert_element_type.33, pred[8]{0:T(512)(128)(4,1)S(1)} %and_bitcast_fusion), kind=kOutput, calls=%fused_computation.6 | convolution fusion | flops 1612185600 | bytes 21495848 | tf_op jit(solution)/shard_map/rkd,kde->kre/dot_general | solution.py:19
  188.0 3.8 %fusion.2 = bf16[12,96,1024]{2,0,1:T(8,128)(2,1)S(1)} fusion(f32[8,96,1024]{2,1,0:T(8,128)S(1)} %convolution_multiply_fusion, s32[8]{0:T(128)S(1)} %get-tuple-element.5), kind=kOutput, calls=%fused_computation.5 | convolution fusion | flops 114425952 | bytes 5505056 | tf_op jit(solution)/shard_map/ka,kre->are/dot_general | solution.py:29
  191.8 2.9 %reshape.58 = bf16[12,96,8,128]{3,2,0,1:T(8,128)(2,1)} reshape(bf16[12,96,1024]{2,0,1:T(8,128)(2,1)S(1)} %fusion.2) | data formatting | bytes 4718592 | tf_op jit(solution)/shard_map/reshape | solution.py:32
  194.7 4.0 %copy.14 = bf16[12,8,96,128]{3,2,1,0:T(8,128)(2,1)} copy(bf16[12,8,96,128]{3,1,0,2:T(8,128)(2,1)} %bitcast.27) | data formatting | bytes 4718592 | tf_op jit(solution)/shard_map/transpose | solution.py:33
  198.7 2.7 gather_fusion.1
  201.4 0.3 broadcast_select_fusion
  201.7 59.5 %all_to_all.5 = bf16[96,96,128]{2,1,0:T(8,128)(2,1)S(1)} all-to-all(bf16[96,96,128]{2,1,0:T(8,128)(2,1)S(1)} %broadcast_select_fusion), channel_id=1, replica_groups=mesh['blk'=8,'pair'=4] {'blk'}, dimensions={0} | all-to-all | bytes 4718592 | tf_op jit(solution)/shard_map/all_to_all | solution.py:37
  261.2 1.1 reduce
  (8 shorter events, 0.0 us)
Async XLA Ops:
  6.5 66.2 %all-gather.3.cloned.1.call-start = ((), (), s32[]{:S(2)}) async-start(), calls=%async_computation.1 | async-start | bytes 3538944 | tf_op jit(solution)/shard_map/all_gather | solution.py:16
  9.1 0.8 copy-start.1
  9.1 0.8 copy-start
  9.1 0.8 copy-start.2
  9.1 169.8 %all-gather.5.cloned.1.call-start = ((), (), s32[]{:S(2)}) async-start(), calls=%async_computation.2 | async-start | bytes 20971520 | tf_op jit(solution)/shard_map/all_gather | solution.py:22
Sparse Core Ops, SparseCore 0:
  9.5 63.1 all-gather.2
  74.3 104.5 all-gather.4
where the time goes:
time: 269 us
  waiting for transfers between devices  165 us (61%)
  blocking collectives  59.5 us (22%)
  local copies, waits for them, and re-layouts  14.5 us (5%)
  between operations  13.5 us (5%)
  matrix products  12.9 us (5%)
  other arithmetic  3.97 us (1%)
    all_gather x1, waiting for transfers between devices, per_device(): lax.all_gather(integrals, 'pair', axis=1, tiled=True)  101 us
    all_gather x1, waiting for transfers between devices, per_device(): whole_rows = lax.all_gather(masked, 'blk', axis=0, tiled=True)  62.7 us
    all_to_all x1, blocking collectives, per_device(): lax.all_to_all(by_slot, 'blk', split_axis=0, concat_axis=0, tiled=True)  59.5 us
    dot_general x1, matrix products, per_device(): jnp.einsum('rkd,kde->kre', picked, lax.all_gather(integrals, 'pair', axis...  9.13 us
  transfers between devices with their start and end apart: 2, of which 2 were waited for; matrix products, arithmetic and copies ran while one was open for 2% of the time, Pallas kernels for 0%

commit v1 on v0

v1 whole, which is shorter than its diff:
```python
import functools

import jax
import jax.numpy as jnp
from jax import lax
from jax.experimental import pallas as pl
from jax.experimental.pallas import tpu as pltpu
from jax.sharding import PartitionSpec as P

LANES = 128


def blk_swap(value, dz, dx, nz, nx):
    pairs = [(z * nx + x, (z ^ dz) * nx + (x ^ dx)) for z in range(nz) for x in range(nx)]
    return lax.ppermute(value, "blk", pairs)


def pair_swap(value, dy, dc, ny, nc):
    pairs = [(y * nc + c, (y ^ dy) * nc + (c ^ dc)) for y in range(ny) for c in range(nc)]
    return lax.ppermute(value, "pair", pairs)


def pick(position, options):
    value = options[0]
    for index in range(1, len(options)):
        value = jnp.where(position == index, options[index], value)
    return value


def product_kernel(nx, nc, rows, ctile, keep, pos, *refs):
    units, blocks, outs = refs[:nx], refs[nx : nx + nc], refs[nx + nc :]
    ny = len(outs)
    x, c = pos[0], pos[1]
    depth = blocks[0].shape[1]
    parts = [unit[0] for unit in units]
    lhs = jnp.concatenate([pick(x ^ at, parts) for at in range(nx)], axis=0)
    total = None
    for d in range(nc):
        which = c ^ d
        columns = pick(which, [lhs[:, i * depth : (i + 1) * depth] for i in range(nc)])
        term = jnp.dot(columns, blocks[d][0], preferred_element_type=jnp.float32)
        total = term if total is None else total + term
    total = total * keep[pl.program_id(0)].astype(jnp.float32)
    for s in range(ny):
        pieces = [total[(at * ny + s) * rows : (at * ny + s + 1) * rows] for at in range(nx)]
        outs[s][0] = jnp.concatenate(pieces, axis=0).astype(outs[s].dtype)


def products(units, blocks, ctile, keep, pos, ny, rows):
    nx, nc = len(units), len(blocks)
    slots, depth, width = blocks[0].shape
    tile_count, unit_rows, unit_columns = units[0].shape
    out = jax.ShapeDtypeStruct((slots, nx * rows, width), jnp.bfloat16)
    return pl.pallas_call(
        functools.partial(product_kernel, nx, nc, rows),
        grid_spec=pltpu.PrefetchScalarGridSpec(
            num_scalar_prefetch=3,
            grid=(slots,),
            in_specs=[pl.BlockSpec((1, unit_rows, unit_columns), lambda k, ct, kp, ps: (ct[k], 0, 0))] * nx
            + [pl.BlockSpec((1, depth, width), lambda k, ct, kp, ps: (k, 0, 0))] * nc,
            out_specs=[pl.BlockSpec((1, nx * rows, width), lambda k, ct, kp, ps: (k, 0, 0))] * ny,
        ),
        out_shape=[out] * ny,
        cost_estimate=pl.CostEstimate(
            flops=2 * slots * nx * unit_rows * unit_columns * width,
            bytes_accessed=2 * slots * nc * depth * width,
            transcendentals=0,
        ),
        compiler_params=pltpu.CompilerParams(vmem_limit_bytes=32 * 2**20),
        name="products",
    )(ctile, keep, pos, *units, *blocks)


def route_kernel(ny, nx, nz, atile, slot_tile, pos, *refs):
    parts, outs, total = refs[:ny], refs[ny : ny + nx], refs[ny + nx]
    x, z = pos[0], pos[2]
    slots = parts[0].shape[0]
    per_tile = total.shape[2] // LANES
    owned = outs[0].shape[0] // nz
    total[...] = jnp.zeros_like(total)

    def add(k, _):
        value = parts[0][k].astype(jnp.float32)
        for part in parts[1:]:
            value += part[k].astype(jnp.float32)
        total[atile[k]] += value
        return 0

    lax.fori_loop(0, slots, add, 0)
    for d in range(nx):
        for dz in range(nz):
            owner = (z ^ dz) * nx + (x ^ d)
            for i in range(owned):
                tile = slot_tile[owner * owned + i]
                a = lax.div(tile, per_tile)
                column = pl.multiple_of(lax.rem(tile, per_tile) * LANES, LANES)
                outs[d][dz * owned + i] = total[a, :, pl.ds(column, LANES)].astype(outs[d].dtype)


def route(parts, atile, slot_tile, pos, tile_count, nx, nz):
    slots, rows, width = parts[0].shape
    result_tiles = slot_tile.shape[0]
    out = jax.ShapeDtypeStruct((result_tiles // nx, rows, LANES), jnp.bfloat16)
    smem = pl.BlockSpec(memory_space=pltpu.SMEM)
    vmem = pl.BlockSpec(memory_space=pltpu.VMEM)
    return pl.pallas_call(
        functools.partial(route_kernel, len(parts), nx, nz),
        in_specs=[smem] * 3 + [vmem] * len(parts),
        out_specs=[vmem] * nx,
        out_shape=[out] * nx,
        scratch_shapes=[pltpu.VMEM((tile_count, rows, width), jnp.float32)],
        cost_estimate=pl.CostEstimate(
            flops=2 * slots * rows * width, bytes_accessed=4 * slots * rows * width, transcendentals=0
        ),
        compiler_params=pltpu.CompilerParams(vmem_limit_bytes=32 * 2**20),
        name="route",
    )(atile, slot_tile, pos, *parts)


def add_kernel(n, *refs):
    parts, outs = refs[:n], refs[n:]
    value = parts[0][...].astype(jnp.float32)
    for part in parts[1:]:
        value += part[...].astype(jnp.float32)
    count = outs[0].shape[0]
    for i, out in enumerate(outs):
        out[...] = value[i * count : (i + 1) * count].astype(out.dtype)


def add_split(parts, nz):
    tiles, rows, lanes = parts[0].shape
    out = jax.ShapeDtypeStruct((tiles // nz, rows, lanes), jnp.bfloat16)
    vmem = pl.BlockSpec(memory_space=pltpu.VMEM)
    return pl.pallas_call(
        functools.partial(add_kernel, len(parts)),
        in_specs=[vmem] * len(parts),
        out_specs=[vmem] * nz,
        out_shape=[out] * nz,
        cost_estimate=pl.CostEstimate(
            flops=tiles * rows * lanes, bytes_accessed=4 * tiles * rows * lanes, transcendentals=0
        ),
        compiler_params=pltpu.CompilerParams(vmem_limit_bytes=32 * 2**20),
        name="add_split",
    )(*parts)


def final_kernel(nz, pos, *refs):
    out = refs[-1]
    z = pos[2]
    for ahead in range(nz):
        value = None
        for e in range(nz):
            term = refs[e * nz + (e ^ ahead)][...].astype(jnp.float32)
            value = term if value is None else value + term
        out[:, z ^ ahead] = value.astype(out.dtype)


def final_sum(received, pos, nz):
    owned, rows, lanes = received[0][0].shape
    smem = pl.BlockSpec(memory_space=pltpu.SMEM)
    vmem = pl.BlockSpec(memory_space=pltpu.VMEM)
    return pl.pallas_call(
        functools.partial(final_kernel, nz),
        in_specs=[smem] + [vmem] * (nz * nz),
        out_specs=vmem,
        out_shape=jax.ShapeDtypeStruct((owned, nz, rows, lanes), jnp.bfloat16),
        compiler_params=pltpu.CompilerParams(vmem_limit_bytes=32 * 2**20),
        name="final_sum",
    )(pos, *[part for line in received for part in line])


def per_device(nz, nx, ny, nc, amplitudes, tile_mask, integrals, block_tiles, block_keep, slot_tile):
    blk, pair = lax.axis_index("blk"), lax.axis_index("pair")
    z, x, y, c = blk // nx, blk % nx, pair // nc, pair % nc
    pos = jnp.stack([x, c, z]).astype(jnp.int32)
    ctile, atile = block_tiles[:, 0], block_tiles[:, 1]
    _, rows, tile_count, contracted = amplitudes.shape
    columns = contracted // ny

    blocks = [integrals] + [pair_swap(integrals, 0, d, ny, nc) for d in range(1, nc)]

    masked = amplitudes[0] * tile_mask[0].astype(jnp.bfloat16)[:, :, None]
    masked = masked.transpose(1, 0, 2)
    pieces = []
    for d in range(ny):
        piece = lax.dynamic_slice_in_dim(masked, (y ^ d) * columns, columns, axis=2)
        pieces.append(pair_swap(piece, d, 0, ny, nc) if d else piece)
    unit = jnp.concatenate(pieces, axis=1)

    received = [[None] * nz for _ in range(nz)]
    for dz in range(nz):
        here = blk_swap(unit, dz, 0, nz, nx) if dz else unit
        units = [here] + [blk_swap(here, 0, d, nz, nx) for d in range(1, nx)]
        partial = products(units, blocks, ctile, block_keep, pos, ny, rows)
        parts = [partial[0]] + [pair_swap(partial[d], d, 0, ny, nc) for d in range(1, ny)]
        by_owner = route(parts, atile, slot_tile, pos, tile_count, nx, nz)
        mine = [by_owner[0]] + [blk_swap(by_owner[d], 0, d, nz, nx) for d in range(1, nx)]
        to_column = add_split(mine, nz)
        for e in range(nz):
            received[e][dz] = blk_swap(to_column[e], e, 0, nz, nx) if e else to_column[0]
    out = final_sum(received, pos, nz)
    return out.reshape(out.shape[0], 1, out.shape[1] * out.shape[2], LANES)


def solution(mesh):
    holders, pairs = mesh.shape["blk"], mesh.shape["pair"]
    nx = 1
    while (2 * nx) ** 2 <= holders:
        nx *= 2
    nc = 2 if pairs % 2 == 0 else 1
    placed = (
        P("pair", "blk", None, None),
        P("pair", "blk", None),
        P("blk", "pair", None),
        P("blk", None),
        P("blk"),
        P(),
    )
    return jax.shard_map(
        functools.partial(per_device, holders // nx, nx, pairs // nc, nc),
        mesh=mesh,
        in_specs=placed,
        out_specs=P("blk", "pair", None, None),
        check_vma=False,
    )
```

time: 269 us -> 125 us (0.46)
  waiting for transfers between devices: 165 us -> 49.7 us
  blocking collectives: 59.5 us -> 0 us
  starting transfers between devices: 0.04 us -> 36.9 us
  Pallas kernels: 0 us -> 32.2 us
  between operations: 13.5 us -> 0.16 us
  matrix products: 12.9 us -> 0 us
  local copies, waits for them, and re-layouts: 14.5 us -> 3.74 us
    all_gather x2 -> x0, waiting for transfers between devices: 164 us -> none  [the longest x1 101 us: per_device(): lax.all_gather(integrals, 'pair', axis=1, tiled=True)]
    all_to_all x1 -> x0, blocking collectives: 59.5 us -> none  [per_device(): lax.all_to_all(by_slot, 'blk', split_axis=0, concat_axis=0, tiled=True)]
    ppermute x0 -> x29, waiting for transfers between devices: none -> 49.7 us  [the longest x23 39.5 us: blk_swap(): return lax.ppermute(value, 'blk', pairs)]
    ppermute x0 -> x29, starting transfers between devices: none -> 36.9 us  [the longest x23 29.6 us: blk_swap(): return lax.ppermute(value, 'blk', pairs)]
    pallas_call x0 -> x13, Pallas kernels: none -> 32.2 us  [the longest x4 25.7 us: products(): pl.pallas_call(functools.partial(product_kernel, nx, nc, rows), grid_spec...]
    dot_general x2 -> x0, matrix products: 12.9 us -> none  [the longest x1 9.13 us: per_device(): jnp.einsum('rkd,kde->kre', picked, lax.all_gather(integrals, 'pair', axis...]
    gather x2 -> x0, local copies, waits for them, and re-layouts: 4.46 us -> none  [the longest x1 2.66 us: per_device(): by_slot = jnp.take(tile_rows, slot_tile, axis=0)]
    transpose x1 -> x0, local copies, waits for them, and re-layouts: 3.98 us -> none  [per_device(): tile_rows = per_tile.reshape(tile_count, rows_all, BW, TV).transpose(0, 2...]
  transfers between devices with their start and end apart: 2 -> 29, of which waited for: 2 -> 10; matrix products, arithmetic and copies ran while one was open for 2% -> 2% of each run, Pallas kernels for 0% -> 25%
where the time goes in v1:
time: 125 us
  waiting for transfers between devices  49.7 us (40%)
  starting transfers between devices  36.9 us (30%)
  Pallas kernels  32.2 us (26%)
  local copies, waits for them, and re-layouts  3.74 us (3%)
  other arithmetic  2.04 us (2%)
    ppermute x23, waiting for transfers between devices, blk_swap(): return lax.ppermute(value, 'blk', pairs)  39.5 us
    ppermute x23, starting transfers between devices, blk_swap(): return lax.ppermute(value, 'blk', pairs)  29.6 us
    pallas_call x4, Pallas kernels, products(): pl.pallas_call(functools.partial(product_kernel, nx, nc, rows), grid_spec...  25.7 us
    ppermute x6, waiting for transfers between devices, pair_swap(): return lax.ppermute(value, 'pair', pairs)  10.2 us
    ppermute x6, starting transfers between devices, pair_swap(): return lax.ppermute(value, 'pair', pairs)  7.35 us
    pallas_call x4, Pallas kernels, route(): pl.pallas_call(functools.partial(route_kernel, len(parts), nx, nz), in_sp...  4.8 us
    unnamed x8, local copies, waits for them, and re-layouts  2.85 us
  transfers between devices with their start and end apart: 29, of which 10 were waited for; matrix products, arithmetic and copies ran while one was open for 2% of the time, Pallas kernels for 25%

profile of v1, /device:TPU:0, one launch (start us, length us, event | category | flops | bytes accessed | tf_op | source)
XLA Modules:
  0.0 124.8 jit_solution(8599739536979308562)
XLA Ops:
  2.5 2.6 %collective-permute-start = (bf16[12,12,512]{2,1,0:T(8,128)(2,1)S(1)}, bf16[12,12,512]{2,1,0:T(8,128)(2,1)S(1)}, u32[]{:S(2)}, u32[]{:S(2)}) collective-permute-start(bf16[12,12,512]{2,1,0:T(8,128)(2,1)S(1)} %get-tuple-element.70), channel_id=1, source_target_pairs={{0,2},{1,3},{2,0},{3,1},{4,6},{5,7},{6,4},{7,5},{8,10},{9,11},{10,... | collective-permute-start | bytes 442376 | tf_op jit(solution)/shard_map/ppermute | solution.py:20
  5.1 5.6 %collective-permute-done = bf16[12,12,512]{2,1,0:T(8,128)(2,1)S(1)} collective-permute-done((bf16[12,12,512]{2,1,0:T(8,128)(2,1)S(1)}, bf16[12,12,512]{2,1,0:T(8,128)(2,1)S(1)}, u32[]{:S(2)}, u32[]{:S(2)}) %collective-permute-start) | collective-permute-done | bytes 147488 | tf_op jit(solution)/shard_map/ppermute | solution.py:20
  10.7 3.9 %collective-permute-start.13 = (bf16[12,24,512]{2,1,0:T(8,128)(2,1)S(1)}, bf16[12,24,512]{2,1,0:T(8,128)(2,1)S(1)}, u32[]{:S(2)}, u32[]{:S(2)}) collective-permute-start(bf16[12,24,512]{2,1,0:T(8,128)(2,1)S(1)} %pad_maximum_fusion.refs_0_), channel_id=1, source_target_pairs={{0,24},{4,28},{8,16},{12,20},{16,8},{20,12},{24,0},{28,4},{1,25},{... | collective-permute-start | bytes 884744 | tf_op jit(solution)/shard_map/ppermute | solution.py:15
  15.2 7.4 %collective-permute-done.13.refs_0_ = bf16[12,24,512]{2,1,0:T(8,128)(2,1)S(1)} collective-permute-done((bf16[12,24,512]{2,1,0:T(8,128)(2,1)S(1)}, bf16[12,24,512]{2,1,0:T(8,128)(2,1)S(1)}, u32[]{:S(2)}, u32[]{:S(2)}) %collective-permute-start.13) | collective-permute-done | bytes 294944 | tf_op jit(solution)/shard_map/ppermute | solution.py:15
  22.6 1.7 %collective-permute-start.14 = (bf16[12,24,512]{2,1,0:T(8,128)(2,1)S(1)}, bf16[12,24,512]{2,1,0:T(8,128)(2,1)S(1)}, u32[]{:S(2)}, u32[]{:S(2)}) collective-permute-start(bf16[12,24,512]{2,1,0:T(8,128)(2,1)S(1)} %collective-permute-done.13.refs_0_), channel_id=1, source_target_pairs={{0,4},{4,0},{8,12},{12,8},{16,20},{20,16},{24,28},{28,24},{1,5},{5... | collective-permute-start | bytes 884744 | tf_op jit(solution)/shard_map/ppermute | solution.py:15
  24.3 15.3 %collective-permute-done.9.refs_0_ = bf16[12,24,512]{2,1,0:T(8,128)(2,1)S(1)} collective-permute-done((bf16[12,24,512]{2,1,0:T(8,128)(2,1)S(1)}, bf16[12,24,512]{2,1,0:T(8,128)(2,1)S(1)}, u32[]{:S(2)}, u32[]{:S(2)}) %collective-permute-start.9) | collective-permute-done | bytes 294944 | tf_op jit(solution)/shard_map/ppermute | solution.py:15
  44.0 2.2 %copy-done = bf16[8,256,1024]{2,1,0:T(8,128)(2,1)S(1)} copy-done((bf16[8,256,1024]{2,1,0:T(8,128)(2,1)S(1)}, bf16[8,256,1024]{2,1,0:T(8,128)(2,1)}, u32[]{:S(2)}) %copy-start) | copy-done | bytes 4194328
  46.8 6.4 %products.7 = (bf16[8,24,1024]{2,1,0:T(8,128)(2,1)S(1)}, bf16[8,24,1024]{2,1,0:T(8,128)(2,1)S(1)}) custom-call(s32[8]{0:T(128)S(1)} %get-tuple-element.71.ctile, s32[8]{0:T(128)S(1)} %copy-done.2, s32[3]{0:T(128)S(1)} %pad_add_fusion.pos, bf16[12,24,512]{2,1,0:T(8,128)(2,1)S(1)} %collective-permute-done.13.refs_0_, ...), custom_call_target="tpu_custom_call" | custom-call | flops 402653184 | bytes 8388608 | tf_op jit(solution)/shard_map/products/pallas_call | solution.py:54
  53.2 1.6 %collective-permute-start.15 = (bf16[8,24,1024]{2,1,0:T(8,128)(2,1)S(1)}, bf16[8,24,1024]{2,1,0:T(8,128)(2,1)S(1)}, u32[]{:S(2)}, u32[]{:S(2)}) collective-permute-start(bf16[8,24,1024]{2,1,0:T(8,128)(2,1)S(1)} %get-tuple-element.53), channel_id=1, source_target_pairs={{0,2},{1,3},{2,0},{3,1},{4,6},{5,7},{6,4},{7,5},{8,10},{9,11},{10,... | collective-permute-start | bytes 1179656 | tf_op jit(solution)/shard_map/ppermute | solution.py:20
  54.8 6.4 %products.6 = (bf16[8,24,1024]{2,1,0:T(8,128)(2,1)S(1)}, bf16[8,24,1024]{2,1,0:T(8,128)(2,1)S(1)}) custom-call(s32[8]{0:T(128)S(1)} %get-tuple-element.71.ctile, s32[8]{0:T(128)S(1)} %copy-done.2, s32[3]{0:T(128)S(1)} %pad_add_fusion.pos, bf16[12,24,512]{2,1,0:T(8,128)(2,1)S(1)} %collective-permute-done.9.refs_0_, ...), custom_call_target="tpu_custom_call" | custom-call | flops 402653184 | bytes 8388608 | tf_op jit(solution)/shard_map/products/pallas_call | solution.py:54
  61.8 6.5 %products.5 = (bf16[8,24,1024]{2,1,0:T(8,128)(2,1)S(1)}, bf16[8,24,1024]{2,1,0:T(8,128)(2,1)S(1)}) custom-call(s32[8]{0:T(128)S(1)} %get-tuple-element.71.ctile, s32[8]{0:T(128)S(1)} %copy-done.2, s32[3]{0:T(128)S(1)} %pad_add_fusion.pos, bf16[12,24,512]{2,1,0:T(8,128)(2,1)S(1)} %collective-permute-done.5.refs_0_, ...), custom_call_target="tpu_custom_call" | custom-call | flops 402653184 | bytes 8388608 | tf_op jit(solution)/shard_map/products/pallas_call | solution.py:54
  69.8 6.4 %products.4 = (bf16[8,24,1024]{2,1,0:T(8,128)(2,1)S(1)}, bf16[8,24,1024]{2,1,0:T(8,128)(2,1)S(1)}) custom-call(s32[8]{0:T(128)S(1)} %get-tuple-element.71.ctile, s32[8]{0:T(128)S(1)} %copy-done.2, s32[3]{0:T(128)S(1)} %pad_add_fusion.pos, bf16[12,24,512]{2,1,0:T(8,128)(2,1)S(1)} %pad_maximum_fusion.refs_0_, ...), custom_call_target="tpu_custom_call" | custom-call | flops 402653184 | bytes 8388608 | tf_op jit(solution)/shard_map/products/pallas_call | solution.py:54
  83.3 4.6 %collective-permute-done.3.refs_1_ = bf16[8,24,1024]{2,1,0:T(8,128)(2,1)S(1)} collective-permute-done((bf16[8,24,1024]{2,1,0:T(8,128)(2,1)S(1)}, bf16[8,24,1024]{2,1,0:T(8,128)(2,1)S(1)}, u32[]{:S(2)}, u32[]{:S(2)}) %collective-permute-start.3) | collective-permute-done | bytes 393248 | tf_op jit(solution)/shard_map/ppermute | solution.py:20
  89.8 2.7 %collective-permute-start.24 = (bf16[12,24,128]{2,1,0:T(8,128)(2,1)S(1)}, bf16[12,24,128]{2,1,0:T(8,128)(2,1)S(1)}, u32[]{:S(2)}, u32[]{:S(2)}) collective-permute-start(bf16[12,24,128]{2,1,0:T(8,128)(2,1)S(1)} %get-tuple-element.64), channel_id=1, source_target_pairs={{0,16},{4,20},{8,24},{12,28},{16,0},{20,4},{24,8},{28,12},{1,17},{... | collective-permute-start | bytes 221192 | tf_op jit(solution)/shard_map/ppermute | solution.py:15
  92.6 1.9 %collective-permute-done.12.refs_1_ = bf16[48,24,128]{2,1,0:T(8,128)(2,1)S(1)} collective-permute-done((bf16[48,24,128]{2,1,0:T(8,128)(2,1)S(1)}, bf16[48,24,128]{2,1,0:T(8,128)(2,1)S(1)}, u32[]{:S(2)}, u32[]{:S(2)}) %collective-permute-start.12) | collective-permute-done | bytes 294944 | tf_op jit(solution)/shard_map/ppermute | solution.py:15
  94.4 2.5 %collective-permute-start.28 = (bf16[12,24,128]{2,1,0:T(8,128)(2,1)S(1)}, bf16[12,24,128]{2,1,0:T(8,128)(2,1)S(1)}, u32[]{:S(2)}, u32[]{:S(2)}) collective-permute-start(bf16[12,24,128]{2,1,0:T(8,128)(2,1)S(1)} %get-tuple-element.68), channel_id=1, source_target_pairs={{0,24},{4,28},{8,16},{12,20},{16,8},{20,12},{24,0},{28,4},{1,25},{... | collective-permute-start | bytes 221192 | tf_op jit(solution)/shard_map/ppermute | solution.py:15
  97.0 3.3 %collective-permute-done.8.refs_1_ = bf16[48,24,128]{2,1,0:T(8,128)(2,1)S(1)} collective-permute-done((bf16[48,24,128]{2,1,0:T(8,128)(2,1)S(1)}, bf16[48,24,128]{2,1,0:T(8,128)(2,1)S(1)}, u32[]{:S(2)}, u32[]{:S(2)}) %collective-permute-start.8) | collective-permute-done | bytes 294944 | tf_op jit(solution)/shard_map/ppermute | solution.py:15
  100.4 3.1 %collective-permute-done.4.refs_1_ = bf16[48,24,128]{2,1,0:T(8,128)(2,1)S(1)} collective-permute-done((bf16[48,24,128]{2,1,0:T(8,128)(2,1)S(1)}, bf16[48,24,128]{2,1,0:T(8,128)(2,1)S(1)}, u32[]{:S(2)}, u32[]{:S(2)}) %collective-permute-start.4) | collective-permute-done | bytes 294944 | tf_op jit(solution)/shard_map/ppermute | solution.py:15
  103.5 2.2 %collective-permute-start.27 = (bf16[12,24,128]{2,1,0:T(8,128)(2,1)S(1)}, bf16[12,24,128]{2,1,0:T(8,128)(2,1)S(1)}, u32[]{:S(2)}, u32[]{:S(2)}) collective-permute-start(bf16[12,24,128]{2,1,0:T(8,128)(2,1)S(1)} %get-tuple-element.67), channel_id=1, source_target_pairs={{0,24},{4,28},{8,16},{12,20},{16,8},{20,12},{24,0},{28,4},{1,25},{... | collective-permute-start | bytes 221192 | tf_op jit(solution)/shard_map/ppermute | solution.py:15
  108.1 2.2 %collective-permute-start.26 = (bf16[12,24,128]{2,1,0:T(8,128)(2,1)S(1)}, bf16[12,24,128]{2,1,0:T(8,128)(2,1)S(1)}, u32[]{:S(2)}, u32[]{:S(2)}) collective-permute-start(bf16[12,24,128]{2,1,0:T(8,128)(2,1)S(1)} %get-tuple-element.66), channel_id=1, source_target_pairs={{0,24},{4,28},{8,16},{12,20},{16,8},{20,12},{24,0},{28,4},{1,25},{... | collective-permute-start | bytes 221192 | tf_op jit(solution)/shard_map/ppermute | solution.py:15
  110.3 4.6 %collective-permute-done.23.refs_10_ = bf16[12,24,128]{2,1,0:T(8,128)(2,1)S(1)} collective-permute-done((bf16[12,24,128]{2,1,0:T(8,128)(2,1)S(1)}, bf16[12,24,128]{2,1,0:T(8,128)(2,1)S(1)}, u32[]{:S(2)}, u32[]{:S(2)}) %collective-permute-start.23) | collective-permute-done | bytes 73760 | tf_op jit(solution)/shard_map/ppermute | solution.py:15
  114.9 2.3 %collective-permute-start.21 = (bf16[12,24,128]{2,1,0:T(8,128)(2,1)S(1)}, bf16[12,24,128]{2,1,0:T(8,128)(2,1)S(1)}, u32[]{:S(2)}, u32[]{:S(2)}) collective-permute-start(bf16[12,24,128]{2,1,0:T(8,128)(2,1)S(1)} %get-tuple-element.61), channel_id=1, source_target_pairs={{0,16},{4,20},{8,24},{12,28},{16,0},{20,4},{24,8},{28,12},{1,17},{... | collective-permute-start | bytes 221192 | tf_op jit(solution)/shard_map/ppermute | solution.py:15
  117.3 2.2 %collective-permute-start.25 = (bf16[12,24,128]{2,1,0:T(8,128)(2,1)S(1)}, bf16[12,24,128]{2,1,0:T(8,128)(2,1)S(1)}, u32[]{:S(2)}, u32[]{:S(2)}) collective-permute-start(bf16[12,24,128]{2,1,0:T(8,128)(2,1)S(1)} %get-tuple-element.65), channel_id=1, source_target_pairs={{0,24},{4,28},{8,16},{12,20},{16,8},{20,12},{24,0},{28,4},{1,25},{... | collective-permute-start | bytes 221192 | tf_op jit(solution)/shard_map/ppermute | solution.py:15
  120.2 3.2 %collective-permute-done.25.refs_12_ = bf16[12,24,128]{2,1,0:T(8,128)(2,1)S(1)} collective-permute-done((bf16[12,24,128]{2,1,0:T(8,128)(2,1)S(1)}, bf16[12,24,128]{2,1,0:T(8,128)(2,1)S(1)}, u32[]{:S(2)}, u32[]{:S(2)}) %collective-permute-start.25) | collective-permute-done | bytes 73760 | tf_op jit(solution)/shard_map/ppermute | solution.py:15
  (62 shorter events, 23.9 us)
Async XLA Ops:
  0.0 44.0 %collective-permute-start.2 = (bf16[8,256,1024]{2,1,0:T(8,128)(2,1)}, bf16[8,256,1024]{2,1,0:T(8,128)(2,1)}, u32[]{:S(2)}, u32[]{:S(2)}) collective-permute-start(bf16[8,256,1024]{2,1,0:T(8,128)(2,1)} %refs_2_.7), channel_id=1, source_target_pairs={{0,1},{1,0},{2,3},{3,2},{4,5},{5,4},{6,7},{7,6},{8,9},{9,8},{10,11... | collective-permute-start | bytes 12582920 | tf_op jit(solution)/shard_map/ppermute | solution.py:20
  10.7 11.9 %collective-permute-start.13 = (bf16[12,24,512]{2,1,0:T(8,128)(2,1)S(1)}, bf16[12,24,512]{2,1,0:T(8,128)(2,1)S(1)}, u32[]{:S(2)}, u32[]{:S(2)}) collective-permute-start(bf16[12,24,512]{2,1,0:T(8,128)(2,1)S(1)} %pad_maximum_fusion.refs_0_), channel_id=1, source_target_pairs={{0,24},{4,28},{8,16},{12,20},{16,8},{20,12},{24,0},{28,4},{1,25},{... | collective-permute-start | bytes 884744 | tf_op jit(solution)/shard_map/ppermute | solution.py:15
  14.6 25.0 %collective-permute-start.9 = (bf16[12,24,512]{2,1,0:T(8,128)(2,1)S(1)}, bf16[12,24,512]{2,1,0:T(8,128)(2,1)S(1)}, u32[]{:S(2)}, u32[]{:S(2)}) collective-permute-start(bf16[12,24,512]{2,1,0:T(8,128)(2,1)S(1)} %pad_maximum_fusion.refs_0_), channel_id=1, source_target_pairs={{0,16},{4,20},{8,24},{12,28},{16,0},{20,4},{24,8},{28,12},{1,17},{... | collective-permute-start | bytes 884744 | tf_op jit(solution)/shard_map/ppermute | solution.py:15
  14.6 27.1 %collective-permute-start.5 = (bf16[12,24,512]{2,1,0:T(8,128)(2,1)S(1)}, bf16[12,24,512]{2,1,0:T(8,128)(2,1)S(1)}, u32[]{:S(2)}, u32[]{:S(2)}) collective-permute-start(bf16[12,24,512]{2,1,0:T(8,128)(2,1)S(1)} %pad_maximum_fusion.refs_0_), channel_id=1, source_target_pairs={{0,8},{4,12},{8,0},{12,4},{16,24},{20,28},{24,16},{28,20},{1,9},{5... | collective-permute-start | bytes 884744 | tf_op jit(solution)/shard_map/ppermute | solution.py:15
  22.6 21.4 %collective-permute-start.14 = (bf16[12,24,512]{2,1,0:T(8,128)(2,1)S(1)}, bf16[12,24,512]{2,1,0:T(8,128)(2,1)S(1)}, u32[]{:S(2)}, u32[]{:S(2)}) collective-permute-start(bf16[12,24,512]{2,1,0:T(8,128)(2,1)S(1)} %collective-permute-done.13.refs_0_), channel_id=1, source_target_pairs={{0,4},{4,0},{8,12},{12,8},{16,20},{20,16},{24,28},{28,24},{1,5},{5... | collective-permute-start | bytes 884744 | tf_op jit(solution)/shard_map/ppermute | solution.py:15
  39.6 15.2 %collective-permute-start.10 = (bf16[12,24,512]{2,1,0:T(8,128)(2,1)S(1)}, bf16[12,24,512]{2,1,0:T(8,128)(2,1)S(1)}, u32[]{:S(2)}, u32[]{:S(2)}) collective-permute-start(bf16[12,24,512]{2,1,0:T(8,128)(2,1)S(1)} %collective-permute-done.9.refs_0_), channel_id=1, source_target_pairs={{0,4},{4,0},{8,12},{12,8},{16,20},{20,16},{24,28},{28,24},{1,5},{5... | collective-permute-start | bytes 884744 | tf_op jit(solution)/shard_map/ppermute | solution.py:15
  41.2 28.6 %collective-permute-start.1 = (bf16[12,24,512]{2,1,0:T(8,128)(2,1)S(1)}, bf16[12,24,512]{2,1,0:T(8,128)(2,1)S(1)}, u32[]{:S(2)}, u32[]{:S(2)}) collective-permute-start(bf16[12,24,512]{2,1,0:T(8,128)(2,1)S(1)} %pad_maximum_fusion.refs_0_), channel_id=1, source_target_pairs={{0,4},{4,0},{8,12},{12,8},{16,20},{20,16},{24,28},{28,24},{1,5},{5... | collective-permute-start | bytes 884744 | tf_op jit(solution)/shard_map/ppermute | solution.py:15
  41.7 20.1 %collective-permute-start.6 = (bf16[12,24,512]{2,1,0:T(8,128)(2,1)S(1)}, bf16[12,24,512]{2,1,0:T(8,128)(2,1)S(1)}, u32[]{:S(2)}, u32[]{:S(2)}) collective-permute-start(bf16[12,24,512]{2,1,0:T(8,128)(2,1)S(1)} %collective-permute-done.5.refs_0_), channel_id=1, source_target_pairs={{0,4},{4,0},{8,12},{12,8},{16,20},{20,16},{24,28},{28,24},{1,5},{5... | collective-permute-start | bytes 884744 | tf_op jit(solution)/shard_map/ppermute | solution.py:15
  53.2 23.7 %collective-permute-start.15 = (bf16[8,24,1024]{2,1,0:T(8,128)(2,1)S(1)}, bf16[8,24,1024]{2,1,0:T(8,128)(2,1)S(1)}, u32[]{:S(2)}, u32[]{:S(2)}) collective-permute-start(bf16[8,24,1024]{2,1,0:T(8,128)(2,1)S(1)} %get-tuple-element.53), channel_id=1, source_target_pairs={{0,2},{1,3},{2,0},{3,1},{4,6},{5,7},{6,4},{7,5},{8,10},{9,11},{10,... | collective-permute-start | bytes 1179656 | tf_op jit(solution)/shard_map/ppermute | solution.py:20
  61.2 17.5 %collective-permute-start.11 = (bf16[8,24,1024]{2,1,0:T(8,128)(2,1)S(1)}, bf16[8,24,1024]{2,1,0:T(8,128)(2,1)S(1)}, u32[]{:S(2)}, u32[]{:S(2)}) collective-permute-start(bf16[8,24,1024]{2,1,0:T(8,128)(2,1)S(1)} %get-tuple-element.48), channel_id=1, source_target_pairs={{0,2},{1,3},{2,0},{3,1},{4,6},{5,7},{6,4},{7,5},{8,10},{9,11},{10,... | collective-permute-start | bytes 1179656 | tf_op jit(solution)/shard_map/ppermute | solution.py:20
  68.3 13.1 %collective-permute-start.7 = (bf16[8,24,1024]{2,1,0:T(8,128)(2,1)S(1)}, bf16[8,24,1024]{2,1,0:T(8,128)(2,1)S(1)}, u32[]{:S(2)}, u32[]{:S(2)}) collective-permute-start(bf16[8,24,1024]{2,1,0:T(8,128)(2,1)S(1)} %get-tuple-element.43), channel_id=1, source_target_pairs={{0,2},{1,3},{2,0},{3,1},{4,6},{5,7},{6,4},{7,5},{8,10},{9,11},{10,... | collective-permute-start | bytes 1179656 | tf_op jit(solution)/shard_map/ppermute | solution.py:20
  76.2 11.7 %collective-permute-start.3 = (bf16[8,24,1024]{2,1,0:T(8,128)(2,1)S(1)}, bf16[8,24,1024]{2,1,0:T(8,128)(2,1)S(1)}, u32[]{:S(2)}, u32[]{:S(2)}) collective-permute-start(bf16[8,24,1024]{2,1,0:T(8,128)(2,1)S(1)} %get-tuple-element.38), channel_id=1, source_target_pairs={{0,2},{1,3},{2,0},{3,1},{4,6},{5,7},{6,4},{7,5},{8,10},{9,11},{10,... | collective-permute-start | bytes 1179656 | tf_op jit(solution)/shard_map/ppermute | solution.py:20
  78.1 11.6 %collective-permute-start.16 = (bf16[48,24,128]{2,1,0:T(8,128)(2,1)S(1)}, bf16[48,24,128]{2,1,0:T(8,128)(2,1)S(1)}, u32[]{:S(2)}, u32[]{:S(2)}) collective-permute-start(bf16[48,24,128]{2,1,0:T(8,128)(2,1)S(1)} %get-tuple-element.55), channel_id=1, source_target_pairs={{0,4},{4,0},{8,12},{12,8},{16,20},{20,16},{24,28},{28,24},{1,5},{5... | collective-permute-start | bytes 884744 | tf_op jit(solution)/shard_map/ppermute | solution.py:15
  79.9 14.5 %collective-permute-start.12 = (bf16[48,24,128]{2,1,0:T(8,128)(2,1)S(1)}, bf16[48,24,128]{2,1,0:T(8,128)(2,1)S(1)}, u32[]{:S(2)}, u32[]{:S(2)}) collective-permute-start(bf16[48,24,128]{2,1,0:T(8,128)(2,1)S(1)} %get-tuple-element.50), channel_id=1, source_target_pairs={{0,4},{4,0},{8,12},{12,8},{16,20},{20,16},{24,28},{28,24},{1,5},{5... | collective-permute-start | bytes 884744 | tf_op jit(solution)/shard_map/ppermute | solution.py:15
  82.7 17.7 %collective-permute-start.8 = (bf16[48,24,128]{2,1,0:T(8,128)(2,1)S(1)}, bf16[48,24,128]{2,1,0:T(8,128)(2,1)S(1)}, u32[]{:S(2)}, u32[]{:S(2)}) collective-permute-start(bf16[48,24,128]{2,1,0:T(8,128)(2,1)S(1)} %get-tuple-element.45), channel_id=1, source_target_pairs={{0,4},{4,0},{8,12},{12,8},{16,20},{20,16},{24,28},{28,24},{1,5},{5... | collective-permute-start | bytes 884744 | tf_op jit(solution)/shard_map/ppermute | solution.py:15
  89.1 14.4 %collective-permute-start.4 = (bf16[48,24,128]{2,1,0:T(8,128)(2,1)S(1)}, bf16[48,24,128]{2,1,0:T(8,128)(2,1)S(1)}, u32[]{:S(2)}, u32[]{:S(2)}) collective-permute-start(bf16[48,24,128]{2,1,0:T(8,128)(2,1)S(1)} %get-tuple-element.40), channel_id=1, source_target_pairs={{0,4},{4,0},{8,12},{12,8},{16,20},{20,16},{24,28},{28,24},{1,5},{5... | collective-permute-start | bytes 884744 | tf_op jit(solution)/shard_map/ppermute | solution.py:15
  89.8 13.8 %collective-permute-start.20 = (bf16[12,24,128]{2,1,0:T(8,128)(2,1)S(1)}, bf16[12,24,128]{2,1,0:T(8,128)(2,1)S(1)}, u32[]{:S(2)}, u32[]{:S(2)}) collective-permute-start(bf16[12,24,128]{2,1,0:T(8,128)(2,1)S(1)} %get-tuple-element.60), channel_id=1, source_target_pairs={{0,8},{4,12},{8,0},{12,4},{16,24},{20,28},{24,16},{28,20},{1,9},{5... | collective-permute-start | bytes 221192 | tf_op jit(solution)/shard_map/ppermute | solution.py:15
  89.8 15.9 %collective-permute-start.24 = (bf16[12,24,128]{2,1,0:T(8,128)(2,1)S(1)}, bf16[12,24,128]{2,1,0:T(8,128)(2,1)S(1)}, u32[]{:S(2)}, u32[]{:S(2)}) collective-permute-start(bf16[12,24,128]{2,1,0:T(8,128)(2,1)S(1)} %get-tuple-element.64), channel_id=1, source_target_pairs={{0,16},{4,20},{8,24},{12,28},{16,0},{20,4},{24,8},{28,12},{1,17},{... | collective-permute-start | bytes 221192 | tf_op jit(solution)/shard_map/ppermute | solution.py:15
  94.4 12.7 %collective-permute-start.28 = (bf16[12,24,128]{2,1,0:T(8,128)(2,1)S(1)}, bf16[12,24,128]{2,1,0:T(8,128)(2,1)S(1)}, u32[]{:S(2)}, u32[]{:S(2)}) collective-permute-start(bf16[12,24,128]{2,1,0:T(8,128)(2,1)S(1)} %get-tuple-element.68), channel_id=1, source_target_pairs={{0,24},{4,28},{8,16},{12,20},{16,8},{20,12},{24,0},{28,4},{1,25},{... | collective-permute-start | bytes 221192 | tf_op jit(solution)/shard_map/ppermute | solution.py:15
  103.5 11.4 %collective-permute-start.23 = (bf16[12,24,128]{2,1,0:T(8,128)(2,1)S(1)}, bf16[12,24,128]{2,1,0:T(8,128)(2,1)S(1)}, u32[]{:S(2)}, u32[]{:S(2)}) collective-permute-start(bf16[12,24,128]{2,1,0:T(8,128)(2,1)S(1)} %get-tuple-element.63), channel_id=1, source_target_pairs={{0,16},{4,20},{8,24},{12,28},{16,0},{20,4},{24,8},{28,12},{1,17},{... | collective-permute-start | bytes 221192 | tf_op jit(solution)/shard_map/ppermute | solution.py:15
  103.5 11.4 %collective-permute-start.27 = (bf16[12,24,128]{2,1,0:T(8,128)(2,1)S(1)}, bf16[12,24,128]{2,1,0:T(8,128)(2,1)S(1)}, u32[]{:S(2)}, u32[]{:S(2)}) collective-permute-start(bf16[12,24,128]{2,1,0:T(8,128)(2,1)S(1)} %get-tuple-element.67), channel_id=1, source_target_pairs={{0,24},{4,28},{8,16},{12,20},{16,8},{20,12},{24,0},{28,4},{1,25},{... | collective-permute-start | bytes 221192 | tf_op jit(solution)/shard_map/ppermute | solution.py:15
  105.8 11.5 %collective-permute-start.18 = (bf16[12,24,128]{2,1,0:T(8,128)(2,1)S(1)}, bf16[12,24,128]{2,1,0:T(8,128)(2,1)S(1)}, u32[]{:S(2)}, u32[]{:S(2)}) collective-permute-start(bf16[12,24,128]{2,1,0:T(8,128)(2,1)S(1)} %get-tuple-element.58), channel_id=1, source_target_pairs={{0,8},{4,12},{8,0},{12,4},{16,24},{20,28},{24,16},{28,20},{1,9},{5... | collective-permute-start | bytes 221192 | tf_op jit(solution)/shard_map/ppermute | solution.py:15
  107.1 12.3 %collective-permute-start.22 = (bf16[12,24,128]{2,1,0:T(8,128)(2,1)S(1)}, bf16[12,24,128]{2,1,0:T(8,128)(2,1)S(1)}, u32[]{:S(2)}, u32[]{:S(2)}) collective-permute-start(bf16[12,24,128]{2,1,0:T(8,128)(2,1)S(1)} %get-tuple-element.62), channel_id=1, source_target_pairs={{0,16},{4,20},{8,24},{12,28},{16,0},{20,4},{24,8},{28,12},{1,17},{... | collective-permute-start | bytes 221192 | tf_op jit(solution)/shard_map/ppermute | solution.py:15
  108.1 11.3 %collective-permute-start.26 = (bf16[12,24,128]{2,1,0:T(8,128)(2,1)S(1)}, bf16[12,24,128]{2,1,0:T(8,128)(2,1)S(1)}, u32[]{:S(2)}, u32[]{:S(2)}) collective-permute-start(bf16[12,24,128]{2,1,0:T(8,128)(2,1)S(1)} %get-tuple-element.66), channel_id=1, source_target_pairs={{0,24},{4,28},{8,16},{12,20},{16,8},{20,12},{24,0},{28,4},{1,25},{... | collective-permute-start | bytes 221192 | tf_op jit(solution)/shard_map/ppermute | solution.py:15
  (9 other events, 51.8 us)

commit v2 on v0

v2 whole, which is shorter than its diff:
```python
import functools

import jax
import jax.numpy as jnp
from jax import lax
from jax.experimental import pallas as pl
from jax.experimental.pallas import tpu as pltpu
from jax.sharding import PartitionSpec as P

LANES = 128
SMEM = pl.BlockSpec(memory_space=pltpu.SMEM)
VMEM = pl.BlockSpec(memory_space=pltpu.VMEM)
ANY = pl.BlockSpec(memory_space=pl.ANY)
GRANT = 32 * 2**20
WEIGHT = 20_000_000_000


def blk_swap(value, dz, dx, nz, nx):
    pairs = [(z * nx + x, (z ^ dz) * nx + (x ^ dx)) for z in range(nz) for x in range(nx)]
    return lax.ppermute(value, "blk", pairs)


def slab_swap(value, dx, dy, nz, nx, ny, nc):
    pairs = [
        (((z * nx + x) * ny + y) * nc + c, ((z * nx + (x ^ dx)) * ny + (y ^ dy)) * nc + c)
        for z in range(nz)
        for x in range(nx)
        for y in range(ny)
        for c in range(nc)
    ]
    return lax.ppermute(value, ("blk", "pair"), pairs)


def pair_swap(value, dy, dc, ny, nc):
    pairs = [(y * nc + c, (y ^ dy) * nc + (c ^ dc)) for y in range(ny) for c in range(nc)]
    return lax.ppermute(value, "pair", pairs)


def pick(position, options):
    value = options[0]
    for index in range(1, len(options)):
        value = jnp.where(position == index, options[index], value)
    return value


def bf16(*shape):
    return jax.ShapeDtypeStruct(shape, jnp.bfloat16)


class Step:
    def __init__(self, body, scalars, arrays, outs, scratch=()):
        self.body, self.scalars, self.arrays = body, list(scalars), list(arrays)
        self.outs, self.scratch = list(outs), list(scratch)


def launch(name, steps, after):
    scalars, arrays = [], []
    for step in steps:
        for value in step.scalars:
            if not any(value is other for other in scalars):
                scalars.append(value)
        for value in step.arrays:
            if not any(value is other for other in arrays):
                arrays.append(value)
    operands = scalars + arrays
    find = lambda value: next(i for i, other in enumerate(operands) if other is value)
    outs = [out for step in steps for out in step.outs]
    scratch = [s for step in steps for s in step.scratch]

    def kernel(*refs):
        out_refs = refs[len(operands) + len(after) :]
        scratch_refs = out_refs[len(outs) :]
        o = s = 0
        for step in steps:
            step.body(
                [refs[find(value)] for value in step.scalars],
                [refs[find(value)] for value in step.arrays],
                out_refs[o : o + len(step.outs)],
                scratch_refs[s : s + len(step.scratch)],
            )
            o, s = o + len(step.outs), s + len(step.scratch)

    results = pl.pallas_call(
        kernel,
        in_specs=[SMEM] * len(scalars) + [VMEM] * len(arrays) + [ANY] * len(after),
        out_specs=[VMEM] * len(outs),
        out_shape=outs,
        scratch_shapes=scratch,
        cost_estimate=pl.CostEstimate(flops=WEIGHT, bytes_accessed=0, transcendentals=0),
        compiler_params=pltpu.CompilerParams(vmem_limit_bytes=GRANT),
        name=name,
    )(*operands, *after)
    split, o = [], 0
    for step in steps:
        split.append(results[o : o + len(step.outs)])
        o += len(step.outs)
    return split


class Meta:
    def __init__(self, slots):
        self.ctile, self.atile, self.keep = 0, slots, 2 * slots
        self.x, self.c, self.z = (3 * slots + i for i in range(3))


def join(parts):
    tiles, rows, columns = parts[0].shape

    def body(_, refs, outs, __):
        outs[0][...] = jnp.concatenate([ref[...] for ref in refs], axis=1)

    return Step(body, [], parts, [bf16(tiles, rows * len(parts), columns)])


def hold(values, after):
    def kernel(*refs):
        sources, outs, sems = refs[: len(values)], refs[len(values) + len(after) : -1], refs[-1]
        copies = [pltpu.make_async_copy(s, o, sems.at[i]) for i, (s, o) in enumerate(zip(sources, outs, strict=True))]
        for copy in copies:
            copy.start()
        for copy in copies:
            copy.wait()

    return pl.pallas_call(
        kernel,
        in_specs=[ANY] * (len(values) + len(after)),
        out_specs=[VMEM] * len(values),
        out_shape=[bf16(*value.shape) for value in values],
        scratch_shapes=[pltpu.SemaphoreType.DMA((len(values),))],
        cost_estimate=pl.CostEstimate(flops=WEIGHT, bytes_accessed=0, transcendentals=0),
        compiler_params=pltpu.CompilerParams(vmem_limit_bytes=GRANT),
        name="hold",
    )(*values, *after)


def pack(ctile, here):
    slots = ctile.shape[0]

    def body(scalars, refs, outs, _):
        for k in range(slots):
            outs[0][k] = refs[0][scalars[0][k]]

    return Step(body, [ctile], [here], [bf16(slots, *here.shape[1:])])


def through(value):
    def body(_, refs, outs, __):
        outs[0][...] = refs[0][...]

    return Step(body, [], [value], [bf16(*value.shape)])


def products(meta, at, here, others, blocks, ny, rows):
    nx, nc = 1 + len(others), len(blocks)
    slots, depth, width = blocks[0].shape
    whole = isinstance(others[0], list)
    flat = [o for other in others for o in other] if whole else list(others)
    each = len(others[0]) if whole else 1

    def body(scalars, refs, outs, _):
        meta_ref = scalars[0]
        here_ref, other_refs, block_refs = refs[0], refs[1 : 1 + len(flat)], refs[1 + len(flat) :]
        x, c = meta_ref[at.x], meta_ref[at.c]
        for k in range(slots):
            tile = meta_ref[at.ctile + k]
            parts = [here_ref[tile]]
            for d in range(nx - 1):
                pieces = [ref[tile if whole else k] for ref in other_refs[d * each : (d + 1) * each]]
                parts.append(jnp.concatenate(pieces, axis=0) if whole else pieces[0])
            lhs = jnp.concatenate([pick(x ^ i, parts) for i in range(nx)], axis=0)
            total = None
            for d in range(nc):
                columns = pick(c ^ d, [lhs[:, i * depth : (i + 1) * depth] for i in range(nc)])
                term = jnp.dot(columns, block_refs[d][k], preferred_element_type=jnp.float32)
                total = term if total is None else total + term
            total = total * meta_ref[at.keep + k].astype(jnp.float32)
            for s in range(ny):
                pieces = [total[(i * ny + s) * rows : (i * ny + s + 1) * rows] for i in range(nx)]
                outs[s][k] = jnp.concatenate(pieces, axis=0).astype(outs[s].dtype)

    return Step(body, [meta], [here, *flat, *blocks], [bf16(slots, nx * rows, width)] * ny)


def route(meta, at, slot_tile, parts, tile_count, nx, nz):
    slots, rows, width = parts[0].shape
    owned = slot_tile.shape[0] // (nx * nz)
    per_tile = width // LANES

    def body(scalars, refs, outs, scratch):
        meta_ref, slot_ref = scalars
        total = scratch[0]
        x, z = meta_ref[at.x], meta_ref[at.z]
        total[...] = jnp.zeros_like(total)

        def add(k, _):
            value = refs[0][k].astype(jnp.float32)
            for ref in refs[1:]:
                value += ref[k].astype(jnp.float32)
            total[meta_ref[at.atile + k]] += value
            return 0

        lax.fori_loop(0, slots, add, 0)
        for d in range(nx):
            for dz in range(nz):
                owner = (z ^ dz) * nx + (x ^ d)
                for i in range(owned):
                    tile = slot_ref[owner * owned + i]
                    a = lax.div(tile, per_tile)
                    column = pl.multiple_of(lax.rem(tile, per_tile) * LANES, LANES)
                    outs[d][dz * owned + i] = total[a, :, pl.ds(column, LANES)].astype(outs[d].dtype)

    scratch = [pltpu.VMEM((tile_count, rows, width), jnp.float32)]
    return Step(body, [meta, slot_tile], parts, [bf16(nz * owned, rows, LANES)] * nx, scratch)


def add_split(chunks, nz):
    tiles, rows, lanes = chunks[0][0].shape
    count, each = tiles // nz, len(chunks[0])

    def body(_, refs, outs, __):
        for i in range(len(chunks)):
            for e, out in enumerate(outs):
                span = slice(e * count, (e + 1) * count)
                value = refs[i * each][span].astype(jnp.float32)
                for part in refs[i * each + 1 : (i + 1) * each]:
                    value += part[span].astype(jnp.float32)
                out[:, i] = value.astype(out.dtype)

    flat = [part for chunk in chunks for part in chunk]
    return Step(body, [], flat, [bf16(count, len(chunks), rows, lanes)] * nz)


def final_sum(meta, at, received, groups, nz):
    owned, _, rows, lanes = received[0][0].shape
    where = {d: (g, i) for g, group in enumerate(groups) for i, d in enumerate(group)}

    def body(scalars, refs, outs, _):
        z = scalars[0][at.z]
        for ahead in range(nz):
            value = None
            for e in range(nz):
                g, i = where[e ^ ahead]
                term = refs[g * nz + e][:, i].astype(jnp.float32)
                value = term if value is None else value + term
            outs[0][:, z ^ ahead] = value.astype(outs[0].dtype)

    flat = [part for line in received for part in line]
    return Step(body, [meta], flat, [bf16(owned, nz, rows, lanes)])


def per_device(nz, nx, ny, nc, amplitudes, tile_mask, integrals, block_tiles, block_keep, slot_tile):
    blk, pair = lax.axis_index("blk"), lax.axis_index("pair")
    z, x, y, c = blk // nx, blk % nx, pair // nc, pair % nc
    _, rows, tile_count, contracted = amplitudes.shape
    slots = block_keep.shape[0]
    columns = contracted // ny
    at = Meta(slots)

    blocks = [integrals] + [pair_swap(integrals, 0, d, ny, nc) for d in range(1, nc)]
    ctile = block_tiles[:, 0]
    place = jnp.stack([x, c, z]).astype(jnp.int32)
    meta = jnp.concatenate([ctile, block_tiles[:, 1], block_keep, place])
    their_ctile = [blk_swap(ctile, 0, d, nz, nx) for d in range(1, nx)]

    masked = amplitudes[0] * tile_mask[0].astype(jnp.bfloat16)[:, :, None]
    masked = masked.transpose(1, 0, 2)
    pieces = [lax.dynamic_slice_in_dim(masked, (y ^ d) * columns, columns, axis=2) for d in range(ny)]

    here, others, partial, by_owner, received = {}, {}, {}, {}, []
    last = []

    def run(name, *steps):
        nonlocal last
        results = launch(name, [step for step, _ in steps], last)
        last = results[0][:1]
        for (_, use), result in zip(steps, results, strict=True):
            use(result)

    def do_join(from_y):
        def use(out):
            here[0] = out[0]
            here[1] = blk_swap(out[0], 1, 0, nz, nx)

        return join(from_y), use

    def do_relay(d, s):
        def use(out):
            others[0][d - 1].append(blk_swap(out[0], 0, d, nz, nx))

        return through(from_y[s]), use

    def do_spread():
        def use(out):
            for d in range(2, nz):
                if d & -d == d:
                    here[d] = blk_swap(out[0], d, 0, nz, nx)

        return through(here[0]), use

    def do_pack(d, i):
        def use(out):
            others.setdefault(d, {})[i] = blk_swap(out[0], 0, i, nz, nx)

        return pack(their_ctile[i - 1], here[d]), use

    def do_forward(d):
        def use(out):
            for step in range(1, d & -d):
                if step & -step == step:
                    here[d | step] = blk_swap(out[0], step, 0, nz, nx)

        return through(here[d]), use

    def do_products(d):
        def use(out):
            partial[d] = [out[0]] + [pair_swap(out[i], i, 0, ny, nc) for i in range(1, ny)]

        rest = others[d] if isinstance(others[d], list) else [others[d][i] for i in range(1, nx)]
        return products(meta, at, here[d], rest, blocks, ny, rows), use

    def do_route(d):
        def use(out):
            by_owner[d] = [out[0]] + [blk_swap(out[i], 0, i, nz, nx) for i in range(1, nx)]

        return route(meta, at, slot_tile, partial[d], tile_count, nx, nz), use

    def do_add(group):
        def use(out):
            received.append([out[0]] + [blk_swap(out[e], e, 0, nz, nx) for e in range(1, nz)])

        return add_split([by_owner[d] for d in group], nz), use

    from_y = [pieces[0]] + [pair_swap(pieces[d], d, 0, ny, nc) for d in range(1, ny)]
    others[0] = [[blk_swap(from_y[0], 0, dx, nz, nx)] for dx in range(1, nx)]
    blocks = [blocks[0], *hold(blocks[1:], pieces[:1])] if nc > 1 else blocks
    last = blocks[1:2]
    run("join", do_join(from_y), *[do_relay(d, s) for d in range(1, nx) for s in range(1, ny)])
    last = [last[0], *[other[0] for other in others[0]]]
    run("spread", do_spread())
    slots_of, groups = plan(nz)
    for slot in slots_of:
        steps = []
        for what, d in slot:
            if what == "arrive":
                steps += [do_pack(d, i) for i in range(1, nx)]
            elif what == "forward":
                steps.append(do_forward(d))
            else:
                steps.append({"multiply": do_products, "route": do_route, "add": do_add}[what](d))
        run("_".join(what for what, _ in slot), *steps)
    out = launch("final_sum", [final_sum(meta, at, received, groups, nz)], last)[0][0]
    return out.reshape(out.shape[0], 1, out.shape[1] * out.shape[2], LANES)


def plan(nz):
    m, r, a, f, s = "multiply", "route", "arrive", "forward", "add"
    if nz == 4:
        return [
            [(m, 0)],
            [(a, 1)],
            [(f, 2)],
            [(r, 0)],
            [(a, 2)],
            [(m, 1)],
            [(m, 2), (a, 3)],
            [(r, 1)],
            [(m, 3)],
            [(r, 2), (s, (0, 1))],
            [(r, 3)],
            [(s, (2,))],
            [(s, (3,))],
        ], [(0, 1), (2,), (3,)]
    slots = [[(m, 0)]]
    for d in range(1, nz):
        slots.append([(a, d)] + ([(f, d)] if d & -d > 1 else []))
        slots.append([(m, d), (r, d - 1)])
    slots += [[(r, nz - 1)]] + [[(s, (d,))] for d in range(nz)]
    return slots, [(d,) for d in range(nz)]


def solution(mesh):
    holders, pairs = mesh.shape["blk"], mesh.shape["pair"]
    nx = 1
    while (2 * nx) ** 2 <= holders:
        nx *= 2
    nc = 2 if pairs % 2 == 0 else 1
    placed = (
        P("pair", "blk", None, None),
        P("pair", "blk", None),
        P("blk", "pair", None),
        P("blk", None),
        P("blk"),
        P(),
    )
    return jax.shard_map(
        functools.partial(per_device, holders // nx, nx, pairs // nc, nc),
        mesh=mesh,
        in_specs=placed,
        out_specs=P("blk", "pair", None, None),
        check_vma=False,
    )
```

time: 269 us -> 87.4 us (0.32)
  waiting for transfers between devices: 165 us -> 27.4 us
  blocking collectives: 59.5 us -> 0 us
  starting transfers between devices: 0.04 us -> 37.8 us
  Pallas kernels: 0 us -> 18.3 us
  between operations: 13.5 us -> 0.16 us
  matrix products: 12.9 us -> 0 us
  local copies, waits for them, and re-layouts: 14.5 us -> 1.63 us
    all_gather x2 -> x0, waiting for transfers between devices: 164 us -> none  [the longest x1 101 us: per_device(): lax.all_gather(integrals, 'pair', axis=1, tiled=True)]
    all_to_all x1 -> x0, blocking collectives: 59.5 us -> none  [per_device(): lax.all_to_all(by_slot, 'blk', split_axis=0, concat_axis=0, tiled=True)]
    ppermute x0 -> x28, starting transfers between devices: none -> 37.8 us  [the longest x22 29.7 us: blk_swap(): return lax.ppermute(value, 'blk', pairs)]
    ppermute x0 -> x28, waiting for transfers between devices: none -> 27.4 us  [the longest x22 21.5 us: blk_swap(): return lax.ppermute(value, 'blk', pairs)]
    pallas_call x0 -> x17, Pallas kernels: none -> 18.3 us  [the longest x16 16.1 us: launch(): pl.pallas_call(kernel, in_specs=[SMEM] * len(scalars) + [VMEM] * len(arra...]
    dot_general x2 -> x0, matrix products: 12.9 us -> none  [the longest x1 9.13 us: per_device(): jnp.einsum('rkd,kde->kre', picked, lax.all_gather(integrals, 'pair', axis...]
    gather x2 -> x0, local copies, waits for them, and re-layouts: 4.46 us -> none  [the longest x1 2.66 us: per_device(): by_slot = jnp.take(tile_rows, slot_tile, axis=0)]
    transpose x1 -> x0, local copies, waits for them, and re-layouts: 3.98 us -> none  [per_device(): tile_rows = per_tile.reshape(tile_count, rows_all, BW, TV).transpose(0, 2...]
  transfers between devices with their start and end apart: 2 -> 28, of which waited for: 2 -> 15; matrix products, arithmetic and copies ran while one was open for 2% -> 4% of each run, Pallas kernels for 0% -> 19%
where the time goes in v2:
time: 87.4 us; the launch traced here: 87.2 us
  starting transfers between devices  37.8 us (43%)
  waiting for transfers between devices  27.4 us (31%)
  Pallas kernels  18.3 us (21%)
  other arithmetic  1.88 us (2%)
  local copies, waits for them, and re-layouts  1.63 us (2%)
    ppermute x22, starting transfers between devices, blk_swap(): return lax.ppermute(value, 'blk', pairs)  29.7 us
    ppermute x22, waiting for transfers between devices, blk_swap(): return lax.ppermute(value, 'blk', pairs)  21.5 us
    pallas_call x16, Pallas kernels, launch(): pl.pallas_call(kernel, in_specs=[SMEM] * len(scalars) + [VMEM] * len(arra...  16.1 us
    ppermute x6, starting transfers between devices, pair_swap(): return lax.ppermute(value, 'pair', pairs)  8.12 us
    ppermute x6, waiting for transfers between devices, pair_swap(): return lax.ppermute(value, 'pair', pairs)  5.89 us
    pallas_call x1, Pallas kernels, hold(): pl.pallas_call(kernel, in_specs=[ANY] * (len(values) + len(after)), out_s...  2.2 us
  transfers between devices with their start and end apart: 28, of which 15 were waited for; matrix products, arithmetic and copies ran while one was open for 4% of the time, Pallas kernels for 19%

profile of v2, /device:TPU:0, one launch (start us, length us, event | category | flops | bytes accessed | tf_op | source)
XLA Modules:
  0.0 87.2 jit_solution(4821243926682435418)
XLA Ops:
  1.2 2.5 %collective-permute-start = (s32[8]{0:T(128)S(1)}, s32[8]{0:T(128)S(1)}, u32[]{:S(2)}, u32[]{:S(2)}) collective-permute-start(s32[8]{0:T(128)S(1)} %get-tuple-element.70), channel_id=1, source_target_pairs={{0,4},{4,0},{8,12},{12,8},{16,20},{20,16},{24,28},{28,24},{1,5},{5... | collective-permute-start | bytes 104 | tf_op jit(solution)/shard_map/ppermute | solution.py:20
  5.7 1.6 %collective-permute-start.1 = (bf16[12,12,512]{2,1,0:T(8,128)(2,1)S(1)}, bf16[12,12,512]{2,1,0:T(8,128)(2,1)S(1)}, u32[]{:S(2)}, u32[]{:S(2)}) collective-permute-start(bf16[12,12,512]{2,1,0:T(8,128)(2,1)S(1)} %get-tuple-element.67), channel_id=1, source_target_pairs={{0,2},{1,3},{2,0},{3,1},{4,6},{5,7},{6,4},{7,5},{8,10},{9,11},{10,... | collective-permute-start | bytes 442376 | tf_op jit(solution)/shard_map/ppermute | solution.py:36
  8.6 2.2 %hold.1.refs_2_.refs_5_.refs_4_ = bf16[8,256,1024]{2,1,0:T(8,128)(2,1)S(1)} custom-call(bf16[8,256,1024]{2,1,0:T(8,128)(2,1)} %collective-permute-done.2.refs_0_, bf16[12,12,512]{2,1,0:T(8,128)(2,1)S(1)} %get-tuple-element.68.refs_1_.refs_0_), custom_call_target="tpu_custom_call" | custom-call | flops 20000000000 | tf_op jit(solution)/shard_map/hold/pallas_call | solution.py:124
  10.8 2.0 %collective-permute-done.1.refs_1_ = bf16[12,12,512]{2,1,0:T(8,128)(2,1)S(1)} collective-permute-done((bf16[12,12,512]{2,1,0:T(8,128)(2,1)S(1)}, bf16[12,12,512]{2,1,0:T(8,128)(2,1)S(1)}, u32[]{:S(2)}, u32[]{:S(2)}) %collective-permute-start.1) | collective-permute-done | bytes 147488 | tf_op jit(solution)/shard_map/ppermute | solution.py:36
  13.3 1.8 %collective-permute-start.7 = (bf16[12,24,512]{2,1,0:T(8,128)(2,1)S(1)}, bf16[12,24,512]{2,1,0:T(8,128)(2,1)S(1)}, u32[]{:S(2)}, u32[]{:S(2)}) collective-permute-start(bf16[12,24,512]{2,1,0:T(8,128)(2,1)S(1)} %get-tuple-element.36.refs_0_.refs_1_), channel_id=1, source_target_pairs={{0,8},{4,12},{8,0},{12,4},{16,24},{20,28},{24,16},{28,20},{1,9},{5... | collective-permute-start | bytes 884744 | tf_op jit(solution)/shard_map/ppermute | solution.py:20
  15.1 2.7 %collective-permute-start.4 = (bf16[12,24,512]{2,1,0:T(8,128)(2,1)S(1)}, bf16[12,24,512]{2,1,0:T(8,128)(2,1)S(1)}, u32[]{:S(2)}, u32[]{:S(2)}) collective-permute-start(bf16[12,24,512]{2,1,0:T(8,128)(2,1)S(1)} %spread.1.refs_6_), channel_id=1, source_target_pairs={{0,16},{4,20},{8,24},{12,28},{16,0},{20,4},{24,8},{28,12},{1,17},{... | collective-permute-start | bytes 884744 | tf_op jit(solution)/shard_map/ppermute | solution.py:20
  19.2 2.1 %multiply.3 = (bf16[8,24,1024]{2,1,0:T(8,128)(2,1)S(1)}, bf16[8,24,1024]{2,1,0:T(8,128)(2,1)S(1)}) custom-call(s32[27]{0:T(128)S(1)} %concatenate.3.refs_0_, bf16[12,24,512]{2,1,0:T(8,128)(2,1)S(1)} %get-tuple-element.36.refs_0_.refs_1_, bf16[12,12,512]{2,1,0:T(8,128)(2,1)S(1)} %collective-permute-done.3.refs_2_, ...), custom_call_target="tpu_custom_call" | custom-call | flops 20000000000 | tf_op jit(solution)/shard_map/multiply/pallas_call | solution.py:83
  21.3 1.6 %collective-permute-start.6 = (bf16[8,24,1024]{2,1,0:T(8,128)(2,1)S(1)}, bf16[8,24,1024]{2,1,0:T(8,128)(2,1)S(1)}, u32[]{:S(2)}, u32[]{:S(2)}) collective-permute-start(bf16[8,24,1024]{2,1,0:T(8,128)(2,1)S(1)} %get-tuple-element.39), channel_id=1, source_target_pairs={{0,2},{1,3},{2,0},{3,1},{4,6},{5,7},{6,4},{7,5},{8,10},{9,11},{10,... | collective-permute-start | bytes 1179656 | tf_op jit(solution)/shard_map/ppermute | solution.py:36
  22.9 4.8 %collective-permute-done.7.refs_1_ = bf16[12,24,512]{2,1,0:T(8,128)(2,1)S(1)} collective-permute-done((bf16[12,24,512]{2,1,0:T(8,128)(2,1)S(1)}, bf16[12,24,512]{2,1,0:T(8,128)(2,1)S(1)}, u32[]{:S(2)}, u32[]{:S(2)}) %collective-permute-start.7) | collective-permute-done | bytes 294944 | tf_op jit(solution)/shard_map/ppermute | solution.py:20
  35.1 2.1 %multiply.4 = (bf16[8,24,1024]{2,1,0:T(8,128)(2,1)S(1)}, bf16[8,24,1024]{2,1,0:T(8,128)(2,1)S(1)}) custom-call(s32[27]{0:T(128)S(1)} %concatenate.3.refs_0_, bf16[12,24,512]{2,1,0:T(8,128)(2,1)S(1)} %collective-permute-done.7.refs_1_, bf16[8,24,512]{2,1,0:T(8,128)(2,1)S(1)} %collective-permute-done.10.refs_2_, bf16[8,256,1024]{2,1,0:T(8,128)(2,1)S(1)} %copy-done, ...), custom_call_target="tpu_custom_call" | custom-call | flops 20000000000 | tf_op jit(solution)/shard_map/multiply/pallas_call | solution.py:83
  38.7 1.9 %collective-permute-done.8.refs_3_ = bf16[8,24,512]{2,1,0:T(8,128)(2,1)S(1)} collective-permute-done((bf16[8,24,512]{2,1,0:T(8,128)(2,1)S(1)}, bf16[8,24,512]{2,1,0:T(8,128)(2,1)S(1)}, u32[]{:S(2)}, u32[]{:S(2)}) %collective-permute-start.8) | collective-permute-done | bytes 196640 | tf_op jit(solution)/shard_map/ppermute | solution.py:20
  40.6 2.1 %multiply_arrive.1 = (bf16[8,24,1024]{2,1,0:T(8,128)(2,1)S(1)}, bf16[8,24,1024]{2,1,0:T(8,128)(2,1)S(1)}, bf16[8,24,512]{2,1,0:T(8,128)(2,1)S(1)}) custom-call(s32[27]{0:T(128)S(1)} %concatenate.3.refs_0_, s32[8]{0:T(128)S(1)} %collective-permute-done.refs_0_.refs_1_, bf16[12,24,512]{2,1,0:T(8,128)(2,1)S(1)} %collective-permute-done.4.refs_0_.refs_1_.refs_2_, ...), custom_call_target="tpu_custom_call" | custom-call | flops 20000000000 | tf_op jit(solution)/shard_map/multiply_arrive/pallas_call | solution.py:83
  42.7 1.6 %collective-permute-start.11 = (bf16[8,24,1024]{2,1,0:T(8,128)(2,1)S(1)}, bf16[8,24,1024]{2,1,0:T(8,128)(2,1)S(1)}, u32[]{:S(2)}, u32[]{:S(2)}) collective-permute-start(bf16[8,24,1024]{2,1,0:T(8,128)(2,1)S(1)} %get-tuple-element.43), channel_id=1, source_target_pairs={{0,2},{1,3},{2,0},{3,1},{4,6},{5,7},{6,4},{7,5},{8,10},{9,11},{10,... | collective-permute-start | bytes 1179656 | tf_op jit(solution)/shard_map/ppermute | solution.py:36
  45.5 3.6 %collective-permute-done.13.refs_3_ = bf16[8,24,1024]{2,1,0:T(8,128)(2,1)S(1)} collective-permute-done((bf16[8,24,1024]{2,1,0:T(8,128)(2,1)S(1)}, bf16[8,24,1024]{2,1,0:T(8,128)(2,1)S(1)}, u32[]{:S(2)}, u32[]{:S(2)}) %collective-permute-start.13) | collective-permute-done | bytes 393248 | tf_op jit(solution)/shard_map/ppermute | solution.py:36
  50.3 1.5 %collective-permute-start.14 = (bf16[48,24,128]{2,1,0:T(8,128)(2,1)S(1)}, bf16[48,24,128]{2,1,0:T(8,128)(2,1)S(1)}, u32[]{:S(2)}, u32[]{:S(2)}) collective-permute-start(bf16[48,24,128]{2,1,0:T(8,128)(2,1)S(1)} %get-tuple-element.47), channel_id=1, source_target_pairs={{0,4},{4,0},{8,12},{12,8},{16,20},{20,16},{24,28},{28,24},{1,5},{5... | collective-permute-start | bytes 884744 | tf_op jit(solution)/shard_map/ppermute | solution.py:20
  51.9 2.1 %multiply.5 = (bf16[8,24,1024]{2,1,0:T(8,128)(2,1)S(1)}, bf16[8,24,1024]{2,1,0:T(8,128)(2,1)S(1)}) custom-call(s32[27]{0:T(128)S(1)} %concatenate.3.refs_0_, bf16[12,24,512]{2,1,0:T(8,128)(2,1)S(1)} %collective-permute-done.9.refs_6_.refs_1_, bf16[8,24,512]{2,1,0:T(8,128)(2,1)S(1)} %collective-permute-done.15.refs_2_, bf16[8,256,1024]{2,1,0:T(8,128)(2,1)S(1)} %copy-done, ...), custom_call_target="tpu_custom_call" | custom-call | flops 20000000000 | tf_op jit(solution)/shard_map/multiply/pallas_call | solution.py:83
  55.6 1.5 %collective-permute-done.14.refs_7_ = bf16[48,24,128]{2,1,0:T(8,128)(2,1)S(1)} collective-permute-done((bf16[48,24,128]{2,1,0:T(8,128)(2,1)S(1)}, bf16[48,24,128]{2,1,0:T(8,128)(2,1)S(1)}, u32[]{:S(2)}, u32[]{:S(2)}) %collective-permute-start.14) | collective-permute-done | bytes 294944 | tf_op jit(solution)/shard_map/ppermute | solution.py:20
  58.4 1.5 %collective-permute-start.16 = (bf16[12,2,24,128]{3,2,1,0:T(8,128)(2,1)S(1)}, bf16[12,2,24,128]{3,2,1,0:T(8,128)(2,1)S(1)}, u32[]{:S(2)}, u32[]{:S(2)}) collective-permute-start(bf16[12,2,24,128]{3,2,1,0:T(8,128)(2,1)S(1)} %get-tuple-element.51), channel_id=1, source_target_pairs={{0,8},{4,12},{8,0},{12,4},{16,24},{20,28},{24,16},{28,20},{1,9},{5... | collective-permute-start | bytes 442376 | tf_op jit(solution)/shard_map/ppermute | solution.py:20
  59.9 2.6 %collective-permute-start.17 = (bf16[12,2,24,128]{3,2,1,0:T(8,128)(2,1)S(1)}, bf16[12,2,24,128]{3,2,1,0:T(8,128)(2,1)S(1)}, u32[]{:S(2)}, u32[]{:S(2)}) collective-permute-start(bf16[12,2,24,128]{3,2,1,0:T(8,128)(2,1)S(1)} %get-tuple-element.52), channel_id=1, source_target_pairs={{0,16},{4,20},{8,24},{12,28},{16,0},{20,4},{24,8},{28,12},{1,17},{... | collective-permute-start | bytes 442376 | tf_op jit(solution)/shard_map/ppermute | solution.py:20
  66.4 3.4 %collective-permute-done.19.refs_1_ = bf16[48,24,128]{2,1,0:T(8,128)(2,1)S(1)} collective-permute-done((bf16[48,24,128]{2,1,0:T(8,128)(2,1)S(1)}, bf16[48,24,128]{2,1,0:T(8,128)(2,1)S(1)}, u32[]{:S(2)}, u32[]{:S(2)}) %collective-permute-start.19) | collective-permute-done | bytes 294944 | tf_op jit(solution)/shard_map/ppermute | solution.py:20
  70.6 2.5 %collective-permute-done.24.refs_1_ = bf16[48,24,128]{2,1,0:T(8,128)(2,1)S(1)} collective-permute-done((bf16[48,24,128]{2,1,0:T(8,128)(2,1)S(1)}, bf16[48,24,128]{2,1,0:T(8,128)(2,1)S(1)}, u32[]{:S(2)}, u32[]{:S(2)}) %collective-permute-start.24) | collective-permute-done | bytes 294944 | tf_op jit(solution)/shard_map/ppermute | solution.py:20
  73.0 2.0 %collective-permute-start.22 = (bf16[12,1,24,128]{3,2,1,0:T(8,128)(2,1)S(1)}, bf16[12,1,24,128]{3,2,1,0:T(8,128)(2,1)S(1)}, u32[]{:S(2)}, u32[]{:S(2)}) collective-permute-start(bf16[12,1,24,128]{3,2,1,0:T(8,128)(2,1)S(1)} %get-tuple-element.60), channel_id=1, source_target_pairs={{0,16},{4,20},{8,24},{12,28},{16,0},{20,4},{24,8},{28,12},{1,17},{... | collective-permute-start | bytes 221192 | tf_op jit(solution)/shard_map/ppermute | solution.py:20
  77.0 2.6 %collective-permute-start.26 = (bf16[12,1,24,128]{3,2,1,0:T(8,128)(2,1)S(1)}, bf16[12,1,24,128]{3,2,1,0:T(8,128)(2,1)S(1)}, u32[]{:S(2)}, u32[]{:S(2)}) collective-permute-start(bf16[12,1,24,128]{3,2,1,0:T(8,128)(2,1)S(1)} %get-tuple-element.65), channel_id=1, source_target_pairs={{0,16},{4,20},{8,24},{12,28},{16,0},{20,4},{24,8},{28,12},{1,17},{... | collective-permute-start | bytes 221192 | tf_op jit(solution)/shard_map/ppermute | solution.py:20
  82.3 3.5 %collective-permute-done.27.refs_12_ = bf16[12,1,24,128]{3,2,1,0:T(8,128)(2,1)S(1)} collective-permute-done((bf16[12,1,24,128]{3,2,1,0:T(8,128)(2,1)S(1)}, bf16[12,1,24,128]{3,2,1,0:T(8,128)(2,1)S(1)}, u32[]{:S(2)}, u32[]{:S(2)}) %collective-permute-start.27) | collective-permute-done | bytes 73760 | tf_op jit(solution)/shard_map/ppermute | solution.py:20
  (59 shorter events, 31.1 us)
Async XLA Ops:
  0.0 8.6 %collective-permute-start.2 = (bf16[8,256,1024]{2,1,0:T(8,128)(2,1)}, bf16[8,256,1024]{2,1,0:T(8,128)(2,1)}, u32[]{:S(2)}, u32[]{:S(2)}) collective-permute-start(bf16[8,256,1024]{2,1,0:T(8,128)(2,1)} %refs_3_.3), channel_id=1, source_target_pairs={{0,1},{1,0},{2,3},{3,2},{4,5},{5,4},{6,7},{7,6},{8,9},{9,8},{10,11... | collective-permute-start | bytes 12582920 | tf_op jit(solution)/shard_map/ppermute | solution.py:36
  1.2 21.7 %collective-permute-start = (s32[8]{0:T(128)S(1)}, s32[8]{0:T(128)S(1)}, u32[]{:S(2)}, u32[]{:S(2)}) collective-permute-start(s32[8]{0:T(128)S(1)} %get-tuple-element.70), channel_id=1, source_target_pairs={{0,4},{4,0},{8,12},{12,8},{16,20},{20,16},{24,28},{28,24},{1,5},{5... | collective-permute-start | bytes 104 | tf_op jit(solution)/shard_map/ppermute | solution.py:20
  5.7 7.1 %collective-permute-start.1 = (bf16[12,12,512]{2,1,0:T(8,128)(2,1)S(1)}, bf16[12,12,512]{2,1,0:T(8,128)(2,1)S(1)}, u32[]{:S(2)}, u32[]{:S(2)}) collective-permute-start(bf16[12,12,512]{2,1,0:T(8,128)(2,1)S(1)} %get-tuple-element.67), channel_id=1, source_target_pairs={{0,2},{1,3},{2,0},{3,1},{4,6},{5,7},{6,4},{7,5},{8,10},{9,11},{10,... | collective-permute-start | bytes 442376 | tf_op jit(solution)/shard_map/ppermute | solution.py:36
  7.3 7.7 %collective-permute-start.3 = (bf16[12,12,512]{2,1,0:T(8,128)(2,1)S(1)}, bf16[12,12,512]{2,1,0:T(8,128)(2,1)S(1)}, u32[]{:S(2)}, u32[]{:S(2)}) collective-permute-start(bf16[12,12,512]{2,1,0:T(8,128)(2,1)S(1)} %get-tuple-element.68.refs_1_.refs_0_), channel_id=1, source_target_pairs={{0,4},{4,0},{8,12},{12,8},{16,20},{20,16},{24,28},{28,24},{1,5},{5... | collective-permute-start | bytes 442376 | tf_op jit(solution)/shard_map/ppermute | solution.py:20
  13.3 14.5 %collective-permute-start.7 = (bf16[12,24,512]{2,1,0:T(8,128)(2,1)S(1)}, bf16[12,24,512]{2,1,0:T(8,128)(2,1)S(1)}, u32[]{:S(2)}, u32[]{:S(2)}) collective-permute-start(bf16[12,24,512]{2,1,0:T(8,128)(2,1)S(1)} %get-tuple-element.36.refs_0_.refs_1_), channel_id=1, source_target_pairs={{0,8},{4,12},{8,0},{12,4},{16,24},{20,28},{24,16},{28,20},{1,9},{5... | collective-permute-start | bytes 884744 | tf_op jit(solution)/shard_map/ppermute | solution.py:20
  15.1 15.1 %collective-permute-start.4 = (bf16[12,24,512]{2,1,0:T(8,128)(2,1)S(1)}, bf16[12,24,512]{2,1,0:T(8,128)(2,1)S(1)}, u32[]{:S(2)}, u32[]{:S(2)}) collective-permute-start(bf16[12,24,512]{2,1,0:T(8,128)(2,1)S(1)} %spread.1.refs_6_), channel_id=1, source_target_pairs={{0,16},{4,20},{8,24},{12,28},{16,0},{20,4},{24,8},{28,12},{1,17},{... | collective-permute-start | bytes 884744 | tf_op jit(solution)/shard_map/ppermute | solution.py:20
  21.3 9.6 %collective-permute-start.6 = (bf16[8,24,1024]{2,1,0:T(8,128)(2,1)S(1)}, bf16[8,24,1024]{2,1,0:T(8,128)(2,1)S(1)}, u32[]{:S(2)}, u32[]{:S(2)}) collective-permute-start(bf16[8,24,1024]{2,1,0:T(8,128)(2,1)S(1)} %get-tuple-element.39), channel_id=1, source_target_pairs={{0,2},{1,3},{2,0},{3,1},{4,6},{5,7},{6,4},{7,5},{8,10},{9,11},{10,... | collective-permute-start | bytes 1179656 | tf_op jit(solution)/shard_map/ppermute | solution.py:36
  28.3 6.8 %collective-permute-start.10 = (bf16[8,24,512]{2,1,0:T(8,128)(2,1)S(1)}, bf16[8,24,512]{2,1,0:T(8,128)(2,1)S(1)}, u32[]{:S(2)}, u32[]{:S(2)}) collective-permute-start(bf16[8,24,512]{2,1,0:T(8,128)(2,1)S(1)} %arrive.2.refs_1_), channel_id=1, source_target_pairs={{0,4},{4,0},{8,12},{12,8},{16,20},{20,16},{24,28},{28,24},{1,5},{5... | collective-permute-start | bytes 589832 | tf_op jit(solution)/shard_map/ppermute | solution.py:20
  30.2 8.5 %collective-permute-start.9 = (bf16[12,24,512]{2,1,0:T(8,128)(2,1)S(1)}, bf16[12,24,512]{2,1,0:T(8,128)(2,1)S(1)}, u32[]{:S(2)}, u32[]{:S(2)}) collective-permute-start(bf16[12,24,512]{2,1,0:T(8,128)(2,1)S(1)} %forward.1.refs_4_), channel_id=1, source_target_pairs={{0,8},{4,12},{8,0},{12,4},{16,24},{20,28},{24,16},{28,20},{1,9},{5... | collective-permute-start | bytes 884744 | tf_op jit(solution)/shard_map/ppermute | solution.py:20
  32.6 7.9 %collective-permute-start.8 = (bf16[8,24,512]{2,1,0:T(8,128)(2,1)S(1)}, bf16[8,24,512]{2,1,0:T(8,128)(2,1)S(1)}, u32[]{:S(2)}, u32[]{:S(2)}) collective-permute-start(bf16[8,24,512]{2,1,0:T(8,128)(2,1)S(1)} %arrive.3.refs_5_), channel_id=1, source_target_pairs={{0,4},{4,0},{8,12},{12,8},{16,20},{20,16},{24,28},{28,24},{1,5},{5... | collective-permute-start | bytes 589832 | tf_op jit(solution)/shard_map/ppermute | solution.py:20
  33.9 21.6 %collective-permute-start.12 = (bf16[48,24,128]{2,1,0:T(8,128)(2,1)S(1)}, bf16[48,24,128]{2,1,0:T(8,128)(2,1)S(1)}, u32[]{:S(2)}, u32[]{:S(2)}) collective-permute-start(bf16[48,24,128]{2,1,0:T(8,128)(2,1)S(1)} %get-tuple-element.44), channel_id=1, source_target_pairs={{0,4},{4,0},{8,12},{12,8},{16,20},{20,16},{24,28},{28,24},{1,5},{5... | collective-permute-start | bytes 884744 | tf_op jit(solution)/shard_map/ppermute | solution.py:20
  37.2 11.9 %collective-permute-start.13 = (bf16[8,24,1024]{2,1,0:T(8,128)(2,1)S(1)}, bf16[8,24,1024]{2,1,0:T(8,128)(2,1)S(1)}, u32[]{:S(2)}, u32[]{:S(2)}) collective-permute-start(bf16[8,24,1024]{2,1,0:T(8,128)(2,1)S(1)} %get-tuple-element.45), channel_id=1, source_target_pairs={{0,2},{1,3},{2,0},{3,1},{4,6},{5,7},{6,4},{7,5},{8,10},{9,11},{10,... | collective-permute-start | bytes 1179656 | tf_op jit(solution)/shard_map/ppermute | solution.py:36
  42.7 12.9 %collective-permute-start.11 = (bf16[8,24,1024]{2,1,0:T(8,128)(2,1)S(1)}, bf16[8,24,1024]{2,1,0:T(8,128)(2,1)S(1)}, u32[]{:S(2)}, u32[]{:S(2)}) collective-permute-start(bf16[8,24,1024]{2,1,0:T(8,128)(2,1)S(1)} %get-tuple-element.43), channel_id=1, source_target_pairs={{0,2},{1,3},{2,0},{3,1},{4,6},{5,7},{6,4},{7,5},{8,10},{9,11},{10,... | collective-permute-start | bytes 1179656 | tf_op jit(solution)/shard_map/ppermute | solution.py:36
  44.3 7.7 %collective-permute-start.15 = (bf16[8,24,512]{2,1,0:T(8,128)(2,1)S(1)}, bf16[8,24,512]{2,1,0:T(8,128)(2,1)S(1)}, u32[]{:S(2)}, u32[]{:S(2)}) collective-permute-start(bf16[8,24,512]{2,1,0:T(8,128)(2,1)S(1)} %get-tuple-element.48), channel_id=1, source_target_pairs={{0,4},{4,0},{8,12},{12,8},{16,20},{20,16},{24,28},{28,24},{1,5},{5... | collective-permute-start | bytes 589832 | tf_op jit(solution)/shard_map/ppermute | solution.py:20
  50.3 6.8 %collective-permute-start.14 = (bf16[48,24,128]{2,1,0:T(8,128)(2,1)S(1)}, bf16[48,24,128]{2,1,0:T(8,128)(2,1)S(1)}, u32[]{:S(2)}, u32[]{:S(2)}) collective-permute-start(bf16[48,24,128]{2,1,0:T(8,128)(2,1)S(1)} %get-tuple-element.47), channel_id=1, source_target_pairs={{0,4},{4,0},{8,12},{12,8},{16,20},{20,16},{24,28},{28,24},{1,5},{5... | collective-permute-start | bytes 884744 | tf_op jit(solution)/shard_map/ppermute | solution.py:20
  54.1 10.2 %collective-permute-start.20 = (bf16[8,24,1024]{2,1,0:T(8,128)(2,1)S(1)}, bf16[8,24,1024]{2,1,0:T(8,128)(2,1)S(1)}, u32[]{:S(2)}, u32[]{:S(2)}) collective-permute-start(bf16[8,24,1024]{2,1,0:T(8,128)(2,1)S(1)} %get-tuple-element.56), channel_id=1, source_target_pairs={{0,2},{1,3},{2,0},{3,1},{4,6},{5,7},{6,4},{7,5},{8,10},{9,11},{10,... | collective-permute-start | bytes 1179656 | tf_op jit(solution)/shard_map/ppermute | solution.py:36
  58.4 16.7 %collective-permute-start.16 = (bf16[12,2,24,128]{3,2,1,0:T(8,128)(2,1)S(1)}, bf16[12,2,24,128]{3,2,1,0:T(8,128)(2,1)S(1)}, u32[]{:S(2)}, u32[]{:S(2)}) collective-permute-start(bf16[12,2,24,128]{3,2,1,0:T(8,128)(2,1)S(1)} %get-tuple-element.51), channel_id=1, source_target_pairs={{0,8},{4,12},{8,0},{12,4},{16,24},{20,28},{24,16},{28,20},{1,9},{5... | collective-permute-start | bytes 442376 | tf_op jit(solution)/shard_map/ppermute | solution.py:20
  59.9 16.4 %collective-permute-start.17 = (bf16[12,2,24,128]{3,2,1,0:T(8,128)(2,1)S(1)}, bf16[12,2,24,128]{3,2,1,0:T(8,128)(2,1)S(1)}, u32[]{:S(2)}, u32[]{:S(2)}) collective-permute-start(bf16[12,2,24,128]{3,2,1,0:T(8,128)(2,1)S(1)} %get-tuple-element.52), channel_id=1, source_target_pairs={{0,16},{4,20},{8,24},{12,28},{16,0},{20,4},{24,8},{28,12},{1,17},{... | collective-permute-start | bytes 442376 | tf_op jit(solution)/shard_map/ppermute | solution.py:20
  62.5 14.5 %collective-permute-start.18 = (bf16[12,2,24,128]{3,2,1,0:T(8,128)(2,1)S(1)}, bf16[12,2,24,128]{3,2,1,0:T(8,128)(2,1)S(1)}, u32[]{:S(2)}, u32[]{:S(2)}) collective-permute-start(bf16[12,2,24,128]{3,2,1,0:T(8,128)(2,1)S(1)} %get-tuple-element.53), channel_id=1, source_target_pairs={{0,24},{4,28},{8,16},{12,20},{16,8},{20,12},{24,0},{28,4},{1,25},{... | collective-permute-start | bytes 442376 | tf_op jit(solution)/shard_map/ppermute | solution.py:20
  63.1 6.7 %collective-permute-start.19 = (bf16[48,24,128]{2,1,0:T(8,128)(2,1)S(1)}, bf16[48,24,128]{2,1,0:T(8,128)(2,1)S(1)}, u32[]{:S(2)}, u32[]{:S(2)}) collective-permute-start(bf16[48,24,128]{2,1,0:T(8,128)(2,1)S(1)} %get-tuple-element.55), channel_id=1, source_target_pairs={{0,4},{4,0},{8,12},{12,8},{16,20},{20,16},{24,28},{28,24},{1,5},{5... | collective-permute-start | bytes 884744 | tf_op jit(solution)/shard_map/ppermute | solution.py:20
  65.5 7.5 %collective-permute-start.24 = (bf16[48,24,128]{2,1,0:T(8,128)(2,1)S(1)}, bf16[48,24,128]{2,1,0:T(8,128)(2,1)S(1)}, u32[]{:S(2)}, u32[]{:S(2)}) collective-permute-start(bf16[48,24,128]{2,1,0:T(8,128)(2,1)S(1)} %get-tuple-element.62), channel_id=1, source_target_pairs={{0,4},{4,0},{8,12},{12,8},{16,20},{20,16},{24,28},{28,24},{1,5},{5... | collective-permute-start | bytes 884744 | tf_op jit(solution)/shard_map/ppermute | solution.py:20
  69.9 9.7 %collective-permute-start.21 = (bf16[12,1,24,128]{3,2,1,0:T(8,128)(2,1)S(1)}, bf16[12,1,24,128]{3,2,1,0:T(8,128)(2,1)S(1)}, u32[]{:S(2)}, u32[]{:S(2)}) collective-permute-start(bf16[12,1,24,128]{3,2,1,0:T(8,128)(2,1)S(1)} %get-tuple-element.59), channel_id=1, source_target_pairs={{0,8},{4,12},{8,0},{12,4},{16,24},{20,28},{24,16},{28,20},{1,9},{5... | collective-permute-start | bytes 221192 | tf_op jit(solution)/shard_map/ppermute | solution.py:20
  73.0 7.7 %collective-permute-start.22 = (bf16[12,1,24,128]{3,2,1,0:T(8,128)(2,1)S(1)}, bf16[12,1,24,128]{3,2,1,0:T(8,128)(2,1)S(1)}, u32[]{:S(2)}, u32[]{:S(2)}) collective-permute-start(bf16[12,1,24,128]{3,2,1,0:T(8,128)(2,1)S(1)} %get-tuple-element.60), channel_id=1, source_target_pairs={{0,16},{4,20},{8,24},{12,28},{16,0},{20,4},{24,8},{28,12},{1,17},{... | collective-permute-start | bytes 221192 | tf_op jit(solution)/shard_map/ppermute | solution.py:20
  75.1 6.4 %collective-permute-start.23 = (bf16[12,1,24,128]{3,2,1,0:T(8,128)(2,1)S(1)}, bf16[12,1,24,128]{3,2,1,0:T(8,128)(2,1)S(1)}, u32[]{:S(2)}, u32[]{:S(2)}) collective-permute-start(bf16[12,1,24,128]{3,2,1,0:T(8,128)(2,1)S(1)} %get-tuple-element.61), channel_id=1, source_target_pairs={{0,24},{4,28},{8,16},{12,20},{16,8},{20,12},{24,0},{28,4},{1,25},{... | collective-permute-start | bytes 221192 | tf_op jit(solution)/shard_map/ppermute | solution.py:20
  (6 other events, 31.4 us)

commit v3 on v2

v3 whole, which is shorter than its diff:
```python
import functools

import jax
import jax.numpy as jnp
from jax import lax
from jax.experimental import pallas as pl
from jax.experimental.pallas import tpu as pltpu
from jax.sharding import PartitionSpec as P

LANES = 128
SMEM = pl.BlockSpec(memory_space=pltpu.SMEM)
VMEM = pl.BlockSpec(memory_space=pltpu.VMEM)
ANY = pl.BlockSpec(memory_space=pl.ANY)
GRANT = 32 * 2**20
PACE = 0.3e9


def blk_swap(value, dz, dx, nz, nx):
    pairs = [(z * nx + x, (z ^ dz) * nx + (x ^ dx)) for z in range(nz) for x in range(nx)]
    return lax.ppermute(value, "blk", pairs)


def slab_swap(value, dx, dy, nz, nx, ny, nc):
    pairs = [
        (((z * nx + x) * ny + y) * nc + c, ((z * nx + (x ^ dx)) * ny + (y ^ dy)) * nc + c)
        for z in range(nz)
        for x in range(nx)
        for y in range(ny)
        for c in range(nc)
    ]
    return lax.ppermute(value, ("blk", "pair"), pairs)


def pair_swap(value, dy, dc, ny, nc):
    pairs = [(y * nc + c, (y ^ dy) * nc + (c ^ dc)) for y in range(ny) for c in range(nc)]
    return lax.ppermute(value, "pair", pairs)


def pick(position, options):
    value = options[0]
    for index in range(1, len(options)):
        value = jnp.where(position == index, options[index], value)
    return value


def bf16(*shape):
    return jax.ShapeDtypeStruct(shape, jnp.bfloat16)


class Step:
    def __init__(self, body, scalars, arrays, outs, scratch=(), far=()):
        self.body, self.scalars, self.arrays, self.far = body, list(scalars), list(arrays), list(far)
        self.outs, self.scratch = list(outs), list(scratch)


def launch(name, steps, after, due):
    scalars, arrays = [], []
    far = [value for step in steps for value in step.far]
    for step in steps:
        for value in step.scalars:
            if not any(value is other for other in scalars):
                scalars.append(value)
        for value in step.arrays:
            if not any(value is other for other in arrays):
                arrays.append(value)
    operands = scalars + arrays + far
    find = lambda value: next(i for i, other in enumerate(operands) if other is value)
    outs = [out for step in steps for out in step.outs]
    scratch = [s for step in steps for s in step.scratch]

    def kernel(*refs):
        out_refs = refs[len(operands) + len(after) :]
        scratch_refs = out_refs[len(outs) :]
        o = s = 0
        for step in steps:
            step.body(
                [refs[find(value)] for value in step.scalars],
                [refs[find(value)] for value in step.arrays + step.far],
                out_refs[o : o + len(step.outs)],
                scratch_refs[s : s + len(step.scratch)],
            )
            o, s = o + len(step.outs), s + len(step.scratch)

    results = pl.pallas_call(
        kernel,
        in_specs=[SMEM] * len(scalars) + [VMEM] * len(arrays) + [ANY] * (len(far) + len(after)),
        out_specs=[VMEM] * len(outs),
        out_shape=outs,
        scratch_shapes=scratch,
        cost_estimate=pl.CostEstimate(flops=int(PACE * due), bytes_accessed=0, transcendentals=0),
        compiler_params=pltpu.CompilerParams(vmem_limit_bytes=GRANT),
        name=name,
    )(*operands, *after)
    split, o = [], 0
    for step in steps:
        split.append(results[o : o + len(step.outs)])
        o += len(step.outs)
    return split


class Rows:
    def __init__(self, arrays, packed):
        self.arrays, self.packed = list(arrays), packed


def gather_rows(refs, index):
    return jnp.concatenate([ref[index] for ref in refs], axis=0) if len(refs) > 1 else refs[0][index]


def read_codes(ref, slots):
    row = ref[ref.shape[0] - 1][:1].astype(jnp.float32)
    lane = lax.broadcasted_iota(jnp.int32, row.shape, 1)
    return [jnp.sum(jnp.where(lane == k, row, 0.0)).astype(jnp.int32) for k in range(slots)]


def pack(codes, rows, slots):
    total = sum(value.shape[1] for value in rows.arrays)

    def body(_, refs, outs, __):
        for k, tile in enumerate(read_codes(refs[-1], slots)):
            outs[0][k] = gather_rows(refs[:-1], tile)

    return Step(body, [], [*rows.arrays, codes], [bf16(slots, total, rows.arrays[0].shape[2])])


def through(arrays):
    tiles, _, depth = arrays[0].shape

    def body(_, refs, outs, __):
        outs[0][...] = jnp.concatenate([ref[...] for ref in refs], axis=1) if len(refs) > 1 else refs[0][...]

    return Step(body, [], arrays, [bf16(tiles, sum(value.shape[1] for value in arrays), depth)])


def hold(value):
    def body(_, refs, outs, scratch):
        copy = pltpu.make_async_copy(refs[0], outs[0], scratch[0])
        copy.start()
        copy.wait()

    return Step(body, [], [], [bf16(*value.shape)], [pltpu.SemaphoreType.DMA(())], [value])


def products(codes, sources, blocks, ny, rows):
    nx, nc = len(sources), len(blocks)
    slots, depth, width = blocks[0].shape
    counts = [len(source.arrays) for source in sources]
    starts = [sum(counts[:d]) for d in range(nx + 1)]

    def body(_, refs, outs, __):
        block_refs = refs[starts[-1] : -1]
        x, c = lax.axis_index("blk") % nx, lax.axis_index("pair") % nc
        for k, tile in enumerate(read_codes(refs[-1], slots)):
            parts = [gather_rows(refs[starts[d] : starts[d + 1]], k if sources[d].packed else tile) for d in range(nx)]
            parts = [pick(x ^ i, parts) for i in range(nx)]
            columns = []
            for part in range(nc):
                pieces = [p[(s * nc + part) * rows : (s * nc + part + 1) * rows] for p in parts for s in range(ny)]
                columns.append(jnp.concatenate(pieces, axis=0))
            total = None
            for d in range(nc):
                term = jnp.dot(pick(c ^ d, columns), block_refs[d][k], preferred_element_type=jnp.float32)
                total = term if total is None else total + term
            for s in range(ny):
                pieces = [total[(i * ny + s) * rows : (i * ny + s + 1) * rows] for i in range(nx)]
                outs[s][k] = jnp.concatenate(pieces, axis=0).astype(outs[s].dtype)

    arrays = [value for source in sources for value in source.arrays] + [*blocks, codes]
    return Step(body, [], arrays, [bf16(slots, nx * rows, width)] * ny)


def route(tiles, keep, slot_tile, parts, tile_count, nx, nz):
    slots, rows, width = parts[0].shape
    owned = slot_tile.shape[0] // (nx * nz)
    per_tile = width // LANES

    def body(scalars, refs, outs, scratch):
        tiles_ref, keep_ref, slot_ref = scalars
        total = scratch[0]
        z, x = lax.axis_index("blk") // nx, lax.axis_index("blk") % nx
        total[...] = jnp.zeros_like(total)

        def add(k, _):
            value = refs[0][k].astype(jnp.float32)
            for ref in refs[1:]:
                value += ref[k].astype(jnp.float32)
            total[tiles_ref[1, k]] += value * keep_ref[k].astype(jnp.float32)
            return 0

        lax.fori_loop(0, slots, add, 0)
        for d in range(nx):
            for dz in range(nz):
                owner = (z ^ dz) * nx + (x ^ d)
                for i in range(owned):
                    tile = slot_ref[owner * owned + i]
                    a = lax.div(tile, per_tile)
                    column = pl.multiple_of(lax.rem(tile, per_tile) * LANES, LANES)
                    outs[d][dz * owned + i] = total[a, :, pl.ds(column, LANES)].astype(outs[d].dtype)

    scratch = [pltpu.VMEM((tile_count, rows, width), jnp.float32)]
    return Step(body, [tiles, keep, slot_tile], parts, [bf16(nz * owned, rows, LANES)] * nx, scratch)


def add_split(chunks, nz):
    tiles, rows, lanes = chunks[0][0].shape
    count, each = tiles // nz, len(chunks[0])

    def body(_, refs, outs, __):
        for i in range(len(chunks)):
            for e, out in enumerate(outs):
                span = slice(e * count, (e + 1) * count)
                value = refs[i * each][span].astype(jnp.float32)
                for part in refs[i * each + 1 : (i + 1) * each]:
                    value += part[span].astype(jnp.float32)
                out[:, i] = value.astype(out.dtype)

    flat = [part for chunk in chunks for part in chunk]
    return Step(body, [], flat, [bf16(count, len(chunks), rows, lanes)] * nz)


def fold(chunks, nz):
    tiles, rows, lanes = chunks[0][0].shape
    count, each = tiles // nz, len(chunks[0])

    def body(_, refs, outs, __):
        for i in range(len(chunks)):
            for e in range(nz):
                span = slice(e * count, (e + 1) * count)
                value = refs[i * each][span].astype(jnp.float32)
                for part in refs[i * each + 1 : (i + 1) * each]:
                    value += part[span].astype(jnp.float32)
                at = slice(e // 2 * count, (e // 2 + 1) * count)
                outs[e % 2][at, i ^ e % 2] = value.astype(outs[e % 2].dtype)

    flat = [part for chunk in chunks for part in chunk]
    return Step(body, [], flat, [bf16(nz // 2 * count, len(chunks), rows, lanes)] * 2)


def final_sum(received, nz, nx):
    owned, _, rows, lanes = received[0][0].shape

    def body(scalars, refs, outs, _):
        z = lax.axis_index("blk") // nx
        for ahead in range(nz):
            value = None
            for ref, (_, columns) in zip(refs, received, strict=True):
                if ahead in columns:
                    term = ref[:, columns.index(ahead)].astype(jnp.float32)
                    value = term if value is None else value + term
            outs[0][:, z ^ ahead] = value.astype(outs[0].dtype)

    return Step(body, [], [value for value, _ in received], [bf16(owned, nz, rows, lanes)])


def per_device(nz, nx, ny, nc, amplitudes, tile_mask, integrals, block_tiles, block_keep, slot_tile):
    pair = lax.axis_index("pair")
    y = pair // nc
    _, rows, tile_count, contracted = amplitudes.shape
    slots = block_keep.shape[0]
    columns = contracted // ny

    siblings = [pair_swap(integrals, 0, d, ny, nc) for d in range(1, nc)]
    blocks = [integrals]
    tiles = block_tiles.T

    masked = jnp.where(tile_mask[0][:, :, None] != 0, amplitudes[0], jnp.zeros((), amplitudes.dtype))
    masked = masked.transpose(1, 0, 2)
    depth = columns // nc
    pieces = []
    for d in range(ny):
        begin = (y ^ d) * columns
        pieces.append(
            jnp.concatenate([lax.dynamic_slice_in_dim(masked, begin + i * depth, depth, axis=2) for i in range(nc)], axis=1)
        )

    here, others, partial, by_owner, folded, received = {}, {}, {}, {}, {}, []
    last = []

    def run(name, due, *steps):
        nonlocal last
        results = launch(name, [step for step, _ in steps], last, due)
        last = list(results[0][:1])
        for (_, use), result in zip(steps, results, strict=True):
            use(result)

    def low_bits():
        return [d for d in range(1, nz) if d & -d == d]

    def do_first(s):
        def use(out):
            for d in range(1, nx):
                others[0][d - 1].append(blk_swap(out[0], 0, d, nz, nx))

        return through([from_y[s]]), use

    def do_along():
        def use(out):
            for d in low_bits():
                here[d] = [blk_swap(out[0], d, 0, nz, nx)]

        return through(from_y), use

    def do_hold(i):
        return hold(siblings[i]), lambda out: blocks.append(out[0])

    def do_pack(d, i):
        def use(out):
            if i:
                others[d][i] = blk_swap(out[0], 0, i, nz, nx)
            else:
                own[d] = out[0]

        others.setdefault(d, {})
        if i:
            return pack(their_codes[i - 1], Rows(here[d], False), slots), use
        return pack(first, Rows(here[d], False), slots), use

    def do_forward(d):
        def use(out):
            for step in range(1, d & -d):
                if step & -step == step:
                    here[d | step] = [blk_swap(out[0], step, 0, nz, nx)]

        return through(here[d]), use

    def do_products(d):
        def use(out):
            partial[d] = [out[0]] + [pair_swap(out[i], i, 0, ny, nc) for i in range(1, ny)]

        if d:
            sources = [Rows([own[d]], True) if d in own else Rows(here[d], False)]
            sources += [Rows([others[d][i]], True) for i in range(1, nx)]
        else:
            sources = [Rows(from_y, False)] + [Rows(other, False) for other in others[0]]
        return products(first, sources, blocks, ny, rows), use

    def do_route(d):
        def use(out):
            by_owner[d] = [out[0]] + [blk_swap(out[i], 0, i, nz, nx) for i in range(1, nx)]

        return route(tiles, block_keep, slot_tile, partial[d], tile_count, nx, nz), use

    def do_add(group):
        def use(out):
            for e in range(nz):
                received.append((blk_swap(out[e], e, 0, nz, nx) if e else out[0], [e ^ d for d in group]))

        return add_split([by_owner[d] for d in group], nz), use

    def do_fold(group):
        def use(out):
            folded[group] = [out[0], blk_swap(out[1], 1, 0, nz, nx)]

        return fold([by_owner[d] for d in group], nz), use

    def do_pass(group):
        def use(out):
            for e in range(0, nz, 2):
                received.append((blk_swap(out[e // 2], e, 0, nz, nx) if e else out[0], [e ^ d for d in group]))

        chunks = [[value.reshape(value.shape[0], -1, LANES) for value in folded[group]]]
        step = add_split(chunks, nz // 2)
        return step, lambda out: use([value.reshape(value.shape[0], len(group), -1, LANES) for value in out])

    from_y = [pieces[0]] + [pair_swap(pieces[d], d, 0, ny, nc) for d in range(1, ny)]
    codes = jnp.pad(tiles[:1].astype(jnp.bfloat16), ((0, nc * rows - 1), (0, depth - slots)))
    first = jnp.concatenate([pieces[0], codes[None]], axis=0)
    others[0] = [[blk_swap(first, 0, dx, nz, nx)] for dx in range(1, nx)]
    their_codes = [other[0] for other in others[0]]
    own = {}
    if nc > 1:
        run("hold", 8, *[do_hold(i) for i in range(nc - 1)])
    run("first", 20, *[do_first(s) for s in range(1, ny)], do_along())
    for due, slot in plan(nz):
        steps = []
        last = last + [value for what, g in slot if what == "sent" for value, _ in received[g * nz : (g + 1) * nz]]
        last = last + [value for what, d in slot if what == "came" for value in here[d]]
        last = last + [value for what, d in slot if what == "got" for value in partial[d][1:]]
        for what, d in slot:
            if what == "arrive":
                steps += [do_pack(d, i) for i in range(1, nx)] + ([do_pack(d, 0)] if len(here[d]) > 1 else [])
            elif what == "forward":
                steps.append(do_forward(d))
            elif what not in ("sent", "came", "got"):
                steps.append({"multiply": do_products, "route": do_route, "add": do_add, "fold": do_fold, "pass": do_pass}[what](d))
        run("_".join(what for what, _ in slot), due, *steps)
    out = launch("final_sum", [final_sum(received, nz, nx)], last, 2)[0][0]
    return out.reshape(out.shape[0], 1, out.shape[1] * out.shape[2], LANES)


def plan(nz):
    m, r, a, f, s = "multiply", "route", "arrive", "forward", "add"
    if nz == 4:
        return [
            (2, [(m, 0)]),
            (4, [(a, 1)]),
            (6, [(f, 2)]),
            (20, [(r, 0)]),
            (20, [(a, 2)]),
            (20, [(m, 1)]),
            (20, [(m, 2), (a, 3)]),
            (20, [(s, (0,))]),
            (20, [(r, 1)]),
            (20, [(m, 3), ("sent", 0)]),
            (20, [(r, 2)]),
            (20, [(s, (1,))]),
            (20, [(r, 3)]),
            (20, [(s, (2,))]),
            (20, [(s, (3,)), ("sent", 1)]),
        ]
    slots = [[(m, 0)]]
    for d in range(1, nz):
        slots.append([(a, d)] + ([(f, d)] if d & -d > 1 else []))
        slots.append([(m, d), (r, d - 1)])
    slots += [[(r, nz - 1)]] + [[(s, (d,))] for d in range(nz)]
    return [(5.0, slot) for slot in slots]


def solution(mesh):
    holders, pairs = mesh.shape["blk"], mesh.shape["pair"]
    nx = 1
    while (2 * nx) ** 2 <= holders:
        nx *= 2
    nc = 2 if pairs % 2 == 0 else 1
    placed = (
        P("pair", "blk", None, None),
        P("pair", "blk", None),
        P("blk", "pair", None),
        P("blk", None),
        P("blk"),
        P(),
    )
    return jax.shard_map(
        functools.partial(per_device, holders // nx, nx, pairs // nc, nc),
        mesh=mesh,
        in_specs=placed,
        out_specs=P("blk", "pair", None, None),
        check_vma=False,
    )
```

time: 87.4 us -> 84.2 us (0.963)
  starting transfers between devices: 37.8 us -> 42.7 us
  waiting for transfers between devices: 27.4 us -> 22.8 us
  Pallas kernels: 18.3 us -> 15.4 us
  local copies, waits for them, and re-layouts: 1.63 us -> 0.21 us
    ppermute x6, waiting for transfers between devices: 5.89 us -> 0.09 us  [pair_swap(): return lax.ppermute(value, 'pair', pairs)]
    ppermute x22 -> x24, starting transfers between devices: 29.7 us -> 33.1 us  [blk_swap(): return lax.ppermute(value, 'blk', pairs)]
    pallas_call x1 -> x0, Pallas kernels: 2.2 us -> none  [hold(): pl.pallas_call(kernel, in_specs=[ANY] * (len(values) + len(after)), out_s...]
    ppermute x6, starting transfers between devices: 8.12 us -> 9.53 us  [pair_swap(): return lax.ppermute(value, 'pair', pairs)]
    ppermute x22 -> x24, waiting for transfers between devices: 21.5 us -> 22.7 us  [blk_swap(): return lax.ppermute(value, 'blk', pairs)]
    select_n x0 -> x1, other arithmetic: none -> 1.19 us  [per_device(): jnp.where(tile_mask[0][:, :, None] != 0, amplitudes[0], jnp.zeros((), amp...]
    mul x1 -> x0, other arithmetic: 1.19 us -> none  [per_device(): masked = amplitudes[0] * tile_mask[0].astype(jnp.bfloat16)[:, :, None]]
    pallas_call x16 -> x18, Pallas kernels: 16.1 us -> 15.4 us  [launch(): pl.pallas_call(kernel, in_specs=[SMEM] * len(scalars) + [VMEM] * len(arra...]
  transfers between devices with their start and end apart: 28 -> 30, of which waited for: 15 -> 11; matrix products, arithmetic and copies ran while one was open for 4% -> 3% of each run, Pallas kernels for 19% -> 17%
where the time goes in v3:
time: 84.2 us; the launch traced here: 84 us
  starting transfers between devices  42.7 us (51%)
  waiting for transfers between devices  22.8 us (27%)
  Pallas kernels  15.4 us (18%)
  other arithmetic  2.7 us (3%)
    ppermute x24, starting transfers between devices, blk_swap(): return lax.ppermute(value, 'blk', pairs)  33.1 us
    ppermute x24, waiting for transfers between devices, blk_swap(): return lax.ppermute(value, 'blk', pairs)  22.7 us
    pallas_call x18, Pallas kernels, launch(): pl.pallas_call(kernel, in_specs=[SMEM] * len(scalars) + [VMEM] * len(arra...  15.4 us
    ppermute x6, starting transfers between devices, pair_swap(): return lax.ppermute(value, 'pair', pairs)  9.53 us
  transfers between devices with their start and end apart: 30, of which 11 were waited for; matrix products, arithmetic and copies ran while one was open for 3% of the time, Pallas kernels for 17%

profile of v3, /device:TPU:0, one launch (start us, length us, event | category | flops | bytes accessed | tf_op | source)
XLA Modules:
  0.0 84.0 jit_solution(10962119625590757082)
XLA Ops:
  2.6 2.6 %collective-permute-start = (bf16[12,24,256]{2,1,0:T(8,128)(2,1)S(1)}, bf16[12,24,256]{2,1,0:T(8,128)(2,1)S(1)}, u32[]{:S(2)}, u32[]{:S(2)}) collective-permute-start(bf16[12,24,256]{2,1,0:T(8,128)(2,1)S(1)} %pad_maximum_fusion.2), channel_id=1, source_target_pairs={{0,2},{1,3},{2,0},{3,1},{4,6},{5,7},{6,4},{7,5},{8,10},{9,11},{10,... | collective-permute-start | bytes 442376 | tf_op jit(solution)/shard_map/ppermute | solution.py:36
  7.6 2.2 %hold.1.refs_2_.refs_5_.refs_3_ = bf16[8,256,1024]{2,1,0:T(8,128)(2,1)S(1)} custom-call(bf16[8,256,1024]{2,1,0:T(8,128)(2,1)} %collective-permute-done.2.refs_0_), custom_call_target="tpu_custom_call" | custom-call | flops 2400000000 | tf_op jit(solution)/shard_map/hold/pallas_call | solution.py:84
  9.8 2.9 %collective-permute-start.3 = (bf16[12,24,256]{2,1,0:T(8,128)(2,1)S(1)}, bf16[12,24,256]{2,1,0:T(8,128)(2,1)S(1)}, u32[]{:S(2)}, u32[]{:S(2)}) collective-permute-start(bf16[12,24,256]{2,1,0:T(8,128)(2,1)S(1)} %get-tuple-element.40.refs_7_), channel_id=1, source_target_pairs={{0,4},{4,0},{8,12},{12,8},{16,20},{20,16},{24,28},{28,24},{1,5},{5... | collective-permute-start | bytes 442376 | tf_op jit(solution)/shard_map/ppermute | solution.py:20
  14.3 2.6 %collective-permute-start.5 = (bf16[12,48,256]{2,1,0:T(8,128)(2,1)S(1)}, bf16[12,48,256]{2,1,0:T(8,128)(2,1)S(1)}, u32[]{:S(2)}, u32[]{:S(2)}) collective-permute-start(bf16[12,48,256]{2,1,0:T(8,128)(2,1)S(1)} %get-tuple-element.43), channel_id=1, source_target_pairs={{0,16},{4,20},{8,24},{12,28},{16,0},{20,4},{24,8},{28,12},{1,17},{... | collective-permute-start | bytes 884744 | tf_op jit(solution)/shard_map/ppermute | solution.py:20
  17.0 1.7 %multiply.2 = (bf16[8,24,1024]{2,1,0:T(8,128)(2,1)S(1)}, bf16[8,24,1024]{2,1,0:T(8,128)(2,1)S(1)}) custom-call(bf16[12,24,256]{2,1,0:T(8,128)(2,1)S(1)} %pad_maximum_fusion.1.refs_1_.refs_0_, bf16[12,24,256]{2,1,0:T(8,128)(2,1)S(1)} %collective-permute-done.refs_0_.refs_1_, bf16[13,24,256]{2,1,0:T(8,128)(2,1)S(1)} %collective-permute-done.1.refs_2_.refs_1_.refs_6_, ...), custom_call_target="tpu_custom_call" | custom-call | flops 600000000 | tf_op jit(solution)/shard_map/multiply/pallas_call | solution.py:84
  18.6 1.8 %collective-permute-start.4 = (bf16[8,24,1024]{2,1,0:T(8,128)(2,1)S(1)}, bf16[8,24,1024]{2,1,0:T(8,128)(2,1)S(1)}, u32[]{:S(2)}, u32[]{:S(2)}) collective-permute-start(bf16[8,24,1024]{2,1,0:T(8,128)(2,1)S(1)} %get-tuple-element.42), channel_id=1, source_target_pairs={{0,2},{1,3},{2,0},{3,1},{4,6},{5,7},{6,4},{7,5},{8,10},{9,11},{10,... | collective-permute-start | bytes 1179656 | tf_op jit(solution)/shard_map/ppermute | solution.py:36
  20.4 7.3 %collective-permute-done.6.refs_0_ = bf16[12,48,256]{2,1,0:T(8,128)(2,1)S(1)} collective-permute-done((bf16[12,48,256]{2,1,0:T(8,128)(2,1)S(1)}, bf16[12,48,256]{2,1,0:T(8,128)(2,1)S(1)}, u32[]{:S(2)}, u32[]{:S(2)}) %collective-permute-start.6) | collective-permute-done | bytes 294944 | tf_op jit(solution)/shard_map/ppermute | solution.py:20
  28.4 1.7 %collective-permute-done.5.refs_0_ = bf16[12,48,256]{2,1,0:T(8,128)(2,1)S(1)} collective-permute-done((bf16[12,48,256]{2,1,0:T(8,128)(2,1)S(1)}, bf16[12,48,256]{2,1,0:T(8,128)(2,1)S(1)}, u32[]{:S(2)}, u32[]{:S(2)}) %collective-permute-start.5) | collective-permute-done | bytes 294944 | tf_op jit(solution)/shard_map/ppermute | solution.py:20
  34.2 1.7 %multiply.3 = (bf16[8,24,1024]{2,1,0:T(8,128)(2,1)S(1)}, bf16[8,24,1024]{2,1,0:T(8,128)(2,1)S(1)}) custom-call(bf16[12,48,256]{2,1,0:T(8,128)(2,1)S(1)} %collective-permute-done.6.refs_0_, bf16[8,48,256]{2,1,0:T(8,128)(2,1)S(1)} %collective-permute-done.10.refs_1_, bf16[8,256,1024]{2,1,0:T(8,128)(2,1)S(1)} %copy-done, ...), custom_call_target="tpu_custom_call" | custom-call | flops 6000000000 | tf_op jit(solution)/shard_map/multiply/pallas_call | solution.py:84
  37.4 2.5 %collective-permute-done.8.refs_1_ = bf16[8,48,256]{2,1,0:T(8,128)(2,1)S(1)} collective-permute-done((bf16[8,48,256]{2,1,0:T(8,128)(2,1)S(1)}, bf16[8,48,256]{2,1,0:T(8,128)(2,1)S(1)}, u32[]{:S(2)}, u32[]{:S(2)}) %collective-permute-start.8) | collective-permute-done | bytes 196640 | tf_op jit(solution)/shard_map/ppermute | solution.py:20
  40.0 1.7 %multiply_arrive.1 = (bf16[8,24,1024]{2,1,0:T(8,128)(2,1)S(1)}, bf16[8,24,1024]{2,1,0:T(8,128)(2,1)S(1)}, bf16[8,48,256]{2,1,0:T(8,128)(2,1)S(1)}) custom-call(bf16[12,48,256]{2,1,0:T(8,128)(2,1)S(1)} %collective-permute-done.5.refs_0_, bf16[8,48,256]{2,1,0:T(8,128)(2,1)S(1)} %collective-permute-done.8.refs_1_, bf16[8,256,1024]{2,1,0:T(8,128)(2,1)S(1)} %copy-done, ...), custom_call_target="tpu_custom_call" | custom-call | flops 6000000000 | tf_op jit(solution)/shard_map/multiply_arrive/pallas_call | solution.py:84
  43.8 2.5 %collective-permute-done.7.refs_1_ = bf16[48,24,128]{2,1,0:T(8,128)(2,1)S(1)} collective-permute-done((bf16[48,24,128]{2,1,0:T(8,128)(2,1)S(1)}, bf16[48,24,128]{2,1,0:T(8,128)(2,1)S(1)}, u32[]{:S(2)}, u32[]{:S(2)}) %collective-permute-start.7) | collective-permute-done | bytes 294944 | tf_op jit(solution)/shard_map/ppermute | solution.py:20
  46.5 2.7 %collective-permute-start.12 = (bf16[12,1,24,128]{3,2,1,0:T(8,128)(2,1)S(1)}, bf16[12,1,24,128]{3,2,1,0:T(8,128)(2,1)S(1)}, u32[]{:S(2)}, u32[]{:S(2)}) collective-permute-start(bf16[12,1,24,128]{3,2,1,0:T(8,128)(2,1)S(1)} %get-tuple-element.50), channel_id=1, source_target_pairs={{0,16},{4,20},{8,24},{12,28},{16,0},{20,4},{24,8},{28,12},{1,17},{... | collective-permute-start | bytes 221192 | tf_op jit(solution)/shard_map/ppermute | solution.py:20
  49.2 1.7 %collective-permute-start.13 = (bf16[12,1,24,128]{3,2,1,0:T(8,128)(2,1)S(1)}, bf16[12,1,24,128]{3,2,1,0:T(8,128)(2,1)S(1)}, u32[]{:S(2)}, u32[]{:S(2)}) collective-permute-start(bf16[12,1,24,128]{3,2,1,0:T(8,128)(2,1)S(1)} %get-tuple-element.51), channel_id=1, source_target_pairs={{0,24},{4,28},{8,16},{12,20},{16,8},{20,12},{24,0},{28,4},{1,25},{... | collective-permute-start | bytes 221192 | tf_op jit(solution)/shard_map/ppermute | solution.py:20
  53.0 2.4 %collective-permute-done.13.refs_9_.refs_3_ = bf16[12,1,24,128]{3,2,1,0:T(8,128)(2,1)S(1)} collective-permute-done((bf16[12,1,24,128]{3,2,1,0:T(8,128)(2,1)S(1)}, bf16[12,1,24,128]{3,2,1,0:T(8,128)(2,1)S(1)}, u32[]{:S(2)}, u32[]{:S(2)}) %collective-permute-start.13) | collective-permute-done | bytes 73760 | tf_op jit(solution)/shard_map/ppermute | solution.py:20
  55.4 1.7 %multiply_sent.1 = (bf16[8,24,1024]{2,1,0:T(8,128)(2,1)S(1)}, bf16[8,24,1024]{2,1,0:T(8,128)(2,1)S(1)}) custom-call(bf16[12,48,256]{2,1,0:T(8,128)(2,1)S(1)} %collective-permute-done.9.refs_5_.refs_0_, bf16[8,48,256]{2,1,0:T(8,128)(2,1)S(1)} %collective-permute-done.17.refs_1_, bf16[8,256,1024]{2,1,0:T(8,128)(2,1)S(1)} %copy-done, ...), custom_call_target="tpu_custom_call" | custom-call | flops 6000000000 | tf_op jit(solution)/shard_map/multiply_sent/pallas_call | solution.py:84
  61.9 2.5 %collective-permute-start.19 = (bf16[12,1,24,128]{3,2,1,0:T(8,128)(2,1)S(1)}, bf16[12,1,24,128]{3,2,1,0:T(8,128)(2,1)S(1)}, u32[]{:S(2)}, u32[]{:S(2)}) collective-permute-start(bf16[12,1,24,128]{3,2,1,0:T(8,128)(2,1)S(1)} %get-tuple-element.61), channel_id=1, source_target_pairs={{0,16},{4,20},{8,24},{12,28},{16,0},{20,4},{24,8},{28,12},{1,17},{... | collective-permute-start | bytes 221192 | tf_op jit(solution)/shard_map/ppermute | solution.py:20
  67.8 2.0 %collective-permute-done.21.refs_1_ = bf16[48,24,128]{2,1,0:T(8,128)(2,1)S(1)} collective-permute-done((bf16[48,24,128]{2,1,0:T(8,128)(2,1)S(1)}, bf16[48,24,128]{2,1,0:T(8,128)(2,1)S(1)}, u32[]{:S(2)}, u32[]{:S(2)}) %collective-permute-start.21) | collective-permute-done | bytes 294944 | tf_op jit(solution)/shard_map/ppermute | solution.py:20
  70.0 1.7 %collective-permute-start.24 = (bf16[12,1,24,128]{3,2,1,0:T(8,128)(2,1)S(1)}, bf16[12,1,24,128]{3,2,1,0:T(8,128)(2,1)S(1)}, u32[]{:S(2)}, u32[]{:S(2)}) collective-permute-start(bf16[12,1,24,128]{3,2,1,0:T(8,128)(2,1)S(1)} %get-tuple-element.68), channel_id=1, source_target_pairs={{0,16},{4,20},{8,24},{12,28},{16,0},{20,4},{24,8},{28,12},{1,17},{... | collective-permute-start | bytes 221192 | tf_op jit(solution)/shard_map/ppermute | solution.py:20
  71.7 2.6 %collective-permute-start.25 = (bf16[12,1,24,128]{3,2,1,0:T(8,128)(2,1)S(1)}, bf16[12,1,24,128]{3,2,1,0:T(8,128)(2,1)S(1)}, u32[]{:S(2)}, u32[]{:S(2)}) collective-permute-start(bf16[12,1,24,128]{3,2,1,0:T(8,128)(2,1)S(1)} %get-tuple-element.69), channel_id=1, source_target_pairs={{0,24},{4,28},{8,16},{12,20},{16,8},{20,12},{24,0},{28,4},{1,25},{... | collective-permute-start | bytes 221192 | tf_op jit(solution)/shard_map/ppermute | solution.py:20
  74.5 2.5 %collective-permute-start.28 = (bf16[12,1,24,128]{3,2,1,0:T(8,128)(2,1)S(1)}, bf16[12,1,24,128]{3,2,1,0:T(8,128)(2,1)S(1)}, u32[]{:S(2)}, u32[]{:S(2)}) collective-permute-start(bf16[12,1,24,128]{3,2,1,0:T(8,128)(2,1)S(1)} %get-tuple-element.73), channel_id=1, source_target_pairs={{0,16},{4,20},{8,24},{12,28},{16,0},{20,4},{24,8},{28,12},{1,17},{... | collective-permute-start | bytes 221192 | tf_op jit(solution)/shard_map/ppermute | solution.py:20
  77.0 1.9 %collective-permute-start.29 = (bf16[12,1,24,128]{3,2,1,0:T(8,128)(2,1)S(1)}, bf16[12,1,24,128]{3,2,1,0:T(8,128)(2,1)S(1)}, u32[]{:S(2)}, u32[]{:S(2)}) collective-permute-start(bf16[12,1,24,128]{3,2,1,0:T(8,128)(2,1)S(1)} %get-tuple-element.74), channel_id=1, source_target_pairs={{0,24},{4,28},{8,16},{12,20},{16,8},{20,12},{24,0},{28,4},{1,25},{... | collective-permute-start | bytes 221192 | tf_op jit(solution)/shard_map/ppermute | solution.py:20
  79.4 2.1 %collective-permute-done.28.refs_14_ = bf16[12,1,24,128]{3,2,1,0:T(8,128)(2,1)S(1)} collective-permute-done((bf16[12,1,24,128]{3,2,1,0:T(8,128)(2,1)S(1)}, bf16[12,1,24,128]{3,2,1,0:T(8,128)(2,1)S(1)}, u32[]{:S(2)}, u32[]{:S(2)}) %collective-permute-start.28) | collective-permute-done | bytes 73760 | tf_op jit(solution)/shard_map/ppermute | solution.py:20
  81.5 1.7 %collective-permute-done.29.refs_15_ = bf16[12,1,24,128]{3,2,1,0:T(8,128)(2,1)S(1)} collective-permute-done((bf16[12,1,24,128]{3,2,1,0:T(8,128)(2,1)S(1)}, bf16[12,1,24,128]{3,2,1,0:T(8,128)(2,1)S(1)}, u32[]{:S(2)}, u32[]{:S(2)}) %collective-permute-start.29) | collective-permute-done | bytes 73760 | tf_op jit(solution)/shard_map/ppermute | solution.py:20
  (71 shorter events, 27.1 us)
Async XLA Ops:
  0.0 7.6 %collective-permute-start.2 = (bf16[8,256,1024]{2,1,0:T(8,128)(2,1)}, bf16[8,256,1024]{2,1,0:T(8,128)(2,1)}, u32[]{:S(2)}, u32[]{:S(2)}) collective-permute-start(bf16[8,256,1024]{2,1,0:T(8,128)(2,1)} %refs_2_.11), channel_id=1, source_target_pairs={{0,1},{1,0},{2,3},{3,2},{4,5},{5,4},{6,7},{7,6},{8,9},{9,8},{10,11... | collective-permute-start | bytes 12582920 | tf_op jit(solution)/shard_map/ppermute | solution.py:36
  2.6 7.2 %collective-permute-start = (bf16[12,24,256]{2,1,0:T(8,128)(2,1)S(1)}, bf16[12,24,256]{2,1,0:T(8,128)(2,1)S(1)}, u32[]{:S(2)}, u32[]{:S(2)}) collective-permute-start(bf16[12,24,256]{2,1,0:T(8,128)(2,1)S(1)} %pad_maximum_fusion.2), channel_id=1, source_target_pairs={{0,2},{1,3},{2,0},{3,1},{4,6},{5,7},{6,4},{7,5},{8,10},{9,11},{10,... | collective-permute-start | bytes 442376 | tf_op jit(solution)/shard_map/ppermute | solution.py:36
  5.9 11.0 %collective-permute-start.1 = (bf16[13,24,256]{2,1,0:T(8,128)(2,1)S(1)}, bf16[13,24,256]{2,1,0:T(8,128)(2,1)S(1)}, u32[]{:S(2)}, u32[]{:S(2)}) collective-permute-start(bf16[13,24,256]{2,1,0:T(8,128)(2,1)S(1)} %pad_maximum_fusion.refs_6_.refs_4_), channel_id=1, source_target_pairs={{0,4},{4,0},{8,12},{12,8},{16,20},{20,16},{24,28},{28,24},{1,5},{5... | collective-permute-start | bytes 479240 | tf_op jit(solution)/shard_map/ppermute | solution.py:20
  9.8 7.1 %collective-permute-start.3 = (bf16[12,24,256]{2,1,0:T(8,128)(2,1)S(1)}, bf16[12,24,256]{2,1,0:T(8,128)(2,1)S(1)}, u32[]{:S(2)}, u32[]{:S(2)}) collective-permute-start(bf16[12,24,256]{2,1,0:T(8,128)(2,1)S(1)} %get-tuple-element.40.refs_7_), channel_id=1, source_target_pairs={{0,4},{4,0},{8,12},{12,8},{16,20},{20,16},{24,28},{28,24},{1,5},{5... | collective-permute-start | bytes 442376 | tf_op jit(solution)/shard_map/ppermute | solution.py:20
  12.8 15.0 %collective-permute-start.6 = (bf16[12,48,256]{2,1,0:T(8,128)(2,1)S(1)}, bf16[12,48,256]{2,1,0:T(8,128)(2,1)S(1)}, u32[]{:S(2)}, u32[]{:S(2)}) collective-permute-start(bf16[12,48,256]{2,1,0:T(8,128)(2,1)S(1)} %get-tuple-element.43), channel_id=1, source_target_pairs={{0,8},{4,12},{8,0},{12,4},{16,24},{20,28},{24,16},{28,20},{1,9},{5... | collective-permute-start | bytes 884744 | tf_op jit(solution)/shard_map/ppermute | solution.py:20
  14.3 15.8 %collective-permute-start.5 = (bf16[12,48,256]{2,1,0:T(8,128)(2,1)S(1)}, bf16[12,48,256]{2,1,0:T(8,128)(2,1)S(1)}, u32[]{:S(2)}, u32[]{:S(2)}) collective-permute-start(bf16[12,48,256]{2,1,0:T(8,128)(2,1)S(1)} %get-tuple-element.43), channel_id=1, source_target_pairs={{0,16},{4,20},{8,24},{12,28},{16,0},{20,4},{24,8},{28,12},{1,17},{... | collective-permute-start | bytes 884744 | tf_op jit(solution)/shard_map/ppermute | solution.py:20
  18.6 12.0 %collective-permute-start.4 = (bf16[8,24,1024]{2,1,0:T(8,128)(2,1)S(1)}, bf16[8,24,1024]{2,1,0:T(8,128)(2,1)S(1)}, u32[]{:S(2)}, u32[]{:S(2)}) collective-permute-start(bf16[8,24,1024]{2,1,0:T(8,128)(2,1)S(1)} %get-tuple-element.42), channel_id=1, source_target_pairs={{0,2},{1,3},{2,0},{3,1},{4,6},{5,7},{6,4},{7,5},{8,10},{9,11},{10,... | collective-permute-start | bytes 1179656 | tf_op jit(solution)/shard_map/ppermute | solution.py:36
  30.1 7.3 %collective-permute-start.9 = (bf16[12,48,256]{2,1,0:T(8,128)(2,1)S(1)}, bf16[12,48,256]{2,1,0:T(8,128)(2,1)S(1)}, u32[]{:S(2)}, u32[]{:S(2)}) collective-permute-start(bf16[12,48,256]{2,1,0:T(8,128)(2,1)S(1)} %forward.1.refs_5_), channel_id=1, source_target_pairs={{0,8},{4,12},{8,0},{12,4},{16,24},{20,28},{24,16},{28,20},{1,9},{5... | collective-permute-start | bytes 884744 | tf_op jit(solution)/shard_map/ppermute | solution.py:20
  32.1 7.9 %collective-permute-start.8 = (bf16[8,48,256]{2,1,0:T(8,128)(2,1)S(1)}, bf16[8,48,256]{2,1,0:T(8,128)(2,1)S(1)}, u32[]{:S(2)}, u32[]{:S(2)}) collective-permute-start(bf16[8,48,256]{2,1,0:T(8,128)(2,1)S(1)} %arrive.3.refs_5_), channel_id=1, source_target_pairs={{0,4},{4,0},{8,12},{12,8},{16,20},{20,16},{24,28},{28,24},{1,5},{5... | collective-permute-start | bytes 589832 | tf_op jit(solution)/shard_map/ppermute | solution.py:20
  32.7 13.6 %collective-permute-start.7 = (bf16[48,24,128]{2,1,0:T(8,128)(2,1)S(1)}, bf16[48,24,128]{2,1,0:T(8,128)(2,1)S(1)}, u32[]{:S(2)}, u32[]{:S(2)}) collective-permute-start(bf16[48,24,128]{2,1,0:T(8,128)(2,1)S(1)} %get-tuple-element.45), channel_id=1, source_target_pairs={{0,4},{4,0},{8,12},{12,8},{16,20},{20,16},{24,28},{28,24},{1,5},{5... | collective-permute-start | bytes 884744 | tf_op jit(solution)/shard_map/ppermute | solution.py:20
  35.9 13.3 %collective-permute-start.14 = (bf16[8,24,1024]{2,1,0:T(8,128)(2,1)S(1)}, bf16[8,24,1024]{2,1,0:T(8,128)(2,1)S(1)}, u32[]{:S(2)}, u32[]{:S(2)}) collective-permute-start(bf16[8,24,1024]{2,1,0:T(8,128)(2,1)S(1)} %get-tuple-element.52), channel_id=1, source_target_pairs={{0,2},{1,3},{2,0},{3,1},{4,6},{5,7},{6,4},{7,5},{8,10},{9,11},{10,... | collective-permute-start | bytes 1179656 | tf_op jit(solution)/shard_map/ppermute | solution.py:36
  41.7 13.7 %collective-permute-start.17 = (bf16[8,48,256]{2,1,0:T(8,128)(2,1)S(1)}, bf16[8,48,256]{2,1,0:T(8,128)(2,1)S(1)}, u32[]{:S(2)}, u32[]{:S(2)}) collective-permute-start(bf16[8,48,256]{2,1,0:T(8,128)(2,1)S(1)} %get-tuple-element.56), channel_id=1, source_target_pairs={{0,4},{4,0},{8,12},{12,8},{16,20},{20,16},{24,28},{28,24},{1,5},{5... | collective-permute-start | bytes 589832 | tf_op jit(solution)/shard_map/ppermute | solution.py:20
  42.3 16.4 %collective-permute-start.16 = (bf16[8,24,1024]{2,1,0:T(8,128)(2,1)S(1)}, bf16[8,24,1024]{2,1,0:T(8,128)(2,1)S(1)}, u32[]{:S(2)}, u32[]{:S(2)}) collective-permute-start(bf16[8,24,1024]{2,1,0:T(8,128)(2,1)S(1)} %get-tuple-element.55), channel_id=1, source_target_pairs={{0,2},{1,3},{2,0},{3,1},{4,6},{5,7},{6,4},{7,5},{8,10},{9,11},{10,... | collective-permute-start | bytes 1179656 | tf_op jit(solution)/shard_map/ppermute | solution.py:36
  52.2 8.7 %collective-permute-start.15 = (bf16[48,24,128]{2,1,0:T(8,128)(2,1)S(1)}, bf16[48,24,128]{2,1,0:T(8,128)(2,1)S(1)}, u32[]{:S(2)}, u32[]{:S(2)}) collective-permute-start(bf16[48,24,128]{2,1,0:T(8,128)(2,1)S(1)} %get-tuple-element.54), channel_id=1, source_target_pairs={{0,4},{4,0},{8,12},{12,8},{16,20},{20,16},{24,28},{28,24},{1,5},{5... | collective-permute-start | bytes 884744 | tf_op jit(solution)/shard_map/ppermute | solution.py:20
  57.0 8.4 %collective-permute-start.22 = (bf16[8,24,1024]{2,1,0:T(8,128)(2,1)S(1)}, bf16[8,24,1024]{2,1,0:T(8,128)(2,1)S(1)}, u32[]{:S(2)}, u32[]{:S(2)}) collective-permute-start(bf16[8,24,1024]{2,1,0:T(8,128)(2,1)S(1)} %get-tuple-element.64), channel_id=1, source_target_pairs={{0,2},{1,3},{2,0},{3,1},{4,6},{5,7},{6,4},{7,5},{8,10},{9,11},{10,... | collective-permute-start | bytes 1179656 | tf_op jit(solution)/shard_map/ppermute | solution.py:36
  59.9 9.9 %collective-permute-start.21 = (bf16[48,24,128]{2,1,0:T(8,128)(2,1)S(1)}, bf16[48,24,128]{2,1,0:T(8,128)(2,1)S(1)}, u32[]{:S(2)}, u32[]{:S(2)}) collective-permute-start(bf16[48,24,128]{2,1,0:T(8,128)(2,1)S(1)} %get-tuple-element.63), channel_id=1, source_target_pairs={{0,4},{4,0},{8,12},{12,8},{16,20},{20,16},{24,28},{28,24},{1,5},{5... | collective-permute-start | bytes 884744 | tf_op jit(solution)/shard_map/ppermute | solution.py:20
  61.0 9.0 %collective-permute-start.18 = (bf16[12,1,24,128]{3,2,1,0:T(8,128)(2,1)S(1)}, bf16[12,1,24,128]{3,2,1,0:T(8,128)(2,1)S(1)}, u32[]{:S(2)}, u32[]{:S(2)}) collective-permute-start(bf16[12,1,24,128]{3,2,1,0:T(8,128)(2,1)S(1)} %get-tuple-element.60), channel_id=1, source_target_pairs={{0,8},{4,12},{8,0},{12,4},{16,24},{20,28},{24,16},{28,20},{1,9},{5... | collective-permute-start | bytes 221192 | tf_op jit(solution)/shard_map/ppermute | solution.py:20
  61.9 9.8 %collective-permute-start.19 = (bf16[12,1,24,128]{3,2,1,0:T(8,128)(2,1)S(1)}, bf16[12,1,24,128]{3,2,1,0:T(8,128)(2,1)S(1)}, u32[]{:S(2)}, u32[]{:S(2)}) collective-permute-start(bf16[12,1,24,128]{3,2,1,0:T(8,128)(2,1)S(1)} %get-tuple-element.61), channel_id=1, source_target_pairs={{0,16},{4,20},{8,24},{12,28},{16,0},{20,4},{24,8},{28,12},{1,17},{... | collective-permute-start | bytes 221192 | tf_op jit(solution)/shard_map/ppermute | solution.py:20
  64.4 9.9 %collective-permute-start.20 = (bf16[12,1,24,128]{3,2,1,0:T(8,128)(2,1)S(1)}, bf16[12,1,24,128]{3,2,1,0:T(8,128)(2,1)S(1)}, u32[]{:S(2)}, u32[]{:S(2)}) collective-permute-start(bf16[12,1,24,128]{3,2,1,0:T(8,128)(2,1)S(1)} %get-tuple-element.62), channel_id=1, source_target_pairs={{0,24},{4,28},{8,16},{12,20},{16,8},{20,12},{24,0},{28,4},{1,25},{... | collective-permute-start | bytes 221192 | tf_op jit(solution)/shard_map/ppermute | solution.py:20
  66.7 7.6 %collective-permute-start.26 = (bf16[48,24,128]{2,1,0:T(8,128)(2,1)S(1)}, bf16[48,24,128]{2,1,0:T(8,128)(2,1)S(1)}, u32[]{:S(2)}, u32[]{:S(2)}) collective-permute-start(bf16[48,24,128]{2,1,0:T(8,128)(2,1)S(1)} %get-tuple-element.70), channel_id=1, source_target_pairs={{0,4},{4,0},{8,12},{12,8},{16,20},{20,16},{24,28},{28,24},{1,5},{5... | collective-permute-start | bytes 884744 | tf_op jit(solution)/shard_map/ppermute | solution.py:20
  69.9 7.1 %collective-permute-start.23 = (bf16[12,1,24,128]{3,2,1,0:T(8,128)(2,1)S(1)}, bf16[12,1,24,128]{3,2,1,0:T(8,128)(2,1)S(1)}, u32[]{:S(2)}, u32[]{:S(2)}) collective-permute-start(bf16[12,1,24,128]{3,2,1,0:T(8,128)(2,1)S(1)} %get-tuple-element.67), channel_id=1, source_target_pairs={{0,8},{4,12},{8,0},{12,4},{16,24},{20,28},{24,16},{28,20},{1,9},{5... | collective-permute-start | bytes 221192 | tf_op jit(solution)/shard_map/ppermute | solution.py:20
  70.0 9.3 %collective-permute-start.24 = (bf16[12,1,24,128]{3,2,1,0:T(8,128)(2,1)S(1)}, bf16[12,1,24,128]{3,2,1,0:T(8,128)(2,1)S(1)}, u32[]{:S(2)}, u32[]{:S(2)}) collective-permute-start(bf16[12,1,24,128]{3,2,1,0:T(8,128)(2,1)S(1)} %get-tuple-element.68), channel_id=1, source_target_pairs={{0,16},{4,20},{8,24},{12,28},{16,0},{20,4},{24,8},{28,12},{1,17},{... | collective-permute-start | bytes 221192 | tf_op jit(solution)/shard_map/ppermute | solution.py:20
  71.7 7.5 %collective-permute-start.25 = (bf16[12,1,24,128]{3,2,1,0:T(8,128)(2,1)S(1)}, bf16[12,1,24,128]{3,2,1,0:T(8,128)(2,1)S(1)}, u32[]{:S(2)}, u32[]{:S(2)}) collective-permute-start(bf16[12,1,24,128]{3,2,1,0:T(8,128)(2,1)S(1)} %get-tuple-element.69), channel_id=1, source_target_pairs={{0,24},{4,28},{8,16},{12,20},{16,8},{20,12},{24,0},{28,4},{1,25},{... | collective-permute-start | bytes 221192 | tf_op jit(solution)/shard_map/ppermute | solution.py:20
  74.5 7.0 %collective-permute-start.28 = (bf16[12,1,24,128]{3,2,1,0:T(8,128)(2,1)S(1)}, bf16[12,1,24,128]{3,2,1,0:T(8,128)(2,1)S(1)}, u32[]{:S(2)}, u32[]{:S(2)}) collective-permute-start(bf16[12,1,24,128]{3,2,1,0:T(8,128)(2,1)S(1)} %get-tuple-element.73), channel_id=1, source_target_pairs={{0,16},{4,20},{8,24},{12,28},{16,0},{20,4},{24,8},{28,12},{1,17},{... | collective-permute-start | bytes 221192 | tf_op jit(solution)/shard_map/ppermute | solution.py:20
  (10 other events, 51.3 us)

commit v4 on v3

--- a/solution.py
+++ b/solution.py
@@ -342,7 +342,7 @@
 
     def do_add(group):
         def use(out):
-            for e in range(nz):
+            for e in reversed(range(nz)):
                 received.append((blk_swap(out[e], e, 0, nz, nx) if e else out[0], [e ^ d for d in group]))
 
         return add_split([by_owner[d] for d in group], nz), use
@@ -401,8 +401,8 @@
             (20, [(m, 2), (a, 3)]),
             (20, [(s, (0,))]),
             (20, [(r, 1)]),
-            (20, [(m, 3), ("sent", 0)]),
-            (20, [(r, 2)]),
+            (20, [(m, 3)]),
+            (20, [(r, 2), ("sent", 0)]),
             (20, [(s, (1,))]),
             (20, [(r, 3)]),
             (20, [(s, (2,))]),

time: 84.2 us -> 82.6 us (0.981)
  waiting for transfers between devices: 22.8 us -> 20.4 us
    ppermute x24, waiting for transfers between devices: 22.7 us -> 20.3 us  [blk_swap(): return lax.ppermute(value, 'blk', pairs)]
  transfers between devices with their start and end apart: 30 -> 30, of which waited for: 11 -> 9; matrix products, arithmetic and copies ran while one was open for 3% -> 3% of each run, Pallas kernels for 17% -> 18%
where the time goes in v4:
time: 82.6 us; the launch traced here: 82.4 us
  starting transfers between devices  43.4 us (53%)
  waiting for transfers between devices  20.4 us (25%)
  Pallas kernels  15.4 us (19%)
  other arithmetic  2.7 us (3%)
    ppermute x24, starting transfers between devices, blk_swap(): return lax.ppermute(value, 'blk', pairs)  33.9 us
    ppermute x24, waiting for transfers between devices, blk_swap(): return lax.ppermute(value, 'blk', pairs)  20.3 us
    pallas_call x18, Pallas kernels, launch(): pl.pallas_call(kernel, in_specs=[SMEM] * len(scalars) + [VMEM] * len(arra...  15.4 us
    ppermute x6, starting transfers between devices, pair_swap(): return lax.ppermute(value, 'pair', pairs)  9.53 us
  transfers between devices with their start and end apart: 30, of which 9 were waited for; matrix products, arithmetic and copies ran while one was open for 3% of the time, Pallas kernels for 18%

profile of v4, /device:TPU:0, one launch (start us, length us, event | category | flops | bytes accessed | tf_op | source)
XLA Modules:
  0.0 82.4 jit_solution(12326859242884241167)
XLA Ops:
  2.6 2.6 %collective-permute-start = (bf16[12,24,256]{2,1,0:T(8,128)(2,1)S(1)}, bf16[12,24,256]{2,1,0:T(8,128)(2,1)S(1)}, u32[]{:S(2)}, u32[]{:S(2)}) collective-permute-start(bf16[12,24,256]{2,1,0:T(8,128)(2,1)S(1)} %pad_maximum_fusion.2), channel_id=1, source_target_pairs={{0,2},{1,3},{2,0},{3,1},{4,6},{5,7},{6,4},{7,5},{8,10},{9,11},{10,... | collective-permute-start | bytes 442376 | tf_op jit(solution)/shard_map/ppermute | solution.py:36
  7.6 2.2 %hold.1.refs_2_.refs_5_.refs_3_ = bf16[8,256,1024]{2,1,0:T(8,128)(2,1)S(1)} custom-call(bf16[8,256,1024]{2,1,0:T(8,128)(2,1)} %collective-permute-done.2.refs_0_), custom_call_target="tpu_custom_call" | custom-call | flops 2400000000 | tf_op jit(solution)/shard_map/hold/pallas_call | solution.py:84
  9.8 2.9 %collective-permute-start.3 = (bf16[12,24,256]{2,1,0:T(8,128)(2,1)S(1)}, bf16[12,24,256]{2,1,0:T(8,128)(2,1)S(1)}, u32[]{:S(2)}, u32[]{:S(2)}) collective-permute-start(bf16[12,24,256]{2,1,0:T(8,128)(2,1)S(1)} %get-tuple-element.40.refs_7_), channel_id=1, source_target_pairs={{0,4},{4,0},{8,12},{12,8},{16,20},{20,16},{24,28},{28,24},{1,5},{5... | collective-permute-start | bytes 442376 | tf_op jit(solution)/shard_map/ppermute | solution.py:20
  14.3 2.6 %collective-permute-start.5 = (bf16[12,48,256]{2,1,0:T(8,128)(2,1)S(1)}, bf16[12,48,256]{2,1,0:T(8,128)(2,1)S(1)}, u32[]{:S(2)}, u32[]{:S(2)}) collective-permute-start(bf16[12,48,256]{2,1,0:T(8,128)(2,1)S(1)} %get-tuple-element.43), channel_id=1, source_target_pairs={{0,16},{4,20},{8,24},{12,28},{16,0},{20,4},{24,8},{28,12},{1,17},{... | collective-permute-start | bytes 884744 | tf_op jit(solution)/shard_map/ppermute | solution.py:20
  17.0 1.7 %multiply.3 = (bf16[8,24,1024]{2,1,0:T(8,128)(2,1)S(1)}, bf16[8,24,1024]{2,1,0:T(8,128)(2,1)S(1)}) custom-call(bf16[12,24,256]{2,1,0:T(8,128)(2,1)S(1)} %pad_maximum_fusion.1.refs_1_.refs_0_, bf16[12,24,256]{2,1,0:T(8,128)(2,1)S(1)} %collective-permute-done.refs_0_.refs_1_, bf16[13,24,256]{2,1,0:T(8,128)(2,1)S(1)} %collective-permute-done.1.refs_2_.refs_1_.refs_6_, ...), custom_call_target="tpu_custom_call" | custom-call | flops 600000000 | tf_op jit(solution)/shard_map/multiply/pallas_call | solution.py:84
  18.6 1.8 %collective-permute-start.4 = (bf16[8,24,1024]{2,1,0:T(8,128)(2,1)S(1)}, bf16[8,24,1024]{2,1,0:T(8,128)(2,1)S(1)}, u32[]{:S(2)}, u32[]{:S(2)}) collective-permute-start(bf16[8,24,1024]{2,1,0:T(8,128)(2,1)S(1)} %get-tuple-element.42), channel_id=1, source_target_pairs={{0,2},{1,3},{2,0},{3,1},{4,6},{5,7},{6,4},{7,5},{8,10},{9,11},{10,... | collective-permute-start | bytes 1179656 | tf_op jit(solution)/shard_map/ppermute | solution.py:36
  20.4 7.3 %collective-permute-done.6.refs_0_ = bf16[12,48,256]{2,1,0:T(8,128)(2,1)S(1)} collective-permute-done((bf16[12,48,256]{2,1,0:T(8,128)(2,1)S(1)}, bf16[12,48,256]{2,1,0:T(8,128)(2,1)S(1)}, u32[]{:S(2)}, u32[]{:S(2)}) %collective-permute-start.6) | collective-permute-done | bytes 294944 | tf_op jit(solution)/shard_map/ppermute | solution.py:20
  28.4 1.7 %collective-permute-done.5.refs_0_ = bf16[12,48,256]{2,1,0:T(8,128)(2,1)S(1)} collective-permute-done((bf16[12,48,256]{2,1,0:T(8,128)(2,1)S(1)}, bf16[12,48,256]{2,1,0:T(8,128)(2,1)S(1)}, u32[]{:S(2)}, u32[]{:S(2)}) %collective-permute-start.5) | collective-permute-done | bytes 294944 | tf_op jit(solution)/shard_map/ppermute | solution.py:20
  34.2 1.7 %multiply.4 = (bf16[8,24,1024]{2,1,0:T(8,128)(2,1)S(1)}, bf16[8,24,1024]{2,1,0:T(8,128)(2,1)S(1)}) custom-call(bf16[12,48,256]{2,1,0:T(8,128)(2,1)S(1)} %collective-permute-done.6.refs_0_, bf16[8,48,256]{2,1,0:T(8,128)(2,1)S(1)} %collective-permute-done.10.refs_1_, bf16[8,256,1024]{2,1,0:T(8,128)(2,1)S(1)} %copy-done, ...), custom_call_target="tpu_custom_call" | custom-call | flops 6000000000 | tf_op jit(solution)/shard_map/multiply/pallas_call | solution.py:84
  37.4 2.5 %collective-permute-done.8.refs_1_ = bf16[8,48,256]{2,1,0:T(8,128)(2,1)S(1)} collective-permute-done((bf16[8,48,256]{2,1,0:T(8,128)(2,1)S(1)}, bf16[8,48,256]{2,1,0:T(8,128)(2,1)S(1)}, u32[]{:S(2)}, u32[]{:S(2)}) %collective-permute-start.8) | collective-permute-done | bytes 196640 | tf_op jit(solution)/shard_map/ppermute | solution.py:20
  40.0 1.7 %multiply_arrive.1 = (bf16[8,24,1024]{2,1,0:T(8,128)(2,1)S(1)}, bf16[8,24,1024]{2,1,0:T(8,128)(2,1)S(1)}, bf16[8,48,256]{2,1,0:T(8,128)(2,1)S(1)}) custom-call(bf16[12,48,256]{2,1,0:T(8,128)(2,1)S(1)} %collective-permute-done.5.refs_0_, bf16[8,48,256]{2,1,0:T(8,128)(2,1)S(1)} %collective-permute-done.8.refs_1_, bf16[8,256,1024]{2,1,0:T(8,128)(2,1)S(1)} %copy-done, ...), custom_call_target="tpu_custom_call" | custom-call | flops 6000000000 | tf_op jit(solution)/shard_map/multiply_arrive/pallas_call | solution.py:84
  43.8 2.5 %collective-permute-done.7.refs_1_ = bf16[48,24,128]{2,1,0:T(8,128)(2,1)S(1)} collective-permute-done((bf16[48,24,128]{2,1,0:T(8,128)(2,1)S(1)}, bf16[48,24,128]{2,1,0:T(8,128)(2,1)S(1)}, u32[]{:S(2)}, u32[]{:S(2)}) %collective-permute-start.7) | collective-permute-done | bytes 294944 | tf_op jit(solution)/shard_map/ppermute | solution.py:20
  46.4 2.3 %collective-permute-start.11 = (bf16[12,1,24,128]{3,2,1,0:T(8,128)(2,1)S(1)}, bf16[12,1,24,128]{3,2,1,0:T(8,128)(2,1)S(1)}, u32[]{:S(2)}, u32[]{:S(2)}) collective-permute-start(bf16[12,1,24,128]{3,2,1,0:T(8,128)(2,1)S(1)} %get-tuple-element.48), channel_id=1, source_target_pairs={{0,24},{4,28},{8,16},{12,20},{16,8},{20,12},{24,0},{28,4},{1,25},{... | collective-permute-start | bytes 221192 | tf_op jit(solution)/shard_map/ppermute | solution.py:20
  48.6 2.2 %collective-permute-start.13 = (bf16[12,1,24,128]{3,2,1,0:T(8,128)(2,1)S(1)}, bf16[12,1,24,128]{3,2,1,0:T(8,128)(2,1)S(1)}, u32[]{:S(2)}, u32[]{:S(2)}) collective-permute-start(bf16[12,1,24,128]{3,2,1,0:T(8,128)(2,1)S(1)} %get-tuple-element.50), channel_id=1, source_target_pairs={{0,8},{4,12},{8,0},{12,4},{16,24},{20,28},{24,16},{28,20},{1,9},{5... | collective-permute-start | bytes 221192 | tf_op jit(solution)/shard_map/ppermute | solution.py:20
  52.7 1.7 %multiply.5 = (bf16[8,24,1024]{2,1,0:T(8,128)(2,1)S(1)}, bf16[8,24,1024]{2,1,0:T(8,128)(2,1)S(1)}) custom-call(bf16[12,48,256]{2,1,0:T(8,128)(2,1)S(1)} %collective-permute-done.9.refs_5_.refs_0_, bf16[8,48,256]{2,1,0:T(8,128)(2,1)S(1)} %collective-permute-done.17.refs_1_, bf16[8,256,1024]{2,1,0:T(8,128)(2,1)S(1)} %copy-done, ...), custom_call_target="tpu_custom_call" | custom-call | flops 6000000000 | tf_op jit(solution)/shard_map/multiply/pallas_call | solution.py:84
  58.8 2.2 %collective-permute-done.15.refs_1_ = bf16[48,24,128]{2,1,0:T(8,128)(2,1)S(1)} collective-permute-done((bf16[48,24,128]{2,1,0:T(8,128)(2,1)S(1)}, bf16[48,24,128]{2,1,0:T(8,128)(2,1)S(1)}, u32[]{:S(2)}, u32[]{:S(2)}) %collective-permute-start.15) | collective-permute-done | bytes 294944 | tf_op jit(solution)/shard_map/ppermute | solution.py:20
  61.0 2.6 %collective-permute-start.18 = (bf16[12,1,24,128]{3,2,1,0:T(8,128)(2,1)S(1)}, bf16[12,1,24,128]{3,2,1,0:T(8,128)(2,1)S(1)}, u32[]{:S(2)}, u32[]{:S(2)}) collective-permute-start(bf16[12,1,24,128]{3,2,1,0:T(8,128)(2,1)S(1)} %get-tuple-element.59), channel_id=1, source_target_pairs={{0,24},{4,28},{8,16},{12,20},{16,8},{20,12},{24,0},{28,4},{1,25},{... | collective-permute-start | bytes 221192 | tf_op jit(solution)/shard_map/ppermute | solution.py:20
  63.7 1.8 %collective-permute-start.20 = (bf16[12,1,24,128]{3,2,1,0:T(8,128)(2,1)S(1)}, bf16[12,1,24,128]{3,2,1,0:T(8,128)(2,1)S(1)}, u32[]{:S(2)}, u32[]{:S(2)}) collective-permute-start(bf16[12,1,24,128]{3,2,1,0:T(8,128)(2,1)S(1)} %get-tuple-element.61), channel_id=1, source_target_pairs={{0,8},{4,12},{8,0},{12,4},{16,24},{20,28},{24,16},{28,20},{1,9},{5... | collective-permute-start | bytes 221192 | tf_op jit(solution)/shard_map/ppermute | solution.py:20
  66.8 1.6 %collective-permute-start.26 = (bf16[48,24,128]{2,1,0:T(8,128)(2,1)S(1)}, bf16[48,24,128]{2,1,0:T(8,128)(2,1)S(1)}, u32[]{:S(2)}, u32[]{:S(2)}) collective-permute-start(bf16[48,24,128]{2,1,0:T(8,128)(2,1)S(1)} %get-tuple-element.70), channel_id=1, source_target_pairs={{0,4},{4,0},{8,12},{12,8},{16,20},{20,16},{24,28},{28,24},{1,5},{5... | collective-permute-start | bytes 884744 | tf_op jit(solution)/shard_map/ppermute | solution.py:20
  68.5 2.6 %collective-permute-start.23 = (bf16[12,1,24,128]{3,2,1,0:T(8,128)(2,1)S(1)}, bf16[12,1,24,128]{3,2,1,0:T(8,128)(2,1)S(1)}, u32[]{:S(2)}, u32[]{:S(2)}) collective-permute-start(bf16[12,1,24,128]{3,2,1,0:T(8,128)(2,1)S(1)} %get-tuple-element.66), channel_id=1, source_target_pairs={{0,24},{4,28},{8,16},{12,20},{16,8},{20,12},{24,0},{28,4},{1,25},{... | collective-permute-start | bytes 221192 | tf_op jit(solution)/shard_map/ppermute | solution.py:20
  71.1 1.8 %collective-permute-start.25 = (bf16[12,1,24,128]{3,2,1,0:T(8,128)(2,1)S(1)}, bf16[12,1,24,128]{3,2,1,0:T(8,128)(2,1)S(1)}, u32[]{:S(2)}, u32[]{:S(2)}) collective-permute-start(bf16[12,1,24,128]{3,2,1,0:T(8,128)(2,1)S(1)} %get-tuple-element.68), channel_id=1, source_target_pairs={{0,8},{4,12},{8,0},{12,4},{16,24},{20,28},{24,16},{28,20},{1,9},{5... | collective-permute-start | bytes 221192 | tf_op jit(solution)/shard_map/ppermute | solution.py:20
  73.6 2.6 %collective-permute-start.27 = (bf16[12,1,24,128]{3,2,1,0:T(8,128)(2,1)S(1)}, bf16[12,1,24,128]{3,2,1,0:T(8,128)(2,1)S(1)}, u32[]{:S(2)}, u32[]{:S(2)}) collective-permute-start(bf16[12,1,24,128]{3,2,1,0:T(8,128)(2,1)S(1)} %get-tuple-element.71), channel_id=1, source_target_pairs={{0,24},{4,28},{8,16},{12,20},{16,8},{20,12},{24,0},{28,4},{1,25},{... | collective-permute-start | bytes 221192 | tf_op jit(solution)/shard_map/ppermute | solution.py:20
  76.2 1.8 %collective-permute-start.29 = (bf16[12,1,24,128]{3,2,1,0:T(8,128)(2,1)S(1)}, bf16[12,1,24,128]{3,2,1,0:T(8,128)(2,1)S(1)}, u32[]{:S(2)}, u32[]{:S(2)}) collective-permute-start(bf16[12,1,24,128]{3,2,1,0:T(8,128)(2,1)S(1)} %get-tuple-element.73), channel_id=1, source_target_pairs={{0,8},{4,12},{8,0},{12,4},{16,24},{20,28},{24,16},{28,20},{1,9},{5... | collective-permute-start | bytes 221192 | tf_op jit(solution)/shard_map/ppermute | solution.py:20
  78.1 1.8 %collective-permute-done.27.refs_12_ = bf16[12,1,24,128]{3,2,1,0:T(8,128)(2,1)S(1)} collective-permute-done((bf16[12,1,24,128]{3,2,1,0:T(8,128)(2,1)S(1)}, bf16[12,1,24,128]{3,2,1,0:T(8,128)(2,1)S(1)}, u32[]{:S(2)}, u32[]{:S(2)}) %collective-permute-start.27) | collective-permute-done | bytes 73760 | tf_op jit(solution)/shard_map/ppermute | solution.py:20
  (71 shorter events, 25.8 us)
Async XLA Ops:
  0.0 7.6 %collective-permute-start.2 = (bf16[8,256,1024]{2,1,0:T(8,128)(2,1)}, bf16[8,256,1024]{2,1,0:T(8,128)(2,1)}, u32[]{:S(2)}, u32[]{:S(2)}) collective-permute-start(bf16[8,256,1024]{2,1,0:T(8,128)(2,1)} %refs_2_.11), channel_id=1, source_target_pairs={{0,1},{1,0},{2,3},{3,2},{4,5},{5,4},{6,7},{7,6},{8,9},{9,8},{10,11... | collective-permute-start | bytes 12582920 | tf_op jit(solution)/shard_map/ppermute | solution.py:36
  2.6 7.2 %collective-permute-start = (bf16[12,24,256]{2,1,0:T(8,128)(2,1)S(1)}, bf16[12,24,256]{2,1,0:T(8,128)(2,1)S(1)}, u32[]{:S(2)}, u32[]{:S(2)}) collective-permute-start(bf16[12,24,256]{2,1,0:T(8,128)(2,1)S(1)} %pad_maximum_fusion.2), channel_id=1, source_target_pairs={{0,2},{1,3},{2,0},{3,1},{4,6},{5,7},{6,4},{7,5},{8,10},{9,11},{10,... | collective-permute-start | bytes 442376 | tf_op jit(solution)/shard_map/ppermute | solution.py:36
  5.9 11.0 %collective-permute-start.1 = (bf16[13,24,256]{2,1,0:T(8,128)(2,1)S(1)}, bf16[13,24,256]{2,1,0:T(8,128)(2,1)S(1)}, u32[]{:S(2)}, u32[]{:S(2)}) collective-permute-start(bf16[13,24,256]{2,1,0:T(8,128)(2,1)S(1)} %pad_maximum_fusion.refs_6_.refs_4_), channel_id=1, source_target_pairs={{0,4},{4,0},{8,12},{12,8},{16,20},{20,16},{24,28},{28,24},{1,5},{5... | collective-permute-start | bytes 479240 | tf_op jit(solution)/shard_map/ppermute | solution.py:20
  9.8 7.1 %collective-permute-start.3 = (bf16[12,24,256]{2,1,0:T(8,128)(2,1)S(1)}, bf16[12,24,256]{2,1,0:T(8,128)(2,1)S(1)}, u32[]{:S(2)}, u32[]{:S(2)}) collective-permute-start(bf16[12,24,256]{2,1,0:T(8,128)(2,1)S(1)} %get-tuple-element.40.refs_7_), channel_id=1, source_target_pairs={{0,4},{4,0},{8,12},{12,8},{16,20},{20,16},{24,28},{28,24},{1,5},{5... | collective-permute-start | bytes 442376 | tf_op jit(solution)/shard_map/ppermute | solution.py:20
  12.8 15.0 %collective-permute-start.6 = (bf16[12,48,256]{2,1,0:T(8,128)(2,1)S(1)}, bf16[12,48,256]{2,1,0:T(8,128)(2,1)S(1)}, u32[]{:S(2)}, u32[]{:S(2)}) collective-permute-start(bf16[12,48,256]{2,1,0:T(8,128)(2,1)S(1)} %get-tuple-element.43), channel_id=1, source_target_pairs={{0,8},{4,12},{8,0},{12,4},{16,24},{20,28},{24,16},{28,20},{1,9},{5... | collective-permute-start | bytes 884744 | tf_op jit(solution)/shard_map/ppermute | solution.py:20
  14.3 15.8 %collective-permute-start.5 = (bf16[12,48,256]{2,1,0:T(8,128)(2,1)S(1)}, bf16[12,48,256]{2,1,0:T(8,128)(2,1)S(1)}, u32[]{:S(2)}, u32[]{:S(2)}) collective-permute-start(bf16[12,48,256]{2,1,0:T(8,128)(2,1)S(1)} %get-tuple-element.43), channel_id=1, source_target_pairs={{0,16},{4,20},{8,24},{12,28},{16,0},{20,4},{24,8},{28,12},{1,17},{... | collective-permute-start | bytes 884744 | tf_op jit(solution)/shard_map/ppermute | solution.py:20
  18.6 12.0 %collective-permute-start.4 = (bf16[8,24,1024]{2,1,0:T(8,128)(2,1)S(1)}, bf16[8,24,1024]{2,1,0:T(8,128)(2,1)S(1)}, u32[]{:S(2)}, u32[]{:S(2)}) collective-permute-start(bf16[8,24,1024]{2,1,0:T(8,128)(2,1)S(1)} %get-tuple-element.42), channel_id=1, source_target_pairs={{0,2},{1,3},{2,0},{3,1},{4,6},{5,7},{6,4},{7,5},{8,10},{9,11},{10,... | collective-permute-start | bytes 1179656 | tf_op jit(solution)/shard_map/ppermute | solution.py:36
  30.1 7.3 %collective-permute-start.9 = (bf16[12,48,256]{2,1,0:T(8,128)(2,1)S(1)}, bf16[12,48,256]{2,1,0:T(8,128)(2,1)S(1)}, u32[]{:S(2)}, u32[]{:S(2)}) collective-permute-start(bf16[12,48,256]{2,1,0:T(8,128)(2,1)S(1)} %forward.1.refs_5_), channel_id=1, source_target_pairs={{0,8},{4,12},{8,0},{12,4},{16,24},{20,28},{24,16},{28,20},{1,9},{5... | collective-permute-start | bytes 884744 | tf_op jit(solution)/shard_map/ppermute | solution.py:20
  32.1 7.9 %collective-permute-start.8 = (bf16[8,48,256]{2,1,0:T(8,128)(2,1)S(1)}, bf16[8,48,256]{2,1,0:T(8,128)(2,1)S(1)}, u32[]{:S(2)}, u32[]{:S(2)}) collective-permute-start(bf16[8,48,256]{2,1,0:T(8,128)(2,1)S(1)} %arrive.3.refs_5_), channel_id=1, source_target_pairs={{0,4},{4,0},{8,12},{12,8},{16,20},{20,16},{24,28},{28,24},{1,5},{5... | collective-permute-start | bytes 589832 | tf_op jit(solution)/shard_map/ppermute | solution.py:20
  32.7 13.6 %collective-permute-start.7 = (bf16[48,24,128]{2,1,0:T(8,128)(2,1)S(1)}, bf16[48,24,128]{2,1,0:T(8,128)(2,1)S(1)}, u32[]{:S(2)}, u32[]{:S(2)}) collective-permute-start(bf16[48,24,128]{2,1,0:T(8,128)(2,1)S(1)} %get-tuple-element.45), channel_id=1, source_target_pairs={{0,4},{4,0},{8,12},{12,8},{16,20},{20,16},{24,28},{28,24},{1,5},{5... | collective-permute-start | bytes 884744 | tf_op jit(solution)/shard_map/ppermute | solution.py:20
  35.9 12.8 %collective-permute-start.14 = (bf16[8,24,1024]{2,1,0:T(8,128)(2,1)S(1)}, bf16[8,24,1024]{2,1,0:T(8,128)(2,1)S(1)}, u32[]{:S(2)}, u32[]{:S(2)}) collective-permute-start(bf16[8,24,1024]{2,1,0:T(8,128)(2,1)S(1)} %get-tuple-element.52), channel_id=1, source_target_pairs={{0,2},{1,3},{2,0},{3,1},{4,6},{5,7},{6,4},{7,5},{8,10},{9,11},{10,... | collective-permute-start | bytes 1179656 | tf_op jit(solution)/shard_map/ppermute | solution.py:36
  41.7 10.4 %collective-permute-start.17 = (bf16[8,48,256]{2,1,0:T(8,128)(2,1)S(1)}, bf16[8,48,256]{2,1,0:T(8,128)(2,1)S(1)}, u32[]{:S(2)}, u32[]{:S(2)}) collective-permute-start(bf16[8,48,256]{2,1,0:T(8,128)(2,1)S(1)} %get-tuple-element.56), channel_id=1, source_target_pairs={{0,4},{4,0},{8,12},{12,8},{16,20},{20,16},{24,28},{28,24},{1,5},{5... | collective-permute-start | bytes 589832 | tf_op jit(solution)/shard_map/ppermute | solution.py:20
  42.3 13.7 %collective-permute-start.16 = (bf16[8,24,1024]{2,1,0:T(8,128)(2,1)S(1)}, bf16[8,24,1024]{2,1,0:T(8,128)(2,1)S(1)}, u32[]{:S(2)}, u32[]{:S(2)}) collective-permute-start(bf16[8,24,1024]{2,1,0:T(8,128)(2,1)S(1)} %get-tuple-element.55), channel_id=1, source_target_pairs={{0,2},{1,3},{2,0},{3,1},{4,6},{5,7},{6,4},{7,5},{8,10},{9,11},{10,... | collective-permute-start | bytes 1179656 | tf_op jit(solution)/shard_map/ppermute | solution.py:36
  46.4 8.0 %collective-permute-start.11 = (bf16[12,1,24,128]{3,2,1,0:T(8,128)(2,1)S(1)}, bf16[12,1,24,128]{3,2,1,0:T(8,128)(2,1)S(1)}, u32[]{:S(2)}, u32[]{:S(2)}) collective-permute-start(bf16[12,1,24,128]{3,2,1,0:T(8,128)(2,1)S(1)} %get-tuple-element.48), channel_id=1, source_target_pairs={{0,24},{4,28},{8,16},{12,20},{16,8},{20,12},{24,0},{28,4},{1,25},{... | collective-permute-start | bytes 221192 | tf_op jit(solution)/shard_map/ppermute | solution.py:20
  48.6 7.3 %collective-permute-start.12 = (bf16[12,1,24,128]{3,2,1,0:T(8,128)(2,1)S(1)}, bf16[12,1,24,128]{3,2,1,0:T(8,128)(2,1)S(1)}, u32[]{:S(2)}, u32[]{:S(2)}) collective-permute-start(bf16[12,1,24,128]{3,2,1,0:T(8,128)(2,1)S(1)} %get-tuple-element.49), channel_id=1, source_target_pairs={{0,16},{4,20},{8,24},{12,28},{16,0},{20,4},{24,8},{28,12},{1,17},{... | collective-permute-start | bytes 221192 | tf_op jit(solution)/shard_map/ppermute | solution.py:20
  48.6 7.3 %collective-permute-start.13 = (bf16[12,1,24,128]{3,2,1,0:T(8,128)(2,1)S(1)}, bf16[12,1,24,128]{3,2,1,0:T(8,128)(2,1)S(1)}, u32[]{:S(2)}, u32[]{:S(2)}) collective-permute-start(bf16[12,1,24,128]{3,2,1,0:T(8,128)(2,1)S(1)} %get-tuple-element.50), channel_id=1, source_target_pairs={{0,8},{4,12},{8,0},{12,4},{16,24},{20,28},{24,16},{28,20},{1,9},{5... | collective-permute-start | bytes 221192 | tf_op jit(solution)/shard_map/ppermute | solution.py:20
  52.1 8.9 %collective-permute-start.15 = (bf16[48,24,128]{2,1,0:T(8,128)(2,1)S(1)}, bf16[48,24,128]{2,1,0:T(8,128)(2,1)S(1)}, u32[]{:S(2)}, u32[]{:S(2)}) collective-permute-start(bf16[48,24,128]{2,1,0:T(8,128)(2,1)S(1)} %get-tuple-element.54), channel_id=1, source_target_pairs={{0,4},{4,0},{8,12},{12,8},{16,20},{20,16},{24,28},{28,24},{1,5},{5... | collective-permute-start | bytes 884744 | tf_op jit(solution)/shard_map/ppermute | solution.py:20
  54.4 11.1 %collective-permute-start.22 = (bf16[8,24,1024]{2,1,0:T(8,128)(2,1)S(1)}, bf16[8,24,1024]{2,1,0:T(8,128)(2,1)S(1)}, u32[]{:S(2)}, u32[]{:S(2)}) collective-permute-start(bf16[8,24,1024]{2,1,0:T(8,128)(2,1)S(1)} %get-tuple-element.64), channel_id=1, source_target_pairs={{0,2},{1,3},{2,0},{3,1},{4,6},{5,7},{6,4},{7,5},{8,10},{9,11},{10,... | collective-permute-start | bytes 1179656 | tf_op jit(solution)/shard_map/ppermute | solution.py:36
  57.2 11.2 %collective-permute-start.21 = (bf16[48,24,128]{2,1,0:T(8,128)(2,1)S(1)}, bf16[48,24,128]{2,1,0:T(8,128)(2,1)S(1)}, u32[]{:S(2)}, u32[]{:S(2)}) collective-permute-start(bf16[48,24,128]{2,1,0:T(8,128)(2,1)S(1)} %get-tuple-element.63), channel_id=1, source_target_pairs={{0,4},{4,0},{8,12},{12,8},{16,20},{20,16},{24,28},{28,24},{1,5},{5... | collective-permute-start | bytes 884744 | tf_op jit(solution)/shard_map/ppermute | solution.py:20
  61.0 10.1 %collective-permute-start.18 = (bf16[12,1,24,128]{3,2,1,0:T(8,128)(2,1)S(1)}, bf16[12,1,24,128]{3,2,1,0:T(8,128)(2,1)S(1)}, u32[]{:S(2)}, u32[]{:S(2)}) collective-permute-start(bf16[12,1,24,128]{3,2,1,0:T(8,128)(2,1)S(1)} %get-tuple-element.59), channel_id=1, source_target_pairs={{0,24},{4,28},{8,16},{12,20},{16,8},{20,12},{24,0},{28,4},{1,25},{... | collective-permute-start | bytes 221192 | tf_op jit(solution)/shard_map/ppermute | solution.py:20
  63.7 7.5 %collective-permute-start.19 = (bf16[12,1,24,128]{3,2,1,0:T(8,128)(2,1)S(1)}, bf16[12,1,24,128]{3,2,1,0:T(8,128)(2,1)S(1)}, u32[]{:S(2)}, u32[]{:S(2)}) collective-permute-start(bf16[12,1,24,128]{3,2,1,0:T(8,128)(2,1)S(1)} %get-tuple-element.60), channel_id=1, source_target_pairs={{0,16},{4,20},{8,24},{12,28},{16,0},{20,4},{24,8},{28,12},{1,17},{... | collective-permute-start | bytes 221192 | tf_op jit(solution)/shard_map/ppermute | solution.py:20
  63.7 9.3 %collective-permute-start.20 = (bf16[12,1,24,128]{3,2,1,0:T(8,128)(2,1)S(1)}, bf16[12,1,24,128]{3,2,1,0:T(8,128)(2,1)S(1)}, u32[]{:S(2)}, u32[]{:S(2)}) collective-permute-start(bf16[12,1,24,128]{3,2,1,0:T(8,128)(2,1)S(1)} %get-tuple-element.61), channel_id=1, source_target_pairs={{0,8},{4,12},{8,0},{12,4},{16,24},{20,28},{24,16},{28,20},{1,9},{5... | collective-permute-start | bytes 221192 | tf_op jit(solution)/shard_map/ppermute | solution.py:20
  68.5 7.8 %collective-permute-start.23 = (bf16[12,1,24,128]{3,2,1,0:T(8,128)(2,1)S(1)}, bf16[12,1,24,128]{3,2,1,0:T(8,128)(2,1)S(1)}, u32[]{:S(2)}, u32[]{:S(2)}) collective-permute-start(bf16[12,1,24,128]{3,2,1,0:T(8,128)(2,1)S(1)} %get-tuple-element.66), channel_id=1, source_target_pairs={{0,24},{4,28},{8,16},{12,20},{16,8},{20,12},{24,0},{28,4},{1,25},{... | collective-permute-start | bytes 221192 | tf_op jit(solution)/shard_map/ppermute | solution.py:20
  71.1 7.0 %collective-permute-start.24 = (bf16[12,1,24,128]{3,2,1,0:T(8,128)(2,1)S(1)}, bf16[12,1,24,128]{3,2,1,0:T(8,128)(2,1)S(1)}, u32[]{:S(2)}, u32[]{:S(2)}) collective-permute-start(bf16[12,1,24,128]{3,2,1,0:T(8,128)(2,1)S(1)} %get-tuple-element.67), channel_id=1, source_target_pairs={{0,16},{4,20},{8,24},{12,28},{16,0},{20,4},{24,8},{28,12},{1,17},{... | collective-permute-start | bytes 221192 | tf_op jit(solution)/shard_map/ppermute | solution.py:20
  (10 other events, 52.1 us)

commit v5 on v4

--- a/solution.py
+++ b/solution.py
@@ -295,7 +295,7 @@
 
     def do_along():
         def use(out):
-            for d in low_bits():
+            for d in reversed(low_bits()):
                 here[d] = [blk_swap(out[0], d, 0, nz, nx)]
 
         return through(from_y), use

time: 82.6 us -> 82.6 us (level)
  no operation moved by 1% of the time
where the time goes in v5:
time: 82.6 us; the launch traced here: 82.3 us
  starting transfers between devices  43.4 us (53%)
  waiting for transfers between devices  20.4 us (25%)
  Pallas kernels  15.4 us (19%)
  other arithmetic  2.7 us (3%)
    ppermute x24, starting transfers between devices, blk_swap(): return lax.ppermute(value, 'blk', pairs)  33.9 us
    ppermute x24, waiting for transfers between devices, blk_swap(): return lax.ppermute(value, 'blk', pairs)  20.3 us
    pallas_call x18, Pallas kernels, launch(): pl.pallas_call(kernel, in_specs=[SMEM] * len(scalars) + [VMEM] * len(arra...  15.4 us
    ppermute x6, starting transfers between devices, pair_swap(): return lax.ppermute(value, 'pair', pairs)  9.53 us
  transfers between devices with their start and end apart: 30, of which 9 were waited for; matrix products, arithmetic and copies ran while one was open for 3% of the time, Pallas kernels for 18%

profile of v5, /device:TPU:0, one launch (start us, length us, event | category | flops | bytes accessed | tf_op | source)
XLA Modules:
  0.0 82.3 jit_solution(12326859242884241167)
XLA Ops:
  2.6 2.6 %collective-permute-start = (bf16[12,24,256]{2,1,0:T(8,128)(2,1)S(1)}, bf16[12,24,256]{2,1,0:T(8,128)(2,1)S(1)}, u32[]{:S(2)}, u32[]{:S(2)}) collective-permute-start(bf16[12,24,256]{2,1,0:T(8,128)(2,1)S(1)} %pad_maximum_fusion.2), channel_id=1, source_target_pairs={{0,2},{1,3},{2,0},{3,1},{4,6},{5,7},{6,4},{7,5},{8,10},{9,11},{10,... | collective-permute-start | bytes 442376 | tf_op jit(solution)/shard_map/ppermute | solution.py:36
  7.6 2.2 %hold.1.refs_2_.refs_5_.refs_3_ = bf16[8,256,1024]{2,1,0:T(8,128)(2,1)S(1)} custom-call(bf16[8,256,1024]{2,1,0:T(8,128)(2,1)} %collective-permute-done.2.refs_0_), custom_call_target="tpu_custom_call" | custom-call | flops 2400000000 | tf_op jit(solution)/shard_map/hold/pallas_call | solution.py:84
  9.8 2.9 %collective-permute-start.3 = (bf16[12,24,256]{2,1,0:T(8,128)(2,1)S(1)}, bf16[12,24,256]{2,1,0:T(8,128)(2,1)S(1)}, u32[]{:S(2)}, u32[]{:S(2)}) collective-permute-start(bf16[12,24,256]{2,1,0:T(8,128)(2,1)S(1)} %get-tuple-element.40.refs_7_), channel_id=1, source_target_pairs={{0,4},{4,0},{8,12},{12,8},{16,20},{20,16},{24,28},{28,24},{1,5},{5... | collective-permute-start | bytes 442376 | tf_op jit(solution)/shard_map/ppermute | solution.py:20
  14.3 2.6 %collective-permute-start.5 = (bf16[12,48,256]{2,1,0:T(8,128)(2,1)S(1)}, bf16[12,48,256]{2,1,0:T(8,128)(2,1)S(1)}, u32[]{:S(2)}, u32[]{:S(2)}) collective-permute-start(bf16[12,48,256]{2,1,0:T(8,128)(2,1)S(1)} %get-tuple-element.43), channel_id=1, source_target_pairs={{0,16},{4,20},{8,24},{12,28},{16,0},{20,4},{24,8},{28,12},{1,17},{... | collective-permute-start | bytes 884744 | tf_op jit(solution)/shard_map/ppermute | solution.py:20
  17.0 1.7 %multiply.3 = (bf16[8,24,1024]{2,1,0:T(8,128)(2,1)S(1)}, bf16[8,24,1024]{2,1,0:T(8,128)(2,1)S(1)}) custom-call(bf16[12,24,256]{2,1,0:T(8,128)(2,1)S(1)} %pad_maximum_fusion.1.refs_1_.refs_0_, bf16[12,24,256]{2,1,0:T(8,128)(2,1)S(1)} %collective-permute-done.refs_0_.refs_1_, bf16[13,24,256]{2,1,0:T(8,128)(2,1)S(1)} %collective-permute-done.1.refs_2_.refs_1_.refs_6_, ...), custom_call_target="tpu_custom_call" | custom-call | flops 600000000 | tf_op jit(solution)/shard_map/multiply/pallas_call | solution.py:84
  18.6 1.8 %collective-permute-start.4 = (bf16[8,24,1024]{2,1,0:T(8,128)(2,1)S(1)}, bf16[8,24,1024]{2,1,0:T(8,128)(2,1)S(1)}, u32[]{:S(2)}, u32[]{:S(2)}) collective-permute-start(bf16[8,24,1024]{2,1,0:T(8,128)(2,1)S(1)} %get-tuple-element.42), channel_id=1, source_target_pairs={{0,2},{1,3},{2,0},{3,1},{4,6},{5,7},{6,4},{7,5},{8,10},{9,11},{10,... | collective-permute-start | bytes 1179656 | tf_op jit(solution)/shard_map/ppermute | solution.py:36
  20.4 7.3 %collective-permute-done.6.refs_0_ = bf16[12,48,256]{2,1,0:T(8,128)(2,1)S(1)} collective-permute-done((bf16[12,48,256]{2,1,0:T(8,128)(2,1)S(1)}, bf16[12,48,256]{2,1,0:T(8,128)(2,1)S(1)}, u32[]{:S(2)}, u32[]{:S(2)}) %collective-permute-start.6) | collective-permute-done | bytes 294944 | tf_op jit(solution)/shard_map/ppermute | solution.py:20
  28.4 1.7 %collective-permute-done.5.refs_0_ = bf16[12,48,256]{2,1,0:T(8,128)(2,1)S(1)} collective-permute-done((bf16[12,48,256]{2,1,0:T(8,128)(2,1)S(1)}, bf16[12,48,256]{2,1,0:T(8,128)(2,1)S(1)}, u32[]{:S(2)}, u32[]{:S(2)}) %collective-permute-start.5) | collective-permute-done | bytes 294944 | tf_op jit(solution)/shard_map/ppermute | solution.py:20
  34.2 1.7 %multiply.4 = (bf16[8,24,1024]{2,1,0:T(8,128)(2,1)S(1)}, bf16[8,24,1024]{2,1,0:T(8,128)(2,1)S(1)}) custom-call(bf16[12,48,256]{2,1,0:T(8,128)(2,1)S(1)} %collective-permute-done.6.refs_0_, bf16[8,48,256]{2,1,0:T(8,128)(2,1)S(1)} %collective-permute-done.10.refs_1_, bf16[8,256,1024]{2,1,0:T(8,128)(2,1)S(1)} %copy-done, ...), custom_call_target="tpu_custom_call" | custom-call | flops 6000000000 | tf_op jit(solution)/shard_map/multiply/pallas_call | solution.py:84
  37.4 2.5 %collective-permute-done.8.refs_1_ = bf16[8,48,256]{2,1,0:T(8,128)(2,1)S(1)} collective-permute-done((bf16[8,48,256]{2,1,0:T(8,128)(2,1)S(1)}, bf16[8,48,256]{2,1,0:T(8,128)(2,1)S(1)}, u32[]{:S(2)}, u32[]{:S(2)}) %collective-permute-start.8) | collective-permute-done | bytes 196640 | tf_op jit(solution)/shard_map/ppermute | solution.py:20
  40.0 1.7 %multiply_arrive.1 = (bf16[8,24,1024]{2,1,0:T(8,128)(2,1)S(1)}, bf16[8,24,1024]{2,1,0:T(8,128)(2,1)S(1)}, bf16[8,48,256]{2,1,0:T(8,128)(2,1)S(1)}) custom-call(bf16[12,48,256]{2,1,0:T(8,128)(2,1)S(1)} %collective-permute-done.5.refs_0_, bf16[8,48,256]{2,1,0:T(8,128)(2,1)S(1)} %collective-permute-done.8.refs_1_, bf16[8,256,1024]{2,1,0:T(8,128)(2,1)S(1)} %copy-done, ...), custom_call_target="tpu_custom_call" | custom-call | flops 6000000000 | tf_op jit(solution)/shard_map/multiply_arrive/pallas_call | solution.py:84
  43.8 2.5 %collective-permute-done.7.refs_1_ = bf16[48,24,128]{2,1,0:T(8,128)(2,1)S(1)} collective-permute-done((bf16[48,24,128]{2,1,0:T(8,128)(2,1)S(1)}, bf16[48,24,128]{2,1,0:T(8,128)(2,1)S(1)}, u32[]{:S(2)}, u32[]{:S(2)}) %collective-permute-start.7) | collective-permute-done | bytes 294944 | tf_op jit(solution)/shard_map/ppermute | solution.py:20
  46.4 2.3 %collective-permute-start.11 = (bf16[12,1,24,128]{3,2,1,0:T(8,128)(2,1)S(1)}, bf16[12,1,24,128]{3,2,1,0:T(8,128)(2,1)S(1)}, u32[]{:S(2)}, u32[]{:S(2)}) collective-permute-start(bf16[12,1,24,128]{3,2,1,0:T(8,128)(2,1)S(1)} %get-tuple-element.48), channel_id=1, source_target_pairs={{0,24},{4,28},{8,16},{12,20},{16,8},{20,12},{24,0},{28,4},{1,25},{... | collective-permute-start | bytes 221192 | tf_op jit(solution)/shard_map/ppermute | solution.py:20
  48.6 2.2 %collective-permute-start.13 = (bf16[12,1,24,128]{3,2,1,0:T(8,128)(2,1)S(1)}, bf16[12,1,24,128]{3,2,1,0:T(8,128)(2,1)S(1)}, u32[]{:S(2)}, u32[]{:S(2)}) collective-permute-start(bf16[12,1,24,128]{3,2,1,0:T(8,128)(2,1)S(1)} %get-tuple-element.50), channel_id=1, source_target_pairs={{0,8},{4,12},{8,0},{12,4},{16,24},{20,28},{24,16},{28,20},{1,9},{5... | collective-permute-start | bytes 221192 | tf_op jit(solution)/shard_map/ppermute | solution.py:20
  52.7 1.7 %multiply.5 = (bf16[8,24,1024]{2,1,0:T(8,128)(2,1)S(1)}, bf16[8,24,1024]{2,1,0:T(8,128)(2,1)S(1)}) custom-call(bf16[12,48,256]{2,1,0:T(8,128)(2,1)S(1)} %collective-permute-done.9.refs_5_.refs_0_, bf16[8,48,256]{2,1,0:T(8,128)(2,1)S(1)} %collective-permute-done.17.refs_1_, bf16[8,256,1024]{2,1,0:T(8,128)(2,1)S(1)} %copy-done, ...), custom_call_target="tpu_custom_call" | custom-call | flops 6000000000 | tf_op jit(solution)/shard_map/multiply/pallas_call | solution.py:84
  58.8 2.2 %collective-permute-done.15.refs_1_ = bf16[48,24,128]{2,1,0:T(8,128)(2,1)S(1)} collective-permute-done((bf16[48,24,128]{2,1,0:T(8,128)(2,1)S(1)}, bf16[48,24,128]{2,1,0:T(8,128)(2,1)S(1)}, u32[]{:S(2)}, u32[]{:S(2)}) %collective-permute-start.15) | collective-permute-done | bytes 294944 | tf_op jit(solution)/shard_map/ppermute | solution.py:20
  61.0 2.6 %collective-permute-start.18 = (bf16[12,1,24,128]{3,2,1,0:T(8,128)(2,1)S(1)}, bf16[12,1,24,128]{3,2,1,0:T(8,128)(2,1)S(1)}, u32[]{:S(2)}, u32[]{:S(2)}) collective-permute-start(bf16[12,1,24,128]{3,2,1,0:T(8,128)(2,1)S(1)} %get-tuple-element.59), channel_id=1, source_target_pairs={{0,24},{4,28},{8,16},{12,20},{16,8},{20,12},{24,0},{28,4},{1,25},{... | collective-permute-start | bytes 221192 | tf_op jit(solution)/shard_map/ppermute | solution.py:20
  63.7 1.8 %collective-permute-start.20 = (bf16[12,1,24,128]{3,2,1,0:T(8,128)(2,1)S(1)}, bf16[12,1,24,128]{3,2,1,0:T(8,128)(2,1)S(1)}, u32[]{:S(2)}, u32[]{:S(2)}) collective-permute-start(bf16[12,1,24,128]{3,2,1,0:T(8,128)(2,1)S(1)} %get-tuple-element.61), channel_id=1, source_target_pairs={{0,8},{4,12},{8,0},{12,4},{16,24},{20,28},{24,16},{28,20},{1,9},{5... | collective-permute-start | bytes 221192 | tf_op jit(solution)/shard_map/ppermute | solution.py:20
  66.8 1.6 %collective-permute-start.26 = (bf16[48,24,128]{2,1,0:T(8,128)(2,1)S(1)}, bf16[48,24,128]{2,1,0:T(8,128)(2,1)S(1)}, u32[]{:S(2)}, u32[]{:S(2)}) collective-permute-start(bf16[48,24,128]{2,1,0:T(8,128)(2,1)S(1)} %get-tuple-element.70), channel_id=1, source_target_pairs={{0,4},{4,0},{8,12},{12,8},{16,20},{20,16},{24,28},{28,24},{1,5},{5... | collective-permute-start | bytes 884744 | tf_op jit(solution)/shard_map/ppermute | solution.py:20
  68.5 2.6 %collective-permute-start.23 = (bf16[12,1,24,128]{3,2,1,0:T(8,128)(2,1)S(1)}, bf16[12,1,24,128]{3,2,1,0:T(8,128)(2,1)S(1)}, u32[]{:S(2)}, u32[]{:S(2)}) collective-permute-start(bf16[12,1,24,128]{3,2,1,0:T(8,128)(2,1)S(1)} %get-tuple-element.66), channel_id=1, source_target_pairs={{0,24},{4,28},{8,16},{12,20},{16,8},{20,12},{24,0},{28,4},{1,25},{... | collective-permute-start | bytes 221192 | tf_op jit(solution)/shard_map/ppermute | solution.py:20
  71.1 1.8 %collective-permute-start.25 = (bf16[12,1,24,128]{3,2,1,0:T(8,128)(2,1)S(1)}, bf16[12,1,24,128]{3,2,1,0:T(8,128)(2,1)S(1)}, u32[]{:S(2)}, u32[]{:S(2)}) collective-permute-start(bf16[12,1,24,128]{3,2,1,0:T(8,128)(2,1)S(1)} %get-tuple-element.68), channel_id=1, source_target_pairs={{0,8},{4,12},{8,0},{12,4},{16,24},{20,28},{24,16},{28,20},{1,9},{5... | collective-permute-start | bytes 221192 | tf_op jit(solution)/shard_map/ppermute | solution.py:20
  73.6 2.6 %collective-permute-start.27 = (bf16[12,1,24,128]{3,2,1,0:T(8,128)(2,1)S(1)}, bf16[12,1,24,128]{3,2,1,0:T(8,128)(2,1)S(1)}, u32[]{:S(2)}, u32[]{:S(2)}) collective-permute-start(bf16[12,1,24,128]{3,2,1,0:T(8,128)(2,1)S(1)} %get-tuple-element.71), channel_id=1, source_target_pairs={{0,24},{4,28},{8,16},{12,20},{16,8},{20,12},{24,0},{28,4},{1,25},{... | collective-permute-start | bytes 221192 | tf_op jit(solution)/shard_map/ppermute | solution.py:20
  76.2 1.9 %collective-permute-start.29 = (bf16[12,1,24,128]{3,2,1,0:T(8,128)(2,1)S(1)}, bf16[12,1,24,128]{3,2,1,0:T(8,128)(2,1)S(1)}, u32[]{:S(2)}, u32[]{:S(2)}) collective-permute-start(bf16[12,1,24,128]{3,2,1,0:T(8,128)(2,1)S(1)} %get-tuple-element.73), channel_id=1, source_target_pairs={{0,8},{4,12},{8,0},{12,4},{16,24},{20,28},{24,16},{28,20},{1,9},{5... | collective-permute-start | bytes 221192 | tf_op jit(solution)/shard_map/ppermute | solution.py:20
  78.1 1.8 %collective-permute-done.27.refs_12_ = bf16[12,1,24,128]{3,2,1,0:T(8,128)(2,1)S(1)} collective-permute-done((bf16[12,1,24,128]{3,2,1,0:T(8,128)(2,1)S(1)}, bf16[12,1,24,128]{3,2,1,0:T(8,128)(2,1)S(1)}, u32[]{:S(2)}, u32[]{:S(2)}) %collective-permute-start.27) | collective-permute-done | bytes 73760 | tf_op jit(solution)/shard_map/ppermute | solution.py:20
  (71 shorter events, 25.8 us)
Async XLA Ops:
  0.0 7.6 %collective-permute-start.2 = (bf16[8,256,1024]{2,1,0:T(8,128)(2,1)}, bf16[8,256,1024]{2,1,0:T(8,128)(2,1)}, u32[]{:S(2)}, u32[]{:S(2)}) collective-permute-start(bf16[8,256,1024]{2,1,0:T(8,128)(2,1)} %refs_2_.11), channel_id=1, source_target_pairs={{0,1},{1,0},{2,3},{3,2},{4,5},{5,4},{6,7},{7,6},{8,9},{9,8},{10,11... | collective-permute-start | bytes 12582920 | tf_op jit(solution)/shard_map/ppermute | solution.py:36
  2.6 7.2 %collective-permute-start = (bf16[12,24,256]{2,1,0:T(8,128)(2,1)S(1)}, bf16[12,24,256]{2,1,0:T(8,128)(2,1)S(1)}, u32[]{:S(2)}, u32[]{:S(2)}) collective-permute-start(bf16[12,24,256]{2,1,0:T(8,128)(2,1)S(1)} %pad_maximum_fusion.2), channel_id=1, source_target_pairs={{0,2},{1,3},{2,0},{3,1},{4,6},{5,7},{6,4},{7,5},{8,10},{9,11},{10,... | collective-permute-start | bytes 442376 | tf_op jit(solution)/shard_map/ppermute | solution.py:36
  5.9 11.0 %collective-permute-start.1 = (bf16[13,24,256]{2,1,0:T(8,128)(2,1)S(1)}, bf16[13,24,256]{2,1,0:T(8,128)(2,1)S(1)}, u32[]{:S(2)}, u32[]{:S(2)}) collective-permute-start(bf16[13,24,256]{2,1,0:T(8,128)(2,1)S(1)} %pad_maximum_fusion.refs_6_.refs_4_), channel_id=1, source_target_pairs={{0,4},{4,0},{8,12},{12,8},{16,20},{20,16},{24,28},{28,24},{1,5},{5... | collective-permute-start | bytes 479240 | tf_op jit(solution)/shard_map/ppermute | solution.py:20
  9.8 7.1 %collective-permute-start.3 = (bf16[12,24,256]{2,1,0:T(8,128)(2,1)S(1)}, bf16[12,24,256]{2,1,0:T(8,128)(2,1)S(1)}, u32[]{:S(2)}, u32[]{:S(2)}) collective-permute-start(bf16[12,24,256]{2,1,0:T(8,128)(2,1)S(1)} %get-tuple-element.40.refs_7_), channel_id=1, source_target_pairs={{0,4},{4,0},{8,12},{12,8},{16,20},{20,16},{24,28},{28,24},{1,5},{5... | collective-permute-start | bytes 442376 | tf_op jit(solution)/shard_map/ppermute | solution.py:20
  12.8 15.0 %collective-permute-start.6 = (bf16[12,48,256]{2,1,0:T(8,128)(2,1)S(1)}, bf16[12,48,256]{2,1,0:T(8,128)(2,1)S(1)}, u32[]{:S(2)}, u32[]{:S(2)}) collective-permute-start(bf16[12,48,256]{2,1,0:T(8,128)(2,1)S(1)} %get-tuple-element.43), channel_id=1, source_target_pairs={{0,8},{4,12},{8,0},{12,4},{16,24},{20,28},{24,16},{28,20},{1,9},{5... | collective-permute-start | bytes 884744 | tf_op jit(solution)/shard_map/ppermute | solution.py:20
  14.3 15.8 %collective-permute-start.5 = (bf16[12,48,256]{2,1,0:T(8,128)(2,1)S(1)}, bf16[12,48,256]{2,1,0:T(8,128)(2,1)S(1)}, u32[]{:S(2)}, u32[]{:S(2)}) collective-permute-start(bf16[12,48,256]{2,1,0:T(8,128)(2,1)S(1)} %get-tuple-element.43), channel_id=1, source_target_pairs={{0,16},{4,20},{8,24},{12,28},{16,0},{20,4},{24,8},{28,12},{1,17},{... | collective-permute-start | bytes 884744 | tf_op jit(solution)/shard_map/ppermute | solution.py:20
  18.6 12.0 %collective-permute-start.4 = (bf16[8,24,1024]{2,1,0:T(8,128)(2,1)S(1)}, bf16[8,24,1024]{2,1,0:T(8,128)(2,1)S(1)}, u32[]{:S(2)}, u32[]{:S(2)}) collective-permute-start(bf16[8,24,1024]{2,1,0:T(8,128)(2,1)S(1)} %get-tuple-element.42), channel_id=1, source_target_pairs={{0,2},{1,3},{2,0},{3,1},{4,6},{5,7},{6,4},{7,5},{8,10},{9,11},{10,... | collective-permute-start | bytes 1179656 | tf_op jit(solution)/shard_map/ppermute | solution.py:36
  30.1 7.3 %collective-permute-start.9 = (bf16[12,48,256]{2,1,0:T(8,128)(2,1)S(1)}, bf16[12,48,256]{2,1,0:T(8,128)(2,1)S(1)}, u32[]{:S(2)}, u32[]{:S(2)}) collective-permute-start(bf16[12,48,256]{2,1,0:T(8,128)(2,1)S(1)} %forward.1.refs_5_), channel_id=1, source_target_pairs={{0,8},{4,12},{8,0},{12,4},{16,24},{20,28},{24,16},{28,20},{1,9},{5... | collective-permute-start | bytes 884744 | tf_op jit(solution)/shard_map/ppermute | solution.py:20
  32.1 7.9 %collective-permute-start.8 = (bf16[8,48,256]{2,1,0:T(8,128)(2,1)S(1)}, bf16[8,48,256]{2,1,0:T(8,128)(2,1)S(1)}, u32[]{:S(2)}, u32[]{:S(2)}) collective-permute-start(bf16[8,48,256]{2,1,0:T(8,128)(2,1)S(1)} %arrive.3.refs_5_), channel_id=1, source_target_pairs={{0,4},{4,0},{8,12},{12,8},{16,20},{20,16},{24,28},{28,24},{1,5},{5... | collective-permute-start | bytes 589832 | tf_op jit(solution)/shard_map/ppermute | solution.py:20
  32.7 13.6 %collective-permute-start.7 = (bf16[48,24,128]{2,1,0:T(8,128)(2,1)S(1)}, bf16[48,24,128]{2,1,0:T(8,128)(2,1)S(1)}, u32[]{:S(2)}, u32[]{:S(2)}) collective-permute-start(bf16[48,24,128]{2,1,0:T(8,128)(2,1)S(1)} %get-tuple-element.45), channel_id=1, source_target_pairs={{0,4},{4,0},{8,12},{12,8},{16,20},{20,16},{24,28},{28,24},{1,5},{5... | collective-permute-start | bytes 884744 | tf_op jit(solution)/shard_map/ppermute | solution.py:20
  35.9 12.8 %collective-permute-start.14 = (bf16[8,24,1024]{2,1,0:T(8,128)(2,1)S(1)}, bf16[8,24,1024]{2,1,0:T(8,128)(2,1)S(1)}, u32[]{:S(2)}, u32[]{:S(2)}) collective-permute-start(bf16[8,24,1024]{2,1,0:T(8,128)(2,1)S(1)} %get-tuple-element.52), channel_id=1, source_target_pairs={{0,2},{1,3},{2,0},{3,1},{4,6},{5,7},{6,4},{7,5},{8,10},{9,11},{10,... | collective-permute-start | bytes 1179656 | tf_op jit(solution)/shard_map/ppermute | solution.py:36
  41.7 10.4 %collective-permute-start.17 = (bf16[8,48,256]{2,1,0:T(8,128)(2,1)S(1)}, bf16[8,48,256]{2,1,0:T(8,128)(2,1)S(1)}, u32[]{:S(2)}, u32[]{:S(2)}) collective-permute-start(bf16[8,48,256]{2,1,0:T(8,128)(2,1)S(1)} %get-tuple-element.56), channel_id=1, source_target_pairs={{0,4},{4,0},{8,12},{12,8},{16,20},{20,16},{24,28},{28,24},{1,5},{5... | collective-permute-start | bytes 589832 | tf_op jit(solution)/shard_map/ppermute | solution.py:20
  42.3 13.7 %collective-permute-start.16 = (bf16[8,24,1024]{2,1,0:T(8,128)(2,1)S(1)}, bf16[8,24,1024]{2,1,0:T(8,128)(2,1)S(1)}, u32[]{:S(2)}, u32[]{:S(2)}) collective-permute-start(bf16[8,24,1024]{2,1,0:T(8,128)(2,1)S(1)} %get-tuple-element.55), channel_id=1, source_target_pairs={{0,2},{1,3},{2,0},{3,1},{4,6},{5,7},{6,4},{7,5},{8,10},{9,11},{10,... | collective-permute-start | bytes 1179656 | tf_op jit(solution)/shard_map/ppermute | solution.py:36
  46.4 8.0 %collective-permute-start.11 = (bf16[12,1,24,128]{3,2,1,0:T(8,128)(2,1)S(1)}, bf16[12,1,24,128]{3,2,1,0:T(8,128)(2,1)S(1)}, u32[]{:S(2)}, u32[]{:S(2)}) collective-permute-start(bf16[12,1,24,128]{3,2,1,0:T(8,128)(2,1)S(1)} %get-tuple-element.48), channel_id=1, source_target_pairs={{0,24},{4,28},{8,16},{12,20},{16,8},{20,12},{24,0},{28,4},{1,25},{... | collective-permute-start | bytes 221192 | tf_op jit(solution)/shard_map/ppermute | solution.py:20
  48.6 7.3 %collective-permute-start.12 = (bf16[12,1,24,128]{3,2,1,0:T(8,128)(2,1)S(1)}, bf16[12,1,24,128]{3,2,1,0:T(8,128)(2,1)S(1)}, u32[]{:S(2)}, u32[]{:S(2)}) collective-permute-start(bf16[12,1,24,128]{3,2,1,0:T(8,128)(2,1)S(1)} %get-tuple-element.49), channel_id=1, source_target_pairs={{0,16},{4,20},{8,24},{12,28},{16,0},{20,4},{24,8},{28,12},{1,17},{... | collective-permute-start | bytes 221192 | tf_op jit(solution)/shard_map/ppermute | solution.py:20
  48.6 7.3 %collective-permute-start.13 = (bf16[12,1,24,128]{3,2,1,0:T(8,128)(2,1)S(1)}, bf16[12,1,24,128]{3,2,1,0:T(8,128)(2,1)S(1)}, u32[]{:S(2)}, u32[]{:S(2)}) collective-permute-start(bf16[12,1,24,128]{3,2,1,0:T(8,128)(2,1)S(1)} %get-tuple-element.50), channel_id=1, source_target_pairs={{0,8},{4,12},{8,0},{12,4},{16,24},{20,28},{24,16},{28,20},{1,9},{5... | collective-permute-start | bytes 221192 | tf_op jit(solution)/shard_map/ppermute | solution.py:20
  52.1 8.9 %collective-permute-start.15 = (bf16[48,24,128]{2,1,0:T(8,128)(2,1)S(1)}, bf16[48,24,128]{2,1,0:T(8,128)(2,1)S(1)}, u32[]{:S(2)}, u32[]{:S(2)}) collective-permute-start(bf16[48,24,128]{2,1,0:T(8,128)(2,1)S(1)} %get-tuple-element.54), channel_id=1, source_target_pairs={{0,4},{4,0},{8,12},{12,8},{16,20},{20,16},{24,28},{28,24},{1,5},{5... | collective-permute-start | bytes 884744 | tf_op jit(solution)/shard_map/ppermute | solution.py:20
  54.4 11.1 %collective-permute-start.22 = (bf16[8,24,1024]{2,1,0:T(8,128)(2,1)S(1)}, bf16[8,24,1024]{2,1,0:T(8,128)(2,1)S(1)}, u32[]{:S(2)}, u32[]{:S(2)}) collective-permute-start(bf16[8,24,1024]{2,1,0:T(8,128)(2,1)S(1)} %get-tuple-element.64), channel_id=1, source_target_pairs={{0,2},{1,3},{2,0},{3,1},{4,6},{5,7},{6,4},{7,5},{8,10},{9,11},{10,... | collective-permute-start | bytes 1179656 | tf_op jit(solution)/shard_map/ppermute | solution.py:36
  57.2 11.2 %collective-permute-start.21 = (bf16[48,24,128]{2,1,0:T(8,128)(2,1)S(1)}, bf16[48,24,128]{2,1,0:T(8,128)(2,1)S(1)}, u32[]{:S(2)}, u32[]{:S(2)}) collective-permute-start(bf16[48,24,128]{2,1,0:T(8,128)(2,1)S(1)} %get-tuple-element.63), channel_id=1, source_target_pairs={{0,4},{4,0},{8,12},{12,8},{16,20},{20,16},{24,28},{28,24},{1,5},{5... | collective-permute-start | bytes 884744 | tf_op jit(solution)/shard_map/ppermute | solution.py:20
  61.0 10.1 %collective-permute-start.18 = (bf16[12,1,24,128]{3,2,1,0:T(8,128)(2,1)S(1)}, bf16[12,1,24,128]{3,2,1,0:T(8,128)(2,1)S(1)}, u32[]{:S(2)}, u32[]{:S(2)}) collective-permute-start(bf16[12,1,24,128]{3,2,1,0:T(8,128)(2,1)S(1)} %get-tuple-element.59), channel_id=1, source_target_pairs={{0,24},{4,28},{8,16},{12,20},{16,8},{20,12},{24,0},{28,4},{1,25},{... | collective-permute-start | bytes 221192 | tf_op jit(solution)/shard_map/ppermute | solution.py:20
  63.7 7.5 %collective-permute-start.19 = (bf16[12,1,24,128]{3,2,1,0:T(8,128)(2,1)S(1)}, bf16[12,1,24,128]{3,2,1,0:T(8,128)(2,1)S(1)}, u32[]{:S(2)}, u32[]{:S(2)}) collective-permute-start(bf16[12,1,24,128]{3,2,1,0:T(8,128)(2,1)S(1)} %get-tuple-element.60), channel_id=1, source_target_pairs={{0,16},{4,20},{8,24},{12,28},{16,0},{20,4},{24,8},{28,12},{1,17},{... | collective-permute-start | bytes 221192 | tf_op jit(solution)/shard_map/ppermute | solution.py:20
  63.7 9.3 %collective-permute-start.20 = (bf16[12,1,24,128]{3,2,1,0:T(8,128)(2,1)S(1)}, bf16[12,1,24,128]{3,2,1,0:T(8,128)(2,1)S(1)}, u32[]{:S(2)}, u32[]{:S(2)}) collective-permute-start(bf16[12,1,24,128]{3,2,1,0:T(8,128)(2,1)S(1)} %get-tuple-element.61), channel_id=1, source_target_pairs={{0,8},{4,12},{8,0},{12,4},{16,24},{20,28},{24,16},{28,20},{1,9},{5... | collective-permute-start | bytes 221192 | tf_op jit(solution)/shard_map/ppermute | solution.py:20
  68.5 7.8 %collective-permute-start.23 = (bf16[12,1,24,128]{3,2,1,0:T(8,128)(2,1)S(1)}, bf16[12,1,24,128]{3,2,1,0:T(8,128)(2,1)S(1)}, u32[]{:S(2)}, u32[]{:S(2)}) collective-permute-start(bf16[12,1,24,128]{3,2,1,0:T(8,128)(2,1)S(1)} %get-tuple-element.66), channel_id=1, source_target_pairs={{0,24},{4,28},{8,16},{12,20},{16,8},{20,12},{24,0},{28,4},{1,25},{... | collective-permute-start | bytes 221192 | tf_op jit(solution)/shard_map/ppermute | solution.py:20
  71.1 7.0 %collective-permute-start.24 = (bf16[12,1,24,128]{3,2,1,0:T(8,128)(2,1)S(1)}, bf16[12,1,24,128]{3,2,1,0:T(8,128)(2,1)S(1)}, u32[]{:S(2)}, u32[]{:S(2)}) collective-permute-start(bf16[12,1,24,128]{3,2,1,0:T(8,128)(2,1)S(1)} %get-tuple-element.67), channel_id=1, source_target_pairs={{0,16},{4,20},{8,24},{12,28},{16,0},{20,4},{24,8},{28,12},{1,17},{... | collective-permute-start | bytes 221192 | tf_op jit(solution)/shard_map/ppermute | solution.py:20
  (10 other events, 52.1 us)
